TPU v7x, 32 devices: a whole 2x2x4 slice. The times are simulated.
32 devices in a mesh: rollout: 4 (over z), ctx: 8 (over y, x, core).
Axes of the slice: x: 2, y: 2, z: 4, core: 2. Of those that a mesh axis runs over, the one named last changes fastest.
Arguments:
- queries: bfloat16 [4, 1024, 4096], P('rollout', 'ctx'), may hold values from -6 to 6
- keys_values: bfloat16 [4, 2, 1024, 1024], P('rollout', None, 'ctx'), may hold values from -6 to 6
- image_rows: bfloat16 [4, 256, 6144], P('rollout', 'ctx'), may hold values from -6 to 6
- cotangent: bfloat16 [4, 1024, 4096], P('rollout', 'ctx'), may hold values from -96 to 96
- seq_image: int32 [4], replicated, may hold values from 0 to 3, as said below
- vis_start: int32 [4], P('rollout'), may hold values from 1 to 63
- comp_lengths: int32 [4, 16], P('rollout'), may hold values from 1 to 58, 704 in all within a row
Outputs:
- grad_queries: bfloat16 [4, 1024, 4096], P('rollout', 'ctx')
- grad_keys_values: bfloat16 [4, 2, 1024, 1024], P('rollout', None, 'ctx')
- grad_image: bfloat16 [4, 256, 6144], P('rollout', 'ctx')
Inputs may be any that keep to these rules, and one draw needn't show every extreme that they name: `seq_image`: each image belongs to exactly one group. The image's rows take positions vis_start to vis_start + 255 of the group's sequence. `comp_lengths`: each group's lengths sum to 704.
All inputs are finite; a program needn't handle non-finite values.
Results may differ from a plain program's by a relative error of at most 0.0068.
Values may be sent and summed in bfloat16 or wider, within the bound.
No kernel may reach another device: no remote copies, remote signals or barrier semaphores. Data moves between devices by JAX's collectives and lax.ppermute only.
A program may use at most 128 MiB of HBM per device.

v0:
```python
import math

import jax
import jax.numpy as jnp
from jax import lax
from jax.sharding import PartitionSpec as P

HEADS = 32
KV_HEADS = 8
HEAD_DIM = 128
VIS = 256
PROMPT = 64


neg_large = -1e30


def contract_last(left, right):
    return lax.dot_general(
        left, right, (((1,), (1,)), ((), ())), preferred_element_type=jnp.float32
    )


def contract_first(left, right):
    return lax.dot_general(
        left, right, (((0,), (0,)), ((), ())), preferred_element_type=jnp.float32
    )


def head_layout(q_rows, kv_rows, head_ratio):
    row_count = q_rows.shape[0]
    q_part = q_rows.reshape(1, row_count, HEADS, HEAD_DIM)
    kv_part = jnp.repeat(kv_rows.reshape(2, row_count, KV_HEADS, HEAD_DIM), head_ratio, axis=2)
    return jnp.concatenate([q_part, kv_part], axis=0)


def fold_heads(block, head_ratio):
    row_count = block.shape[1]
    q_part = block[0].reshape(row_count, HEADS * HEAD_DIM).astype(jnp.bfloat16)
    kv_part = jnp.sum(
        block[1:].reshape(2, row_count, KV_HEADS, head_ratio, HEAD_DIM), axis=3, dtype=jnp.float32
    )
    return (q_part, kv_part.astype(jnp.bfloat16).reshape(2, row_count, KV_HEADS * HEAD_DIM))


def attend(q_head, k_head, v_head, d_head, segment_ids, segment_begin):
    seq_len, head_dim = q_head.shape
    q_block = min(512, seq_len)
    k_block = min(128, seq_len)
    score_scale = 1.0 / math.sqrt(head_dim)
    prefix_len = VIS + PROMPT
    key_blocks = seq_len // k_block
    prefix_blocks = min(-(-prefix_len // k_block), key_blocks)
    column_ids = jnp.arange(k_block, dtype=jnp.int32)
    row_ids = jnp.arange(q_block, dtype=jnp.int32)

    def key_rows(key_index):
        k_begin = key_index * k_block
        k_rows = lax.dynamic_slice_in_dim(k_head, k_begin, k_block, 0)
        v_rows = lax.dynamic_slice_in_dim(v_head, k_begin, k_block, 0)
        seg_cols = lax.dynamic_slice_in_dim(segment_ids, k_begin, k_block, 0)
        return (k_rows, v_rows, seg_cols, k_begin)

    def query_step(block_index, loop_carry):
        dq_out, dk_acc, dv_acc, score_store = loop_carry
        q_begin = block_index * q_block
        q_rows = lax.dynamic_slice_in_dim(q_head, q_begin, q_block, 0)
        d_rows = lax.dynamic_slice_in_dim(d_head, q_begin, q_block, 0)
        seg_rows = lax.dynamic_slice_in_dim(segment_ids, q_begin, q_block, 0)
        positions = q_begin + row_ids
        first_seg = seg_rows[0]
        first_key = jnp.where(first_seg == 0, 0, segment_begin[jnp.maximum(first_seg - 1, 0)])
        upper = (q_begin + q_block - 1) // k_block + 1
        lower = jnp.maximum(first_key // k_block, prefix_blocks)
        prefix_upper = jnp.minimum(prefix_blocks, upper)

        def stats_step(key_index, running):
            row_top, row_total, row_mix, stored = running
            k_rows, v_rows, seg_cols, k_begin = key_rows(key_index)
            visible = ((k_begin + column_ids)[None, :] <= positions[:, None]) & (
                (seg_cols[None, :] == 0) | (seg_cols[None, :] == seg_rows[:, None])
            )
            scores = jnp.where(visible, contract_last(q_rows, k_rows) * score_scale, neg_large)
            d_weights = contract_last(d_rows, v_rows)
            new_top = jnp.maximum(row_top, jnp.max(scores, axis=1))
            shrink = jnp.exp(row_top - new_top)
            exp_terms = jnp.where(visible, jnp.exp(scores - new_top[:, None]), 0.0)
            stored = lax.dynamic_update_index_in_dim(stored, scores, key_index, 0)
            return (
                new_top,
                row_total * shrink + jnp.sum(exp_terms, axis=1),
                row_mix * shrink + jnp.sum(exp_terms * d_weights, axis=1),
                stored,
            )

        running = (
            jnp.full((q_block,), neg_large, jnp.float32),
            jnp.zeros((q_block,), jnp.float32),
            jnp.zeros((q_block,), jnp.float32),
            score_store,
        )
        running = lax.fori_loop(0, prefix_upper, stats_step, running)
        running = lax.fori_loop(lower, upper, stats_step, running)
        row_top, row_total, row_mix, score_store = running
        row_delta = row_mix / row_total

        def grad_step(key_index, sums):
            dq_acc, dk_sums, dv_sums = sums
            k_rows, v_rows, seg_cols, k_begin = key_rows(key_index)
            scores = lax.dynamic_index_in_dim(score_store, key_index, 0, keepdims=False)
            weights = jnp.exp(scores - row_top[:, None]) / row_total[:, None]
            d_weights = contract_last(d_rows, v_rows)
            d_scores = (weights * (d_weights - row_delta[:, None])).astype(jnp.bfloat16)
            dq_acc = dq_acc + jnp.dot(d_scores, k_rows, preferred_element_type=jnp.float32)
            dk_part = contract_first(d_scores, q_rows)
            dv_part = contract_first(weights.astype(jnp.bfloat16), d_rows)
            dk_sums = lax.dynamic_update_slice_in_dim(
                dk_sums,
                lax.dynamic_slice_in_dim(dk_sums, k_begin, k_block, 0) + dk_part,
                k_begin,
                0,
            )
            dv_sums = lax.dynamic_update_slice_in_dim(
                dv_sums,
                lax.dynamic_slice_in_dim(dv_sums, k_begin, k_block, 0) + dv_part,
                k_begin,
                0,
            )
            return (dq_acc, dk_sums, dv_sums)

        sums = (jnp.zeros((q_block, head_dim), jnp.float32), dk_acc, dv_acc)
        sums = lax.fori_loop(0, prefix_upper, grad_step, sums)
        dq_acc, dk_acc, dv_acc = lax.fori_loop(lower, upper, grad_step, sums)
        dq_out = lax.dynamic_update_slice_in_dim(dq_out, dq_acc * score_scale, q_begin, 0)
        return (dq_out, dk_acc, dv_acc, score_store)

    start_carry = (
        jnp.zeros((seq_len, head_dim), jnp.float32),
        jnp.zeros((seq_len, head_dim), jnp.float32),
        jnp.zeros((seq_len, head_dim), jnp.float32),
        jnp.zeros((key_blocks, q_block, k_block), jnp.float32),
    )
    dq_out, dk_acc, dv_acc, score_store = lax.fori_loop(
        0, seq_len // q_block, query_step, start_carry
    )
    return (dq_out, dk_acc * score_scale, dv_acc)


def heads_plan(q_local, kv_local, d_local, segment_ids, segment_begin, vis_begin):
    tok_rows = q_local.shape[0]
    ctx_size = lax.axis_size("ctx")
    seq_len = tok_rows * ctx_size
    head_ratio = HEADS // KV_HEADS
    heads_here = HEADS // ctx_size
    zero_index = jnp.zeros((), jnp.int32)
    d_part = d_local.reshape(1, tok_rows, HEADS, HEAD_DIM)
    packed = jnp.concatenate([head_layout(q_local, kv_local, head_ratio), d_part], axis=0)
    spread = lax.all_to_all(packed, "ctx", split_axis=2, concat_axis=1, tiled=True)

    def head_step(head_index, gradients):
        picked = lax.dynamic_index_in_dim(spread, head_index, 2, keepdims=False)
        head_dq, head_dk, head_dv = attend(
            picked[0], picked[1], picked[2], picked[3], segment_ids, segment_begin
        )
        update = jnp.stack([head_dq, head_dk, head_dv])[:, :, None, :]
        return lax.dynamic_update_slice(
            gradients, update, (zero_index, zero_index, head_index, zero_index)
        )

    gradients = lax.fori_loop(
        0, heads_here, head_step, jnp.zeros((3, seq_len, heads_here, HEAD_DIM), jnp.float32)
    )
    image_part = lax.dynamic_slice_in_dim(gradients, vis_begin, VIS, 1)
    gradients = lax.dynamic_update_slice_in_dim(
        gradients, jnp.zeros((3, VIS, heads_here, HEAD_DIM), jnp.float32), vis_begin, 1
    )
    returned, returned_image = (
        lax.all_to_all(gradients, "ctx", split_axis=1, concat_axis=2, tiled=True),
        lax.all_to_all(image_part, "ctx", split_axis=1, concat_axis=2, tiled=True),
    )
    grad_q, grad_kv = fold_heads(returned, head_ratio)
    image_q, image_kv = fold_heads(returned_image, head_ratio)
    return (grad_q, grad_kv, jnp.concatenate([image_q, image_kv[0], image_kv[1]], axis=1))


def per_device(queries, keys_values, image_rows, cotangent, seq_image, vis_start, comp_lengths):
    tok_rows = queries.shape[1]
    ctx_size = lax.axis_size("ctx")
    ctx_place = lax.axis_index("ctx")
    group_place = lax.axis_index("rollout")
    seq_len = tok_rows * ctx_size
    query_width = HEADS * HEAD_DIM
    kv_width = KV_HEADS * HEAD_DIM
    prefix_len = VIS + PROMPT
    vis_begin = vis_start[0]
    owner_rows = lax.all_gather(image_rows, "rollout", axis=0, tiled=True)
    chosen = lax.dynamic_index_in_dim(owner_rows, seq_image[group_place], 0, keepdims=False)
    every_row = lax.all_gather(chosen, "ctx", axis=0, tiled=True)
    offset = ctx_place * tok_rows + jnp.arange(tok_rows, dtype=jnp.int32) - vis_begin
    inside = (offset >= 0) & (offset < VIS)
    picked_rows = jnp.take(every_row, jnp.clip(offset, 0, VIS - 1), axis=0)
    q_local = jnp.where(inside[:, None], picked_rows[:, :query_width], queries[0])
    fresh_kv = jnp.stack(
        [
            picked_rows[:, query_width : query_width + kv_width],
            picked_rows[:, query_width + kv_width :],
        ]
    )
    kv_local = jnp.where(inside[None, :, None], fresh_kv, keys_values[0])
    d_local = cotangent[0]
    seg_ends = jnp.cumsum(comp_lengths[0])
    positions = jnp.arange(seq_len, dtype=jnp.int32)
    later_ends = jnp.sum(
        (seg_ends[None, :] <= (positions - prefix_len)[:, None]).astype(jnp.int32), axis=1
    )
    segment_ids = jnp.where(positions < prefix_len, 0, 1 + later_ends)
    segment_begin = prefix_len + jnp.concatenate([jnp.zeros((1,), jnp.int32), seg_ends[:-1]])
    grad_q, grad_kv, image_grad = heads_plan(
        q_local, kv_local, d_local, segment_ids, segment_begin, vis_begin
    )
    group_grads = lax.all_gather(image_grad[None], "rollout", axis=0, tiled=True)
    user_group = jnp.sum(
        jnp.where(seq_image == group_place, jnp.arange(seq_image.shape[0], dtype=jnp.int32), 0)
    )
    own_grad = lax.dynamic_index_in_dim(group_grads, user_group, 0, keepdims=True)
    return (grad_q[None], grad_kv[None], own_grad)


def solution(mesh):
    placed = (
        P("rollout", "ctx", None),
        P("rollout", None, "ctx", None),
        P("rollout", "ctx", None),
        P("rollout", "ctx", None),
        P(),
        P("rollout"),
        P("rollout", None),
    )
    return jax.shard_map(
        per_device,
        mesh=mesh,
        in_specs=placed,
        out_specs=(
            P("rollout", "ctx", None),
            P("rollout", None, "ctx", None),
            P("rollout", "ctx", None),
        ),
        check_vma=False,
    )
```

profile of v0, /device:TPU:0, one launch (start us, length us, event | category | flops | bytes accessed | tf_op | source)
XLA Modules:
  0.0 685.3 jit_solution(5600284738532943203)
XLA Ops:
  11.1 38.3 %all-gather.6.cloned.1.call-done = bf16[4,32,6144]{2,1,0:T(8,128)(2,1)} async-done(((bf16[1,32,6144]{2,1,0:T(8,128)(2,1)}), bf16[4,32,6144]{2,1,0:T(8,128)(2,1)}) %all-gather.6.cloned.1.call-update) | async-done | bytes 1572880 | tf_op jit(solution)/shard_map/all_gather | solution.py:196
  54.4 28.7 %all-gather.8.cloned.1.call-done = bf16[1,256,6144]{2,1,0:T(8,128)(2,1)} async-done(((bf16[1,32,6144]{2,1,0:T(8,128)(2,1)}), bf16[1,256,6144]{2,1,0:T(8,128)(2,1)}) %all-gather.8.cloned.1.call-update) | async-done | bytes 3145744 | tf_op jit(solution)/shard_map/all_gather | solution.py:198
  83.1 5.3 gather_fusion
  93.6 4.9 all-to-all-start
  99.0 48.4 %all-to-all-done = bf16[4,128,32,128]{3,1,0,2:T(8,128)(2,1)} async-done(((bf16[4,128,32,128]{3,1,0,2:T(8,128)(2,1)}), bf16[4,128,32,128]{3,1,0,2:T(8,128)(2,1)}, u32[]{:S(2)}, u32[]{:S(2)}) %all-to-all-start) | async-done | bytes 4194336 | tf_op jit(solution)/shard_map/all_to_all | solution.py:158
  147.4 4.8 copy.88
  152.2 408.1 %while.301 = (s32[]{:T(128)}, f32[3,1024,4,128]{3,2,0,1:T(4,128)}, bf16[4,1024,4,128]{3,1,2,0:T(8,128)(2,1)}, s32[1024]{0:T(1024)S(1)}, s32[16]{0:T(128)S(1)}, /...) while((s32[]{:T(128)}, f32[3,1024,4,128]{3,2,0,1:T(4,128)}, ...), condition=%wide.region_19.20_spmd, body=%wide.region_2.19_spmd.sunk | while | flops 206443040 | bytes 25319720 | solution.py:170
  155.2 57.8 %while.302 = (s32[]{:T(128)}, f32[1024,128]{1,0:T(8,128)S(1)}, f32[1024,128]{1,0:T(8,128)S(1)}, f32[1024,128]{1,0:T(8,128)S(1)}, f32[8,512,128]{1,2,0:T(8,128)},...) while((s32[]{:T(128)}, f32[1024,128]{1,0:T(8,128)S(1)}, ...), condition=%wide.region_18.18_spmd.clone.clone, body=%wide.region_3.17_spmd.clone.clone.sunk | while | flops 205525536 | bytes 9065989 | solution.py:143
  155.4 4.5 while.303
  164.6 8.2 %while.305 = (s32[]{:T(128)}, f32[512,128]{1,0:T(8,128)S(1)}, f32[1024,128]{1,0:T(8,128)S(1)}, f32[1024,128]{1,0:T(8,128)S(1)}, s32[]{:T(128)}, /*index=5*/f32[8...) while((s32[]{:T(128)}, f32[512,128]{1,0:T(8,128)S(1)}, ...), condition=%wide.region_15.14_spmd, body=%wide.region_14.13_spmd.sunk | while | flops 67731464 | bytes 2173197 | solution.py:132
  172.8 2.8 while.306
  175.8 4.5 while.303
  183.5 7.4 %while.304 = (s32[]{:T(128)}, f32[512]{0:T(512)S(1)}, f32[512]{0:T(512)S(1)}, f32[512]{0:T(512)S(1)}, f32[8,512,128]{1,2,0:T(8,128)}, /*index=5*/s32[]{:T(128)},...) while((s32[]{:T(128)}, f32[512]{0:T(512)S(1)}, ...), condition=%wide.region_13.12_spmd, body=%wide.region_9.11_spmd.sunk | while | flops 34998020 | bytes 1694225 | solution.py:103
  190.9 8.2 %while.305 = (s32[]{:T(128)}, f32[512,128]{1,0:T(8,128)S(1)}, f32[1024,128]{1,0:T(8,128)S(1)}, f32[1024,128]{1,0:T(8,128)S(1)}, s32[]{:T(128)}, /*index=5*/f32[8...) while((s32[]{:T(128)}, f32[512,128]{1,0:T(8,128)S(1)}, ...), condition=%wide.region_15.14_spmd, body=%wide.region_14.13_spmd.sunk | while | flops 67731464 | bytes 2173197 | solution.py:132
  199.2 13.7 %while.306 = (s32[]{:T(128)}, f32[512,128]{1,0:T(8,128)S(1)}, f32[1024,128]{1,0:T(8,128)S(1)}, f32[1024,128]{1,0:T(8,128)S(1)}, s32[]{:T(128)}, /*index=5*/f32[8...) while((s32[]{:T(128)}, f32[512,128]{1,0:T(8,128)S(1)}, ...), condition=%wide.region_17.16_spmd, body=%wide.region_16.15_spmd.sunk | while | flops 67731464 | bytes 2173197 | solution.py:133
  214.7 39.5 %dynamic_update_slice.66 = f32[3,1024,4,128]{3,2,0,1:T(4,128)} dynamic-update-slice(f32[3,1024,4,128]{3,2,0,1:T(4,128)} %get-tuple-element.2237, f32[3,1024,1,128]{3,2,0,1:T(1,128)S(1)} %copy.121, s32[]{:T(128)} %constant.344.clone.1..sunk, s32[]{:T(128)} %constant.344.clone.1..sunk, s32[]{:T(128)} %get-tuple-element.2236, s32[]{:T(128)} %constant.344.clone.1..sunk) | dynamic-update-slice | bytes 3145732 | tf_op jit(solution)/shard_map/while/body/eval_jaxpr/dynamic_update_slice | solution.py:166
  257.2 57.8 %while.302 = (s32[]{:T(128)}, f32[1024,128]{1,0:T(8,128)S(1)}, f32[1024,128]{1,0:T(8,128)S(1)}, f32[1024,128]{1,0:T(8,128)S(1)}, f32[8,512,128]{1,2,0:T(8,128)},...) while((s32[]{:T(128)}, f32[1024,128]{1,0:T(8,128)S(1)}, ...), condition=%wide.region_18.18_spmd.clone.clone, body=%wide.region_3.17_spmd.clone.clone.sunk | while | flops 205525536 | bytes 9065989 | solution.py:143
  257.4 4.5 while.303
  266.6 8.2 %while.305 = (s32[]{:T(128)}, f32[512,128]{1,0:T(8,128)S(1)}, f32[1024,128]{1,0:T(8,128)S(1)}, f32[1024,128]{1,0:T(8,128)S(1)}, s32[]{:T(128)}, /*index=5*/f32[8...) while((s32[]{:T(128)}, f32[512,128]{1,0:T(8,128)S(1)}, ...), condition=%wide.region_15.14_spmd, body=%wide.region_14.13_spmd.sunk | while | flops 67731464 | bytes 2173197 | solution.py:132
  274.8 2.8 while.306
  277.8 4.5 while.303
  285.5 7.4 %while.304 = (s32[]{:T(128)}, f32[512]{0:T(512)S(1)}, f32[512]{0:T(512)S(1)}, f32[512]{0:T(512)S(1)}, f32[8,512,128]{1,2,0:T(8,128)}, /*index=5*/s32[]{:T(128)},...) while((s32[]{:T(128)}, f32[512]{0:T(512)S(1)}, ...), condition=%wide.region_13.12_spmd, body=%wide.region_9.11_spmd.sunk | while | flops 34998020 | bytes 1694225 | solution.py:103
  292.9 8.2 %while.305 = (s32[]{:T(128)}, f32[512,128]{1,0:T(8,128)S(1)}, f32[1024,128]{1,0:T(8,128)S(1)}, f32[1024,128]{1,0:T(8,128)S(1)}, s32[]{:T(128)}, /*index=5*/f32[8...) while((s32[]{:T(128)}, f32[512,128]{1,0:T(8,128)S(1)}, ...), condition=%wide.region_15.14_spmd, body=%wide.region_14.13_spmd.sunk | while | flops 67731464 | bytes 2173197 | solution.py:132
  301.2 13.7 %while.306 = (s32[]{:T(128)}, f32[512,128]{1,0:T(8,128)S(1)}, f32[1024,128]{1,0:T(8,128)S(1)}, f32[1024,128]{1,0:T(8,128)S(1)}, s32[]{:T(128)}, /*index=5*/f32[8...) while((s32[]{:T(128)}, f32[512,128]{1,0:T(8,128)S(1)}, ...), condition=%wide.region_17.16_spmd, body=%wide.region_16.15_spmd.sunk | while | flops 67731464 | bytes 2173197 | solution.py:133
  316.8 39.5 %dynamic_update_slice.66 = f32[3,1024,4,128]{3,2,0,1:T(4,128)} dynamic-update-slice(f32[3,1024,4,128]{3,2,0,1:T(4,128)} %get-tuple-element.2237, f32[3,1024,1,128]{3,2,0,1:T(1,128)S(1)} %copy.121, s32[]{:T(128)} %constant.344.clone.1..sunk, s32[]{:T(128)} %constant.344.clone.1..sunk, s32[]{:T(128)} %get-tuple-element.2236, s32[]{:T(128)} %constant.344.clone.1..sunk) | dynamic-update-slice | bytes 3145732 | tf_op jit(solution)/shard_map/while/body/eval_jaxpr/dynamic_update_slice | solution.py:166
  359.2 57.8 %while.302 = (s32[]{:T(128)}, f32[1024,128]{1,0:T(8,128)S(1)}, f32[1024,128]{1,0:T(8,128)S(1)}, f32[1024,128]{1,0:T(8,128)S(1)}, f32[8,512,128]{1,2,0:T(8,128)},...) while((s32[]{:T(128)}, f32[1024,128]{1,0:T(8,128)S(1)}, ...), condition=%wide.region_18.18_spmd.clone.clone, body=%wide.region_3.17_spmd.clone.clone.sunk | while | flops 205525536 | bytes 9065989 | solution.py:143
  359.4 4.5 while.303
  368.6 8.2 %while.305 = (s32[]{:T(128)}, f32[512,128]{1,0:T(8,128)S(1)}, f32[1024,128]{1,0:T(8,128)S(1)}, f32[1024,128]{1,0:T(8,128)S(1)}, s32[]{:T(128)}, /*index=5*/f32[8...) while((s32[]{:T(128)}, f32[512,128]{1,0:T(8,128)S(1)}, ...), condition=%wide.region_15.14_spmd, body=%wide.region_14.13_spmd.sunk | while | flops 67731464 | bytes 2173197 | solution.py:132
  379.9 4.5 while.303
  387.5 7.4 %while.304 = (s32[]{:T(128)}, f32[512]{0:T(512)S(1)}, f32[512]{0:T(512)S(1)}, f32[512]{0:T(512)S(1)}, f32[8,512,128]{1,2,0:T(8,128)}, /*index=5*/s32[]{:T(128)},...) while((s32[]{:T(128)}, f32[512]{0:T(512)S(1)}, ...), condition=%wide.region_13.12_spmd, body=%wide.region_9.11_spmd.sunk | while | flops 34998020 | bytes 1694225 | solution.py:103
  395.0 8.2 %while.305 = (s32[]{:T(128)}, f32[512,128]{1,0:T(8,128)S(1)}, f32[1024,128]{1,0:T(8,128)S(1)}, f32[1024,128]{1,0:T(8,128)S(1)}, s32[]{:T(128)}, /*index=5*/f32[8...) while((s32[]{:T(128)}, f32[512,128]{1,0:T(8,128)S(1)}, ...), condition=%wide.region_15.14_spmd, body=%wide.region_14.13_spmd.sunk | while | flops 67731464 | bytes 2173197 | solution.py:132
  403.2 13.7 %while.306 = (s32[]{:T(128)}, f32[512,128]{1,0:T(8,128)S(1)}, f32[1024,128]{1,0:T(8,128)S(1)}, f32[1024,128]{1,0:T(8,128)S(1)}, s32[]{:T(128)}, /*index=5*/f32[8...) while((s32[]{:T(128)}, f32[512,128]{1,0:T(8,128)S(1)}, ...), condition=%wide.region_17.16_spmd, body=%wide.region_16.15_spmd.sunk | while | flops 67731464 | bytes 2173197 | solution.py:133
  418.8 39.5 %dynamic_update_slice.66 = f32[3,1024,4,128]{3,2,0,1:T(4,128)} dynamic-update-slice(f32[3,1024,4,128]{3,2,0,1:T(4,128)} %get-tuple-element.2237, f32[3,1024,1,128]{3,2,0,1:T(1,128)S(1)} %copy.121, s32[]{:T(128)} %constant.344.clone.1..sunk, s32[]{:T(128)} %constant.344.clone.1..sunk, s32[]{:T(128)} %get-tuple-element.2236, s32[]{:T(128)} %constant.344.clone.1..sunk) | dynamic-update-slice | bytes 3145732 | tf_op jit(solution)/shard_map/while/body/eval_jaxpr/dynamic_update_slice | solution.py:166
  461.3 57.8 %while.302 = (s32[]{:T(128)}, f32[1024,128]{1,0:T(8,128)S(1)}, f32[1024,128]{1,0:T(8,128)S(1)}, f32[1024,128]{1,0:T(8,128)S(1)}, f32[8,512,128]{1,2,0:T(8,128)},...) while((s32[]{:T(128)}, f32[1024,128]{1,0:T(8,128)S(1)}, ...), condition=%wide.region_18.18_spmd.clone.clone, body=%wide.region_3.17_spmd.clone.clone.sunk | while | flops 205525536 | bytes 9065989 | solution.py:143
  461.4 4.5 while.303
  470.7 8.2 %while.305 = (s32[]{:T(128)}, f32[512,128]{1,0:T(8,128)S(1)}, f32[1024,128]{1,0:T(8,128)S(1)}, f32[1024,128]{1,0:T(8,128)S(1)}, s32[]{:T(128)}, /*index=5*/f32[8...) while((s32[]{:T(128)}, f32[512,128]{1,0:T(8,128)S(1)}, ...), condition=%wide.region_15.14_spmd, body=%wide.region_14.13_spmd.sunk | while | flops 67731464 | bytes 2173197 | solution.py:132
  481.9 4.5 while.303
  489.6 7.4 %while.304 = (s32[]{:T(128)}, f32[512]{0:T(512)S(1)}, f32[512]{0:T(512)S(1)}, f32[512]{0:T(512)S(1)}, f32[8,512,128]{1,2,0:T(8,128)}, /*index=5*/s32[]{:T(128)},...) while((s32[]{:T(128)}, f32[512]{0:T(512)S(1)}, ...), condition=%wide.region_13.12_spmd, body=%wide.region_9.11_spmd.sunk | while | flops 34998020 | bytes 1694225 | solution.py:103
  497.0 8.2 %while.305 = (s32[]{:T(128)}, f32[512,128]{1,0:T(8,128)S(1)}, f32[1024,128]{1,0:T(8,128)S(1)}, f32[1024,128]{1,0:T(8,128)S(1)}, s32[]{:T(128)}, /*index=5*/f32[8...) while((s32[]{:T(128)}, f32[512,128]{1,0:T(8,128)S(1)}, ...), condition=%wide.region_15.14_spmd, body=%wide.region_14.13_spmd.sunk | while | flops 67731464 | bytes 2173197 | solution.py:132
  505.3 13.7 %while.306 = (s32[]{:T(128)}, f32[512,128]{1,0:T(8,128)S(1)}, f32[1024,128]{1,0:T(8,128)S(1)}, f32[1024,128]{1,0:T(8,128)S(1)}, s32[]{:T(128)}, /*index=5*/f32[8...) while((s32[]{:T(128)}, f32[512,128]{1,0:T(8,128)S(1)}, ...), condition=%wide.region_17.16_spmd, body=%wide.region_16.15_spmd.sunk | while | flops 67731464 | bytes 2173197 | solution.py:133
  520.8 39.5 %dynamic_update_slice.66 = f32[3,1024,4,128]{3,2,0,1:T(4,128)} dynamic-update-slice(f32[3,1024,4,128]{3,2,0,1:T(4,128)} %get-tuple-element.2237, f32[3,1024,1,128]{3,2,0,1:T(1,128)S(1)} %copy.121, s32[]{:T(128)} %constant.344.clone.1..sunk, s32[]{:T(128)} %constant.344.clone.1..sunk, s32[]{:T(128)} %get-tuple-element.2236, s32[]{:T(128)} %constant.344.clone.1..sunk) | dynamic-update-slice | bytes 3145732 | tf_op jit(solution)/shard_map/while/body/eval_jaxpr/dynamic_update_slice | solution.py:166
  560.4 3.0 constant_dynamic-slice_fusion.3
  563.4 23.4 %all_to_all.48 = f32[3,256,4,128]{3,2,0,1:T(4,128)S(1)} all-to-all(f32[3,256,4,128]{3,2,0,1:T(4,128)S(1)} %get-tuple-element.1198), channel_id=1, replica_groups=mesh['rollout'=4,'ctx'=8] {'ctx'}, dimensions={1} | all-to-all | bytes 3145728 | tf_op jit(solution)/shard_map/all_to_all | solution.py:179
  586.8 4.8 all-to-all-start.1
  596.6 36.4 %all-gather.10.cloned.1.call-done = bf16[128,6144]{1,0:T(8,128)(2,1)} async-done(((bf16[32,6144]{1,0:T(8,128)(2,1)}), bf16[128,6144]{1,0:T(8,128)(2,1)}) %all-gather.10.cloned.1.call-update) | async-done | bytes 1572880 | tf_op jit(solution)/shard_map/all_gather | solution.py:221
  634.8 28.4 %all-to-all-done.1 = f32[3,1024,4,128]{3,2,0,1:T(4,128)} async-done(((f32[3,1024,4,128]{3,2,0,1:T(4,128)}), f32[3,1024,4,128]{3,2,0,1:T(4,128)}, u32[]{:S(2)}, u32[]{:S(2)}) %all-to-all-start.1) | async-done | bytes 6291488 | tf_op jit(solution)/shard_map/all_to_all | solution.py:178
  663.1 5.0 copy.118
  669.6 5.7 slice_reduce_fusion
  (818 shorter events, 260.6 us)
Async XLA Ops:
  7.2 45.8 %copy-start = (bf16[1,128,4096]{2,1,0:T(8,128)(2,1)S(1)}, bf16[1,128,4096]{2,1,0:T(8,128)(2,1)}, u32[]{:S(2)}) copy-start(bf16[1,128,4096]{2,1,0:T(8,128)(2,1)} %param.22) | copy-start | bytes 3145732
  7.2 42.2 %all-gather.6.cloned.1.call-start = ((), (), s32[]{:S(2)}) async-start(), calls=%async_computation.3 | async-start | bytes 1966080 | tf_op jit(solution)/shard_map/all_gather | solution.py:196
  7.9 75.2 %all-gather.8.cloned.1.call-start = ((), (), s32[]{:S(2)}) async-start(), calls=%async_computation.4 | async-start | bytes 3538944 | tf_op jit(solution)/shard_map/all_gather | solution.py:198
  88.6 1.2 copy-start.1
  93.6 4.9 copy-start.2
  93.6 53.8 %all-to-all-start = ((bf16[4,128,32,128]{3,1,0,2:T(8,128)(2,1)}), bf16[4,128,32,128]{3,1,0,2:T(8,128)(2,1)}, u32[]{:S(2)}, u32[]{:S(2)}) async-start(bf16[4,128,32,128]{3,1,0,2:T(8,128)(2,1)} %pad_maximum_fusion), calls=%async_computation | async-start | bytes 8388608 | tf_op jit(solution)/shard_map/all_to_all | solution.py:158
  586.8 76.4 %all-to-all-start.1 = ((f32[3,1024,4,128]{3,2,0,1:T(4,128)}), f32[3,1024,4,128]{3,2,0,1:T(4,128)}, u32[]{:S(2)}, u32[]{:S(2)}) async-start(f32[3,1024,4,128]{3,2,0,1:T(4,128)} %get-tuple-element.1199), calls=%async_computation.1 | async-start | bytes 12582912 | tf_op jit(solution)/shard_map/all_to_all | solution.py:178
  591.5 41.4 %all-gather.10.cloned.1.call-start = ((), (), s32[]{:S(2)}) async-start(), calls=%async_computation.5 | async-start | bytes 1966080 | tf_op jit(solution)/shard_map/all_gather | solution.py:221
  592.4 1.7 copy-start.3
Sparse Core Ops, SparseCore 0:
  9.6 39.7 all-gather.5
  51.9 31.1 all-gather.7
  594.5 38.4 all-gather.9
where the time goes:
time: 693 us; the launch traced here: 685 us
  local copies, waits for them, and re-layouts  256 us (37%)
  waiting for transfers between devices  181 us (26%)
  matrix products  150 us (22%)
  other arithmetic  24.6 us (4%)
  blocking collectives  23.4 us (3%)
  loops' own time  22.5 us (3%)
  between operations  18.6 us (3%)
  starting transfers between devices  9.98 us (1%)
    dynamic_update_slice x8, local copies, waits for them, and re-layouts, head_step(): lax.dynamic_update_slice(gradients, update, (zero_index, zero_index, head...  165 us
    dot_general x144, matrix products, contract_last(): lax.dot_general(left, right, (((1,), (1,)), ((), ())), preferred_element_...  75.7 us
    dot_general x96, matrix products, contract_first(): lax.dot_general(left, right, (((0,), (0,)), ((), ())), preferred_element_...  62.9 us
    all_to_all x1, waiting for transfers between devices, heads_plan(): lax.all_to_all(packed, 'ctx', split_axis=2, concat_axis=1, tiled=True)  48.4 us
    all_gather x1, waiting for transfers between devices, per_device(): owner_rows = lax.all_gather(image_rows, 'rollout', axis=0, tiled=True)  38.3 us
    all_gather x1, waiting for transfers between devices, per_device(): lax.all_gather(image_grad[None], 'rollout', axis=0, tiled=True)  36.4 us
    dynamic_update_slice x48, local copies, waits for them, and re-layouts, stats_step(): stored = lax.dynamic_update_index_in_dim(stored, scores, key_index, 0)  35 us
    all_gather x1, waiting for transfers between devices, per_device(): every_row = lax.all_gather(chosen, 'ctx', axis=0, tiled=True)  28.7 us
  transfers between devices with their start and end apart: 5, of which 5 were waited for; matrix products, arithmetic and copies ran while one was open for 1% of the time, Pallas kernels for 0%

commit v1 on v0

v1 whole, which is shorter than its diff:
```python
import functools
import itertools
import math

import jax
import jax.numpy as jnp
from jax import lax
from jax.experimental import pallas as pl
from jax.experimental.pallas import tpu as pltpu
from jax.sharding import PartitionSpec as P

HEADS = 32
KV_HEADS = 8
HEAD_DIM = 128
VIS = 256
PROMPT = 64
NCOMP = 16

RATIO = HEADS // KV_HEADS
PREFIX = VIS + PROMPT
Q_WIDTH = HEADS * HEAD_DIM
KV_WIDTH = KV_HEADS * HEAD_DIM
GROUP_WIDTH = RATIO * HEAD_DIM
IMAGE_BLOCK = 32
HIDDEN = -1e30
SCORE_SCALE = 1.0 / math.sqrt(HEAD_DIM)


def dot_nt(left, right):
    return lax.dot_general(
        left, right, (((1,), (1,)), ((), ())), preferred_element_type=jnp.float32
    )


def dot_nn(left, right):
    return lax.dot_general(
        left, right, (((1,), (0,)), ((), ())), preferred_element_type=jnp.float32
    )


def dot_tn(left, right):
    return lax.dot_general(
        left, right, (((0,), (0,)), ((), ())), preferred_element_type=jnp.float32
    )


def first_kernel(halo, seq_ref, vis_ref, image_ref, kv_ref, number_ref, *out_refs):
    ikv_ref, iq_ref, text_ref, tail_ref = out_refs
    groups = seq_ref.shape[0]
    group = lax.axis_index("rollout")
    here = lax.axis_index("ctx")
    images = [seq_ref[at] for at in range(groups)]
    number = jnp.int32(0)
    if groups == 4:
        for at, weight in enumerate((6, 2, 1)):
            for later in range(at + 1, groups):
                number = number + jnp.where(images[later] < images[at], weight, 0)
    place = jnp.int32(0)
    user = jnp.int32(0)
    for at in range(groups):
        place = place + jnp.where(group == at, images[at], 0)
        user = user + jnp.where(images[at] == group, at, 0)
    number_ref[0] = number
    number_ref[1] = place
    number_ref[2] = user
    iq_ref[...] = image_ref[0, :, :Q_WIDTH]
    ikv_ref[0] = image_ref[0, :, Q_WIDTH : Q_WIDTH + KV_WIDTH]
    ikv_ref[1] = image_ref[0, :, Q_WIDTH + KV_WIDTH :]
    tok_rows = kv_ref.shape[2]
    late_shard = VIS // tok_rows
    at = lax.broadcasted_iota(jnp.int32, (PROMPT, KV_WIDTH), 0)
    ahead = jnp.where(here == 0, 1, 0)
    behind = jnp.where(here == late_shard, 1, 0)
    kept = jnp.where(at < vis_ref[0], ahead, behind) == 1
    for part in range(2):
        rows = kv_ref[0, part, :PROMPT].astype(jnp.float32)
        text_ref[part] = jnp.where(kept, rows, 0.0).astype(jnp.bfloat16)
        tail_ref[part] = kv_ref[0, part, tok_rows - halo :]


def first_arrays(seq_image, vis_start, image_rows, keys_values, halo):
    rows = image_rows.shape[1]
    smem = pl.BlockSpec(memory_space=pltpu.SMEM)
    vmem = pl.BlockSpec(memory_space=pltpu.VMEM)
    tail = min(halo, keys_values.shape[2])
    return pl.pallas_call(
        functools.partial(first_kernel, tail),
        in_specs=[smem, smem, vmem, vmem],
        out_specs=[smem, vmem, vmem, vmem, vmem],
        out_shape=[
            jax.ShapeDtypeStruct((3,), jnp.int32),
            jax.ShapeDtypeStruct((2, rows, KV_WIDTH), jnp.bfloat16),
            jax.ShapeDtypeStruct((rows, Q_WIDTH), jnp.bfloat16),
            jax.ShapeDtypeStruct((2, PROMPT, KV_WIDTH), jnp.bfloat16),
            jax.ShapeDtypeStruct((2, tail, KV_WIDTH), jnp.bfloat16),
        ],
    )(seq_image, vis_start, image_rows, keys_values)


def segments(positions, length_ref):
    end = jnp.int32(PREFIX)
    segment = jnp.where(positions < PREFIX, 0, 1)
    for at in range(NCOMP):
        end = end + length_ref[0, at]
        segment = segment + jnp.where(positions >= end, 1, 0)
    return segment


def hide(visible):
    return jnp.where(visible, 0.0, HIDDEN)


def second_kernel(
    rounds, tok_rows, image_rows, halo, vis_ref, length_ref, d_ref, t_ref, r_ref, *out_refs
):
    *window_refs, near_ref, whole_ref, image_ref, text_ref = out_refs
    here = lax.axis_index("ctx")
    ctx_size = lax.axis_size("ctx")
    row = lax.broadcasted_iota(jnp.int32, (IMAGE_BLOCK, tok_rows), 0)
    column = lax.broadcasted_iota(jnp.int32, (IMAGE_BLOCK, tok_rows), 1)
    place = jnp.where(row < image_rows, row, 1 << 20)
    picks = []
    for pairs in [[]] + rounds:
        target = here
        for source, other in pairs:
            target = jnp.where(here == source, other, target)
        begin = vis_ref[0] + image_rows * target - tok_rows * here
        picks.append(jnp.where(column == place + begin, 1.0, 0.0).astype(jnp.bfloat16))
    picked = dot_nn(jnp.concatenate(picks, axis=0), d_ref[...]).astype(jnp.bfloat16)
    for at, window_ref in enumerate(window_refs):
        window_ref[...] = picked[at * IMAGE_BLOCK : (at + 1) * IMAGE_BLOCK]

    @pl.when(pl.program_id(0) == 0)
    def _():
        vis = vis_ref[0]
        text = t_ref[...].astype(jnp.float32) + r_ref[...].astype(jnp.float32)
        text_ref[...] = text.astype(jnp.bfloat16)
        own_at = lax.broadcasted_iota(jnp.int32, (8, tok_rows), 1) + here * tok_rows
        own_segment = segments(own_at, length_ref)[:1]
        placeholder = (own_at >= vis) & (own_at < vis + VIS)
        own_row = jnp.where(placeholder, -1, own_at)
        whole_ref[...] = hide(own_row >= vis + VIS).astype(jnp.float32)
        own_row = own_row[:1]
        image_at = lax.broadcasted_iota(jnp.int32, (1, RATIO * IMAGE_BLOCK), 1) % IMAGE_BLOCK
        image_row = jnp.where(image_at < image_rows, vis + here * image_rows + image_at, -1)
        text_at = lax.broadcasted_iota(jnp.int32, (PROMPT, tok_rows), 0)
        text_at = text_at + jnp.where(text_at < vis, 0, VIS)
        near_ref[:PROMPT] = hide(text_at <= own_row)
        near_at = lax.broadcasted_iota(jnp.int32, (halo + tok_rows, tok_rows), 0)
        near_at = near_at + (here * tok_rows - halo)
        sees = (near_at <= own_row) & (near_at >= PREFIX)
        sees = sees & (segments(near_at, length_ref) == own_segment)
        near_ref[PROMPT:] = hide(sees)
        at = 0
        for core in range(2):
            for step in range(0, ctx_size, 2):
                begin = (here ^ (step + core)) * image_rows + vis
                shape = (image_rows, RATIO * IMAGE_BLOCK)
                block_at = lax.broadcasted_iota(jnp.int32, shape, 0) + begin
                image_ref[at : at + image_rows] = hide(block_at <= image_row)
                at += image_rows
        image_ref[VIS:] = hide(text_at <= image_row)


def second_arrays(vis_start, lengths, cotangent, text, received, image_rows, halo):
    tok_rows, width = cotangent.shape
    rounds = window_rounds(lax.axis_size("ctx"), tok_rows, image_rows)
    count = len(rounds) + 1
    block = 1024
    spec = pl.BlockSpec
    smem = spec(memory_space=pltpu.SMEM)
    lanes = RATIO * IMAGE_BLOCK
    near = PROMPT + halo + tok_rows
    whole = lambda *shape: spec(shape, lambda at: (0,) * len(shape))
    out = pl.pallas_call(
        functools.partial(second_kernel, rounds, tok_rows, image_rows, halo),
        grid=(width // block,),
        in_specs=[
            smem,
            smem,
            spec((tok_rows, block), lambda at: (0, at)),
            whole(2, PROMPT, KV_WIDTH),
            whole(2, PROMPT, KV_WIDTH),
        ],
        out_specs=[spec((IMAGE_BLOCK, block), lambda at: (0, at)) for _ in range(count)]
        + [
            whole(near, tok_rows),
            whole(8, tok_rows),
            whole(PREFIX, lanes),
            whole(2, PROMPT, KV_WIDTH),
        ],
        out_shape=[jax.ShapeDtypeStruct((IMAGE_BLOCK, width), jnp.bfloat16) for _ in range(count)]
        + [
            jax.ShapeDtypeStruct((near, tok_rows), jnp.float32),
            jax.ShapeDtypeStruct((8, tok_rows), jnp.float32),
            jax.ShapeDtypeStruct((PREFIX, lanes), jnp.float32),
            jax.ShapeDtypeStruct((2, PROMPT, KV_WIDTH), jnp.bfloat16),
        ],
    )(vis_start, lengths, cotangent, text, received)
    return out[:count], rounds, out[count:]


def rows_backward(parts, q_rows, d_rows):
    scale = SCORE_SCALE * math.log2(math.e)
    scores = []
    for keys, values, bias in parts:
        raw = dot_nt(keys, q_rows) * scale
        scores.append(raw if bias.shape[0] == 1 else raw + bias)
    tops = [jnp.max(part, axis=0, keepdims=True) for part in scores]
    tops = [
        top + bias if bias.shape[0] == 1 else top for top, (_, _, bias) in zip(tops, parts)
    ]
    top = functools.reduce(jnp.maximum, tops)
    total = 0.0
    mix = 0.0
    kept = []
    for part, (keys, values, bias) in zip(scores, parts):
        shift = bias - top if bias.shape[0] == 1 else -top
        terms = jnp.exp2(part + shift)
        d_weights = dot_nt(values, d_rows)
        total = total + jnp.sum(terms, axis=0, keepdims=True)
        mix = mix + jnp.sum(terms * d_weights, axis=0, keepdims=True)
        kept.append((terms, d_weights))
    inverse = jnp.where(top > 0.5 * HIDDEN, 1.0 / total, 0.0)
    delta = mix * inverse
    outcome = []
    for terms, d_weights in kept:
        weights = terms * inverse
        d_scores = weights * (d_weights - delta)
        outcome.append((weights.astype(jnp.bfloat16), d_scores.astype(jnp.bfloat16)))
    return outcome


def total_of(refs, at=slice(None)):
    if len(refs) == 1:
        return refs[0][at]
    return sum(ref[at].astype(jnp.float32) for ref in refs).astype(jnp.bfloat16)


def attend_kernel(
    block_count,
    window_count,
    heads,
    halo,
    own,
    number_ref,
    near_ref,
    whole_ref,
    image_bias_ref,
    q_ref,
    d_ref,
    iq_ref,
    text_ref,
    other_text_ref,
    halo_ref,
    own_ref,
    *refs,
):
    block_refs = refs[:block_count]
    window_refs = refs[block_count : block_count + window_count]
    dq_ref, diq_ref, dmine_ref, dpair_ref, dhalo_ref, down_ref = refs[
        block_count + window_count :
    ]
    near_bias = jnp.concatenate([near_ref[...]] * 2, axis=1)
    whole_bias = jnp.concatenate([whole_ref[:1]] * 2, axis=1)
    image_cotangent = total_of(window_refs)
    for head in range(heads):
        lanes = slice(head * HEAD_DIM, (head + 1) * HEAD_DIM)
        spans = [
            slice((head * RATIO + at) * HEAD_DIM, (head * RATIO + at + 1) * HEAD_DIM)
            for at in range(RATIO)
        ]
        visual, text, near = [], [], []
        for part in range(2):
            visual.append(jnp.concatenate([ref[part, :, lanes] for ref in block_refs], axis=0))
            text.append(total_of([text_ref, other_text_ref], (part, slice(None), lanes)))
            near.append(
                jnp.concatenate(
                    [text[part], halo_ref[part, :, lanes], own_ref[0, part, :, lanes]], axis=0
                )
            )
        keys = jnp.concatenate([visual[0], near[0]], axis=0)
        dk_sums = [0.0, 0.0]
        dv_sums = [0.0, 0.0]
        for first in range(0, RATIO, 2):
            pair = spans[first : first + 2]
            q_rows = jnp.concatenate([q_ref[:, span] for span in pair], axis=0)
            d_rows = jnp.concatenate([d_ref[:, span] for span in pair], axis=0)
            outcome = rows_backward(
                [(visual[0], visual[1], whole_bias), (near[0], near[1], near_bias)],
                q_rows,
                d_rows,
            )
            d_scores = jnp.concatenate([part[1] for part in outcome], axis=0)
            dq = dot_tn(keys, d_scores) * SCORE_SCALE
            for at, span in enumerate(pair):
                dq_ref[:, span] = dq[:, at * own : (at + 1) * own].T.astype(jnp.bfloat16)
            for at, (weights, d_part) in enumerate(outcome):
                dk_sums[at] = dk_sums[at] + dot_nn(d_part, q_rows)
                dv_sums[at] = dv_sums[at] + dot_nn(weights, d_rows)
        image_queries = iq_ref[number_ref[1]]
        q_rows = jnp.concatenate([image_queries[:, span] for span in spans], axis=0)
        d_rows = jnp.concatenate([image_cotangent[:, span] for span in spans], axis=0)
        outcome = rows_backward(
            [
                (visual[0], visual[1], image_bias_ref[:VIS]),
                (text[0], text[1], image_bias_ref[VIS:]),
            ],
            q_rows,
            d_rows,
        )
        d_scores = jnp.concatenate([part[1] for part in outcome], axis=0)
        dq = (dot_tn(keys[:PREFIX], d_scores) * SCORE_SCALE).T.astype(jnp.bfloat16)
        for at, span in enumerate(spans):
            diq_ref[:, span] = dq[at * IMAGE_BLOCK : (at + 1) * IMAGE_BLOCK]
        (visual_w, visual_d), (text_w, text_d) = outcome
        for part, sums, pieces, rows, scale in (
            (0, dk_sums, (visual_d, text_d), q_rows, SCORE_SCALE),
            (1, dv_sums, (visual_w, text_w), d_rows, 1.0),
        ):
            of_visual = (sums[0] + dot_nn(pieces[0], rows)) * scale
            of_text = (sums[1][:PROMPT] + dot_nn(pieces[1], rows)) * scale
            rest = sums[1][PROMPT:] * scale
            of_visual = of_visual.astype(jnp.bfloat16)
            dmine_ref[part, :, lanes] = of_visual[: VIS // 2]
            dpair_ref[part, : VIS // 2, lanes] = of_visual[VIS // 2 :]
            dpair_ref[part, VIS // 2 :, lanes] = of_text.astype(jnp.bfloat16)
            dhalo_ref[part, :, lanes] = rest[:halo].astype(jnp.bfloat16)
            down_ref[part, :, lanes] = rest[halo:]


def attend(
    number, masks, queries, cotangent, every_q, text, other_text, halo_kv, own_kv, blocks, windows
):
    heads = 2
    near_bias, whole_bias, image_bias = masks
    own = queries.shape[0]
    halo = halo_kv.shape[1]
    groups = every_q.shape[0]
    columns = PREFIX + halo + own
    products = RATIO * (own * columns + IMAGE_BLOCK * PREFIX) * KV_HEADS
    spec = pl.BlockSpec
    kv_spec = lambda rows: spec((2, rows, heads * HEAD_DIM), lambda at: (0, 0, at))
    q_spec = lambda rows: spec((rows, heads * GROUP_WIDTH), lambda at: (0, at))
    whole = lambda rows: spec((rows, 128), lambda at: (0, 0))
    return pl.pallas_call(
        functools.partial(attend_kernel, len(blocks), len(windows), heads, halo, own),
        grid=(KV_HEADS // heads,),
        in_specs=[
            spec(memory_space=pltpu.SMEM),
            whole(columns - VIS),
            whole(8),
            whole(PREFIX),
            q_spec(own),
            q_spec(own),
            spec((groups, IMAGE_BLOCK, heads * GROUP_WIDTH), lambda at: (0, 0, at)),
            kv_spec(PROMPT),
            kv_spec(PROMPT),
            kv_spec(halo),
            spec((1, 2, own, heads * HEAD_DIM), lambda at: (0, 0, 0, at)),
        ]
        + [kv_spec(block.shape[1]) for block in blocks]
        + [q_spec(IMAGE_BLOCK) for _ in windows],
        out_specs=[
            q_spec(own),
            q_spec(IMAGE_BLOCK),
            kv_spec(VIS // 2),
            kv_spec(VIS // 2 + PROMPT),
            kv_spec(halo),
            kv_spec(own),
        ],
        out_shape=[
            jax.ShapeDtypeStruct((own, Q_WIDTH), jnp.bfloat16),
            jax.ShapeDtypeStruct((IMAGE_BLOCK, Q_WIDTH), jnp.bfloat16),
            jax.ShapeDtypeStruct((2, VIS // 2, KV_WIDTH), jnp.bfloat16),
            jax.ShapeDtypeStruct((2, VIS // 2 + PROMPT, KV_WIDTH), jnp.bfloat16),
            jax.ShapeDtypeStruct((2, halo, KV_WIDTH), jnp.bfloat16),
            jax.ShapeDtypeStruct((2, own, KV_WIDTH), jnp.float32),
        ],
        cost_estimate=pl.CostEstimate(
            flops=10 * products * HEAD_DIM,
            bytes_accessed=12 * 1024 * 1024,
            transcendentals=products,
        ),
    )(
        number,
        near_bias,
        whole_bias,
        image_bias,
        queries,
        cotangent,
        every_q,
        text,
        other_text,
        halo_kv,
        own_kv,
        *blocks,
        *windows,
    )


def route(rows, number, back):
    groups = lax.axis_size("rollout")
    if groups != 4:
        every = lax.all_gather(rows, "rollout", axis=0)
        return lax.dynamic_index_in_dim(every, number[2 if back else 1], 0, keepdims=False)

    def branch(images):
        pairs = [(g, i) if back else (i, g) for g, i in enumerate(images)]
        return lambda moved: lax.ppermute(moved, "rollout", pairs)

    orders = itertools.permutations(range(groups))
    return lax.switch(number[0], [branch(images) for images in orders], rows)


def window_rounds(ctx_size, tok_rows, image_rows):
    rounds = []
    for target in range(ctx_size):
        lowest = (image_rows * target + 1) // tok_rows
        highest = (image_rows * target + image_rows - 1 + PROMPT - 1) // tok_rows
        for source in range(lowest, highest + 1):
            if source == target:
                continue
            for pairs in rounds:
                if all(s != source and t != target for s, t in pairs):
                    pairs.append((source, target))
                    break
            else:
                rounds.append([(source, target)])
    return rounds


def image_windows(windows, rounds):
    parts = [windows[0]] + [
        lax.ppermute(rows, "ctx", pairs) for rows, pairs in zip(windows[1:], rounds)
    ]
    if len(parts) > 8:
        parts = [sum(part.astype(jnp.float32) for part in parts).astype(jnp.bfloat16)]
    return parts


def text_strides(ctx_size, late_shard):
    strides = [1 << at for at in range(1, ctx_size.bit_length() - 1)]
    return [stride for stride in reversed(strides) if stride != late_shard]


def chip_steps(ctx_size):
    return list(range(2, ctx_size, 2))


def gather_prefix(image_kv):
    ctx_size = lax.axis_size("ctx")
    swap = [(at, at ^ 1) for at in range(ctx_size)]
    mine = [image_kv] + [
        lax.ppermute(image_kv, "ctx", [(at, at ^ step) for at in range(ctx_size)])
        for step in chip_steps(ctx_size)
    ]
    if len(mine) > 4:
        mine = [jnp.concatenate(mine, axis=1)]
    return mine + [lax.ppermute(block, "ctx", swap) for block in mine]


def reduce_prefix(d_mine, d_pair, image_rows, later):
    ctx_size = lax.axis_size("ctx")
    other = lax.ppermute(d_pair, "ctx", [(at, at ^ 1) for at in range(ctx_size)])
    chip = d_mine.astype(jnp.float32) + other[:, : VIS // 2].astype(jnp.float32)
    text = d_pair[:, VIS // 2 :].astype(jnp.float32) + other[:, VIS // 2 :].astype(jnp.float32)
    steps = chip_steps(ctx_size)
    rows = [
        chip[:, place * image_rows : (place + 1) * image_rows].astype(jnp.bfloat16)
        for place in range(1, len(steps) + 1)
    ]
    rows, later = lax.optimization_barrier((rows, later))
    total = chip[:, :image_rows]
    for step, part in zip(steps, rows):
        moved = lax.ppermute(part, "ctx", [(at, at ^ step) for at in range(ctx_size)])
        total = total + moved.astype(jnp.float32)
    return total, text.astype(jnp.bfloat16), later


def swap_text(text, late_shard):
    return lax.ppermute(text, "ctx", [(0, late_shard), (late_shard, 0)])


def spread_text(text, late_shard):
    ctx_size = lax.axis_size("ctx")
    holders = [0, late_shard]
    for stride in text_strides(ctx_size, late_shard):
        pairs = [(at, at + stride) for at in holders]
        text = text + lax.ppermute(text, "ctx", pairs)
        holders += [at + stride for at in holders]
    return text, lax.ppermute(text, "ctx", [(at, at + 1) for at in holders])


def collect_text(text, late_shard):
    ctx_size = lax.axis_size("ctx")

    def add(text, pairs):
        moved = lax.ppermute(text, "ctx", pairs)
        return (text.astype(jnp.float32) + moved.astype(jnp.float32)).astype(jnp.bfloat16)

    strides = text_strides(ctx_size, late_shard)
    for place in range(len(strides) - 1, -1, -1):
        holders = [0, late_shard]
        for stride in strides[:place]:
            holders += [at + stride for at in holders]
        text = add(text, [(at + strides[place], at) for at in holders])
    return text.astype(jnp.float32) + swap_text(text, late_shard).astype(jnp.float32)


def halo_cuts(tok_rows, halo):
    cuts = []
    left = halo
    while left > 0:
        cuts.append(min(left, tok_rows))
        left -= cuts[-1]
    return cuts


def halo_rows(tail, halo, tok_rows):
    ctx_size = lax.axis_size("ctx")
    parts = []
    for step, count in enumerate(halo_cuts(tok_rows, halo), 1):
        pairs = [(at, at + step) for at in range(ctx_size - step)]
        rows = tail if count == tail.shape[1] else tail[:, tail.shape[1] - count :]
        parts.insert(0, lax.ppermute(rows, "ctx", pairs))
    return jnp.concatenate(parts, axis=1) if len(parts) > 1 else parts[0]


def halo_return(d_halo, tok_rows):
    halo = d_halo.shape[1]
    ctx_size = lax.axis_size("ctx")
    total = None
    end = halo
    for step, count in enumerate(halo_cuts(tok_rows, halo), 1):
        pairs = [(at + step, at) for at in range(ctx_size - step)]
        part = lax.ppermute(d_halo[:, end - count : end], "ctx", pairs).astype(jnp.float32)
        part = jnp.pad(part, ((0, 0), (tok_rows - count, 0), (0, 0)))
        total = part if total is None else total + part
        end -= count
    return total


def gather_queries(image_q):
    every = lax.all_gather(image_q, "rollout", axis=0)
    missing = IMAGE_BLOCK - every.shape[1]
    return jnp.pad(every, ((0, 0), (0, missing), (0, 0))) if missing else every


def per_device(queries, keys_values, image_rows, cotangent, seq_image, vis_start, comp_lengths):
    tok_rows = queries.shape[1]
    image_count = image_rows.shape[1]
    ctx_size = lax.axis_size("ctx")
    here = lax.axis_index("ctx")
    seq_len = tok_rows * ctx_size
    late_shard = VIS // tok_rows
    longest = 4 * (seq_len - PREFIX) // (3 * NCOMP)
    halo = -(-(longest - 1) // 64) * 64
    q_own, d_own = queries[0], cotangent[0]

    number, image_kv, image_q, text, tail = first_arrays(
        seq_image, vis_start, image_rows, keys_values, halo
    )
    every_q = gather_queries(image_q)
    swapped = swap_text(text, late_shard)
    image_kv = route(image_kv, number, False)
    blocks = gather_prefix(image_kv)
    image_kv, d_later = lax.optimization_barrier((image_kv, d_own))
    windows, rounds, (*masks, text) = second_arrays(
        vis_start, comp_lengths, d_later, text, swapped, image_count, halo
    )
    windows = image_windows(windows, rounds)
    text, other_text = spread_text(text, late_shard)
    halo_kv = halo_rows(tail, halo, tok_rows)

    grad_q, d_image_q, d_mine, d_pair, d_halo, d_own_kv = attend(
        number,
        masks,
        q_own,
        d_own,
        every_q,
        text,
        other_text,
        halo_kv,
        keys_values,
        blocks,
        windows,
    )

    sums, d_text, d_image_q = reduce_prefix(d_mine, d_pair, image_count, d_image_q)
    image_dq = route(d_image_q[:image_count], number, True)
    d_text, d_halo, image_dq = lax.optimization_barrier((d_text, d_halo, image_dq))
    text_at = jnp.arange(PROMPT, dtype=jnp.int32)
    text_here = jnp.where(text_at < vis_start[0], here == 0, here == late_shard)[None, :, None]
    text_part = jnp.where(text_here, collect_text(d_text, late_shard), 0.0)
    text_part = jnp.pad(text_part, ((0, 0), (0, tok_rows - PROMPT), (0, 0)))
    grad_kv = (d_own_kv + halo_return(d_halo, tok_rows) + text_part).astype(jnp.bfloat16)
    grad_image = jnp.pad(image_dq, ((0, 0), (0, 2 * KV_WIDTH)))
    sums, grad_image = lax.optimization_barrier((sums, grad_image))
    sums = jnp.concatenate([sums[0], sums[1]], axis=1).astype(jnp.bfloat16)
    image_dkv = route(sums, number, True)
    grad_image = lax.dynamic_update_slice(grad_image, image_dkv, (0, Q_WIDTH))
    return (grad_q[None], grad_kv[None], grad_image[None])


def solution(mesh):
    placed = (
        P("rollout", "ctx", None),
        P("rollout", None, "ctx", None),
        P("rollout", "ctx", None),
        P("rollout", "ctx", None),
        P(),
        P("rollout"),
        P("rollout", None),
    )
    return jax.shard_map(
        per_device,
        mesh=mesh,
        in_specs=placed,
        out_specs=(
            P("rollout", "ctx", None),
            P("rollout", None, "ctx", None),
            P("rollout", "ctx", None),
        ),
        check_vma=False,
    )
```

time: 693 us -> 150 us (0.22); the launches traced: 685 us -> 150 us
  local copies, waits for them, and re-layouts: 256 us -> 6.85 us
  waiting for transfers between devices: 181 us -> 26.7 us
  matrix products: 150 us -> 0 us
  starting transfers between devices: 9.98 us -> 73.1 us
  blocking collectives: 23.4 us -> 0 us
  Pallas kernels: 0 us -> 23 us
  loops' own time: 22.5 us -> 0.12 us
  other arithmetic: 24.6 us -> 4.51 us
    dynamic_update_slice x56 -> x1, local copies, waits for them, and re-layouts: 199 us -> 0.91 us  [per_device(): grad_image = lax.dynamic_update_slice(grad_image, image_dkv, (0, Q_WIDTH))]
    dot_general x288 -> x0, matrix products: 150 us -> none  [the longest x144 75.7 us: contract_last(): lax.dot_general(left, right, (((1,), (1,)), ((), ())), preferred_element_...]
    all_gather x3 -> x1, waiting for transfers between devices: 103 us -> 0.01 us  [gather_queries(): every = lax.all_gather(image_q, 'rollout', axis=0)]
    all_to_all x2 -> x0, waiting for transfers between devices: 76.8 us -> none  [the longest x1 48.4 us: heads_plan(): lax.all_to_all(packed, 'ctx', split_axis=2, concat_axis=1, tiled=True)]
    ppermute x0 -> x27, starting transfers between devices: none -> 73 us  [the longest x6 19 us: image_windows(): lax.ppermute(rows, 'ctx', pairs)]
    ppermute x0 -> x27, waiting for transfers between devices: none -> 26.7 us  [the longest x3 17.6 us: branch(): return lambda moved: lax.ppermute(moved, 'rollout', pairs)]
    all_to_all x1 -> x0, blocking collectives: 23.4 us -> none  [heads_plan(): lax.all_to_all(image_part, 'ctx', split_axis=1, concat_axis=2, tiled=True)]
    pallas_call x0 -> x3, Pallas kernels: none -> 23 us  [the longest x1 16.1 us: attend(): pl.pallas_call(functools.partial(attend_kernel, len(blocks), len(windows)...]
  transfers between devices with their start and end apart: 5 -> 28, of which waited for: 5 -> 6; matrix products, arithmetic and copies ran while one was open for 1% -> 3% of each run, Pallas kernels for 0% -> 3%
where the time goes in v1:
time: 150 us
  starting transfers between devices  73.1 us (49%)
  waiting for transfers between devices  26.7 us (18%)
  Pallas kernels  23 us (15%)
  between operations  15.3 us (10%)
  local copies, waits for them, and re-layouts  6.85 us (5%)
  other arithmetic  4.51 us (3%)
    ppermute x6, starting transfers between devices, image_windows(): lax.ppermute(rows, 'ctx', pairs)  19 us
    ppermute x3, waiting for transfers between devices, branch(): return lambda moved: lax.ppermute(moved, 'rollout', pairs)  17.6 us
    pallas_call x1, Pallas kernels, attend(): pl.pallas_call(functools.partial(attend_kernel, len(blocks), len(windows)...  16.1 us
    ppermute x1, starting transfers between devices, halo_return(): lax.ppermute(d_halo[:, end - count:end], 'ctx', pairs).astype(jnp.float32)  10.7 us
    ppermute x2, starting transfers between devices, swap_text(): return lax.ppermute(text, 'ctx', [(0, late_shard), (late_shard, 0)])  9.6 us
    ppermute x3, starting transfers between devices, branch(): return lambda moved: lax.ppermute(moved, 'rollout', pairs)  8.95 us
    ppermute x1, starting transfers between devices, halo_rows(): parts.insert(0, lax.ppermute(rows, 'ctx', pairs))  7.23 us
    ppermute x1, starting transfers between devices, spread_text(): return (text, lax.ppermute(text, 'ctx', [(at, at + 1) for at in holders]))  6.06 us
  transfers between devices with their start and end apart: 28, of which 6 were waited for; matrix products, arithmetic and copies ran while one was open for 3% of the time, Pallas kernels for 3%

profile of v1, /device:TPU:0, one launch (start us, length us, event | category | flops | bytes accessed | tf_op | source)
XLA Modules:
  0.0 149.6 jit_solution(6871810902697445601)
XLA Ops:
  7.9 2.1 %shard_map.94 = (s32[3]{0:T(128)}, bf16[2,32,1024]{2,1,0:T(8,128)(2,1)S(1)}, bf16[32,4096]{1,0:T(8,128)(2,1)}, bf16[2,64,1024]{2,1,0:T(8,128)(2,1)}, bf16[2,64,1024]{2,1,0:T(8,128)(2,1)}) custom-call(s32[4]{0:T(128)} %seq_ref.1, s32[1]{0:T(128)} %copy.83.vis_ref, bf16[1,32,6144]{2,1,0:T(8,128)(2,1)} %image_ref.1, bf16[1,2,128,1024]{3,2,1,0:T(8,128)(2,1)} %own_ref.1), custom_call_target="tpu_custom_call" | custom-call | tf_op jit(solution)/shard_map/pallas_call | solution.py:86
  10.0 0.9 copy-done.3
  10.9 4.8 %collective-permute-start.72 = (bf16[2,64,1024]{2,1,0:T(8,128)(2,1)S(1)}, bf16[2,64,1024]{2,1,0:T(8,128)(2,1)S(1)}, u32[]{:S(2)}, u32[]{:S(2)}) collective-permute-start(bf16[2,64,1024]{2,1,0:T(8,128)(2,1)S(1)} %copy-done.3), channel_id=1, source_target_pairs={{0,2},{2,0},{8,10},{10,8},{16,18},{18,16},{24,26},{26,24}} | collective-permute-start | bytes 786440 | tf_op jit(solution)/shard_map/ppermute | solution.py:482
  15.8 0.7 copy-done.5
  16.5 8.7 %conditional.3 = (bf16[2,32,1024]{2,1,0:T(8,128)(2,1)}) conditional(s32[]{:T(128)} %bitcast.24, bf16[2,32,1024]{2,1,0:T(8,128)(2,1)S(1)} %get-tuple-element.184, bf16[2,32,1024]{2,1,0:T(8,128)(2,1)S(1)} %get-tuple-element.184, bf16[2,32,1024]{2,1,0:T(8,128)(2,1)S(1)} %get-tuple-element.184, ...), branch_computations={%region_0.0_spmd, %region_1.0_spmd, %region_2.0_spmd, %region_3.0_... | conditional | bytes 524336 | solution.py:413
  16.5 3.7 %collective-permute-start.17 = (bf16[2,32,1024]{2,1,0:T(8,128)(2,1)S(1)}, bf16[2,32,1024]{2,1,0:T(8,128)(2,1)}, u32[]{:S(2)}, u32[]{:S(2)}) collective-permute-start(bf16[2,32,1024]{2,1,0:T(8,128)(2,1)S(1)} %param.17), channel_id=1, source_target_pairs={{16,0},{24,8},{8,16},{0,24},{17,1},{25,9},{9,17},{1,25},{18,2},{26... | collective-permute-start | bytes 393224 | tf_op jit(solution)/shard_map/cond/branch_17_fun/ppermute | solution.py:410
  20.2 5.0 %collective-permute-done.17 = bf16[2,32,1024]{2,1,0:T(8,128)(2,1)} collective-permute-done((bf16[2,32,1024]{2,1,0:T(8,128)(2,1)S(1)}, bf16[2,32,1024]{2,1,0:T(8,128)(2,1)}, u32[]{:S(2)}, u32[]{:S(2)}) %collective-permute-start.17) | collective-permute-done | bytes 131104 | tf_op jit(solution)/shard_map/cond/branch_17_fun/ppermute | solution.py:410
  25.2 0.2 collective-permute-start.78
  25.3 0.7 copy-done.4
  26.0 4.8 %shard_map.95 = (bf16[32,4096]{1,0:T(8,128)(2,1)}, bf16[32,4096]{1,0:T(8,128)(2,1)}, bf16[32,4096]{1,0:T(8,128)(2,1)}, bf16[32,4096]{1,0:T(8,128)(2,1)}, bf16[32...) custom-call(s32[1]{0:T(128)} %copy.83.vis_ref, ...), custom_call_target="tpu_custom_call" | custom-call | tf_op jit(solution)/shard_map/pallas_call | solution.py:175
  30.8 2.4 %collective-permute-start.73 = (bf16[2,64,1024]{2,1,0:T(8,128)(2,1)}, bf16[2,64,1024]{2,1,0:T(8,128)(2,1)S(1)}, u32[]{:S(2)}, u32[]{:S(2)}) collective-permute-start(bf16[2,64,1024]{2,1,0:T(8,128)(2,1)} %get-tuple-element.191), channel_id=1, source_target_pairs={{0,4},{2,6},{8,12},{10,14},{16,20},{18,22},{24,28},{26,30}} | collective-permute-start | bytes 786440 | tf_op jit(solution)/shard_map/ppermute | solution.py:490
  33.4 2.9 %collective-permute-start.76 = (bf16[2,32,1024]{2,1,0:T(8,128)(2,1)}, bf16[2,32,1024]{2,1,0:T(8,128)(2,1)S(1)}, u32[]{:S(2)}, u32[]{:S(2)}) collective-permute-start(bf16[2,32,1024]{2,1,0:T(8,128)(2,1)} %get-tuple-element.222.refs_0_), channel_id=1, source_target_pairs={{0,2},{1,3},{2,0},{3,1},{4,6},{5,7},{6,4},{7,5},{8,10},{9,11},{10,... | collective-permute-start | bytes 393224 | tf_op jit(solution)/shard_map/ppermute | solution.py:455
  36.4 7.2 %collective-permute-start.75 = (bf16[2,64,1024]{2,1,0:T(8,128)(2,1)S(1)}, bf16[2,64,1024]{2,1,0:T(8,128)(2,1)S(1)}, u32[]{:S(2)}, u32[]{:S(2)}) collective-permute-start(bf16[2,64,1024]{2,1,0:T(8,128)(2,1)S(1)} %copy-done.7), channel_id=1, source_target_pairs={{0,1},{1,2},{2,3},{3,4},{4,5},{5,6},{6,7},{8,9},{9,10},{10,11},{11... | collective-permute-start | bytes 786440 | tf_op jit(solution)/shard_map/ppermute | solution.py:526
  43.6 7.0 %collective-permute-start.83 = (bf16[32,4096]{1,0:T(8,128)(2,1)}, bf16[32,4096]{1,0:T(8,128)(2,1)S(1)}, u32[]{:S(2)}, u32[]{:S(2)}) collective-permute-start(bf16[32,4096]{1,0:T(8,128)(2,1)} %get-tuple-element.194), channel_id=1, source_target_pairs={{0,1},{1,2},{2,6},{8,9},{9,10},{10,14},{16,17},{17,18},{18,22},{24... | collective-permute-start | bytes 786440 | tf_op jit(solution)/shard_map/ppermute | solution.py:435
  50.7 6.5 %collective-permute-start.84 = (bf16[32,4096]{1,0:T(8,128)(2,1)}, bf16[32,4096]{1,0:T(8,128)(2,1)S(1)}, u32[]{:S(2)}, u32[]{:S(2)}) collective-permute-start(bf16[32,4096]{1,0:T(8,128)(2,1)} %get-tuple-element.195), channel_id=1, source_target_pairs={{0,2},{1,3},{2,7},{8,10},{9,11},{10,15},{16,18},{17,19},{18,23},{2... | collective-permute-start | bytes 786440 | tf_op jit(solution)/shard_map/ppermute | solution.py:435
  57.2 0.4 collective-permute-start.81
  57.8 1.0 add.36.text_ref
  58.9 0.7 copy-done.24
  59.6 3.5 %collective-permute-start.85 = (bf16[32,4096]{1,0:T(8,128)(2,1)}, bf16[32,4096]{1,0:T(8,128)(2,1)S(1)}, u32[]{:S(2)}, u32[]{:S(2)}) collective-permute-start(bf16[32,4096]{1,0:T(8,128)(2,1)} %get-tuple-element.196), channel_id=1, source_target_pairs={{0,3},{1,4},{8,11},{9,12},{16,19},{17,20},{24,27},{25,28}} | collective-permute-start | bytes 786440 | tf_op jit(solution)/shard_map/ppermute | solution.py:435
  63.1 0.6 copy-done.25
  63.7 0.7 collective-permute-start.86
  64.4 0.7 collective-permute-start.87
  65.1 0.7 collective-permute-start.88
  65.8 6.1 %collective-permute-start.74 = (bf16[2,64,1024]{2,1,0:T(8,128)(2,1)S(1)}, bf16[2,64,1024]{2,1,0:T(8,128)(2,1)S(1)}, u32[]{:S(2)}, u32[]{:S(2)}) collective-permute-start(bf16[2,64,1024]{2,1,0:T(8,128)(2,1)S(1)} %add.36.text_ref), channel_id=1, source_target_pairs={{0,1},{2,3},{4,5},{6,7},{8,9},{10,11},{12,13},{14,15},{16,17},{18,... | collective-permute-start | bytes 786440 | tf_op jit(solution)/shard_map/ppermute | solution.py:492
  72.0 1.0 collective-permute-done.74.other_text_ref
  73.1 0.6 copy-done.18
  73.7 16.1 %shard_map.96 = (bf16[128,4096]{1,0:T(8,128)(2,1)}, bf16[32,4096]{1,0:T(8,128)(2,1)S(1)}, bf16[2,128,1024]{2,1,0:T(8,128)(2,1)}, bf16[2,192,1024]{2,1,0:T(8,128)...) custom-call(s32[3]{0:T(128)} %get-tuple-element.183.number_ref, f32[256,128]{1,0:T(8,128)} %get-tuple-element.187.near_ref, ...), custom_call_target="tpu_custom_call" | custom-call | flops 3103784960 | bytes 12582912 | tf_op jit(solution)/shard_map/pallas_call | solution.py:346
  89.9 0.4 collective-permute-start.89
  90.3 2.1 %collective-permute-done.89 = bf16[2,192,1024]{2,1,0:T(8,128)(2,1)S(1)} collective-permute-done((bf16[2,192,1024]{2,1,0:T(8,128)(2,1)}, bf16[2,192,1024]{2,1,0:T(8,128)(2,1)S(1)}, u32[]{:S(2)}, u32[]{:S(2)}) %collective-permute-start.89) | collective-permute-done | bytes 786464 | tf_op jit(solution)/shard_map/ppermute | solution.py:465
  92.4 1.2 convert_add_fusion
  93.7 10.9 %conditional.4 = (bf16[32,4096]{1,0:T(8,128)(2,1)}) conditional(s32[]{:T(128)} %bitcast.24, bf16[32,4096]{1,0:T(8,128)(2,1)S(1)} %get-tuple-element.206, bf16[32,4096]{1,0:T(8,128)(2,1)S(1)} %get-tuple-element.206, bf16[32,4096]{1,0:T(8,128)(2,1)S(1)} %get-tuple-element.206, ...), branch_computations={%region_24.0_spmd, %region_25.0_spmd, %region_26.0_spmd, %region_2... | conditional | bytes 1048624 | solution.py:413
  93.8 2.9 %collective-permute-start.41 = (bf16[32,4096]{1,0:T(8,128)(2,1)S(1)}, bf16[32,4096]{1,0:T(8,128)(2,1)}, u32[]{:S(2)}, u32[]{:S(2)}) collective-permute-start(bf16[32,4096]{1,0:T(8,128)(2,1)S(1)} %param.41), channel_id=1, source_target_pairs={{0,16},{8,24},{16,8},{24,0},{1,17},{9,25},{17,9},{25,1},{2,18},{10... | collective-permute-start | bytes 786440 | tf_op jit(solution)/shard_map/cond/branch_17_fun/ppermute | solution.py:410
  96.6 8.0 %collective-permute-done.41 = bf16[32,4096]{1,0:T(8,128)(2,1)} collective-permute-done((bf16[32,4096]{1,0:T(8,128)(2,1)S(1)}, bf16[32,4096]{1,0:T(8,128)(2,1)}, u32[]{:S(2)}, u32[]{:S(2)}) %collective-permute-start.41) | collective-permute-done | bytes 262176 | tf_op jit(solution)/shard_map/cond/branch_17_fun/ppermute | solution.py:410
  104.6 1.7 %collective-permute-start.93 = (bf16[2,32,1024]{2,1,0:T(8,128)(2,1)S(1)}, bf16[2,32,1024]{2,1,0:T(8,128)(2,1)S(1)}, u32[]{:S(2)}, u32[]{:S(2)}) collective-permute-start(bf16[2,32,1024]{2,1,0:T(8,128)(2,1)S(1)} %get-tuple-element.209), channel_id=1, source_target_pairs={{0,2},{1,3},{2,0},{3,1},{4,6},{5,7},{6,4},{7,5},{8,10},{9,11},{10,... | collective-permute-start | bytes 393224 | tf_op jit(solution)/shard_map/ppermute | solution.py:476
  106.3 1.5 collective-permute-start.94
  107.8 0.3 collective-permute-start.95
  108.1 1.0 add_convert_fusion.2
  109.1 10.7 %collective-permute-start.90 = (bf16[2,64,1024]{2,1,0:T(8,128)(2,1)S(1)}, bf16[2,64,1024]{2,1,0:T(8,128)(2,1)S(1)}, u32[]{:S(2)}, u32[]{:S(2)}) collective-permute-start(bf16[2,64,1024]{2,1,0:T(8,128)(2,1)S(1)} %copy-done.6), channel_id=1, source_target_pairs={{1,0},{2,1},{3,2},{4,3},{5,4},{6,5},{7,6},{9,8},{10,9},{11,10},{12... | collective-permute-start | bytes 786440 | tf_op jit(solution)/shard_map/ppermute | solution.py:537
  119.9 1.3 collective-permute-start.91
  121.2 1.0 pad.18
  122.3 5.8 %collective-permute-done.91 = bf16[2,64,1024]{2,1,0:T(8,128)(2,1)S(1)} collective-permute-done((bf16[2,64,1024]{2,1,0:T(8,128)(2,1)S(1)}, bf16[2,64,1024]{2,1,0:T(8,128)(2,1)S(1)}, u32[]{:S(2)}, u32[]{:S(2)}) %collective-permute-start.91) | collective-permute-done | bytes 262176 | tf_op jit(solution)/shard_map/ppermute | solution.py:499
  128.2 4.8 %collective-permute-start.92 = (bf16[2,64,1024]{2,1,0:T(8,128)(2,1)S(1)}, bf16[2,64,1024]{2,1,0:T(8,128)(2,1)S(1)}, u32[]{:S(2)}, u32[]{:S(2)}) collective-permute-start(bf16[2,64,1024]{2,1,0:T(8,128)(2,1)S(1)} %add_convert_fusion.1), channel_id=1, source_target_pairs={{0,2},{2,0},{8,10},{10,8},{16,18},{18,16},{24,26},{26,24}} | collective-permute-start | bytes 786440 | tf_op jit(solution)/shard_map/ppermute | solution.py:482
  133.0 7.1 %conditional.5 = (bf16[1,32,2048]{2,1,0:T(8,128)(2,1)}) conditional(s32[]{:T(128)} %bitcast.24, bf16[32,2048]{1,0:T(8,128)(2,1)S(1)} %pad_maximum_fusion, bf16[32,2048]{1,0:T(8,128)(2,1)S(1)} %pad_maximum_fusion, bf16[32,2048]{1,0:T(8,128)(2,1)S(1)} %pad_maximum_fusion, ...), branch_computations={%region_48.49_spmd, %region_49.50_spmd, %region_50.51_spmd, %regio... | conditional | bytes 524336 | solution.py:413
  133.0 2.4 %collective-permute-start.65 = (bf16[32,2048]{1,0:T(8,128)(2,1)S(1)}, bf16[32,2048]{1,0:T(8,128)(2,1)}, u32[]{:S(2)}, u32[]{:S(2)}) collective-permute-start(bf16[32,2048]{1,0:T(8,128)(2,1)S(1)} %param.65), channel_id=1, source_target_pairs={{0,16},{8,24},{16,8},{24,0},{1,17},{9,25},{17,9},{25,1},{2,18},{10... | collective-permute-start | bytes 393224 | tf_op jit(solution)/shard_map/cond/branch_17_fun/ppermute | solution.py:410
  135.5 4.6 %collective-permute-done.65 = bf16[32,2048]{1,0:T(8,128)(2,1)} collective-permute-done((bf16[32,2048]{1,0:T(8,128)(2,1)S(1)}, bf16[32,2048]{1,0:T(8,128)(2,1)}, u32[]{:S(2)}, u32[]{:S(2)}) %collective-permute-start.65) | collective-permute-done | bytes 131104 | tf_op jit(solution)/shard_map/cond/branch_17_fun/ppermute | solution.py:410
  140.1 0.9 constant_dynamic-update-slice_fusion
  141.1 0.6 copy-done.1
  141.7 1.0 fusion
  (80 shorter events, 0.8 us)
Async XLA Ops:
  7.2 65.9 %all-gather.3.cloned.1.call-start = ((), (), s32[]{:S(2)}) async-start(), calls=%async_computation | async-start | bytes 1310720 | tf_op jit(solution)/shard_map/all_gather | solution.py:545
  10.0 1.0 copy-start.3
  10.9 14.4 %collective-permute-start.72 = (bf16[2,64,1024]{2,1,0:T(8,128)(2,1)S(1)}, bf16[2,64,1024]{2,1,0:T(8,128)(2,1)S(1)}, u32[]{:S(2)}, u32[]{:S(2)}) collective-permute-start(bf16[2,64,1024]{2,1,0:T(8,128)(2,1)S(1)} %copy-done.3), channel_id=1, source_target_pairs={{0,2},{2,0},{8,10},{10,8},{16,18},{18,16},{24,26},{26,24}} | collective-permute-start | bytes 786440 | tf_op jit(solution)/shard_map/ppermute | solution.py:482
  16.5 8.7 %collective-permute-start.17 = (bf16[2,32,1024]{2,1,0:T(8,128)(2,1)S(1)}, bf16[2,32,1024]{2,1,0:T(8,128)(2,1)}, u32[]{:S(2)}, u32[]{:S(2)}) collective-permute-start(bf16[2,32,1024]{2,1,0:T(8,128)(2,1)S(1)} %param.17), channel_id=1, source_target_pairs={{16,0},{24,8},{8,16},{0,24},{17,1},{25,9},{9,17},{1,25},{18,2},{26... | collective-permute-start | bytes 393224 | tf_op jit(solution)/shard_map/cond/branch_17_fun/ppermute | solution.py:410
  25.2 11.1 %collective-permute-start.78 = (bf16[2,32,1024]{2,1,0:T(8,128)(2,1)}, bf16[2,32,1024]{2,1,0:T(8,128)(2,1)S(1)}, u32[]{:S(2)}, u32[]{:S(2)}) collective-permute-start(bf16[2,32,1024]{2,1,0:T(8,128)(2,1)} %get-tuple-element.222.refs_0_), channel_id=1, source_target_pairs={{0,6},{1,7},{2,4},{3,5},{4,2},{5,3},{6,0},{7,1},{8,14},{9,15},{10,... | collective-permute-start | bytes 393224 | tf_op jit(solution)/shard_map/ppermute | solution.py:455
  25.3 11.0 %copy-start.7 = (bf16[2,64,1024]{2,1,0:T(8,128)(2,1)S(1)}, bf16[2,64,1024]{2,1,0:T(8,128)(2,1)}, u32[]{:S(2)}) copy-start(bf16[2,64,1024]{2,1,0:T(8,128)(2,1)} %get-tuple-element.192) | copy-start | bytes 786436
  30.8 26.8 %collective-permute-start.73 = (bf16[2,64,1024]{2,1,0:T(8,128)(2,1)}, bf16[2,64,1024]{2,1,0:T(8,128)(2,1)S(1)}, u32[]{:S(2)}, u32[]{:S(2)}) collective-permute-start(bf16[2,64,1024]{2,1,0:T(8,128)(2,1)} %get-tuple-element.191), channel_id=1, source_target_pairs={{0,4},{2,6},{8,12},{10,14},{16,20},{18,22},{24,28},{26,30}} | collective-permute-start | bytes 786440 | tf_op jit(solution)/shard_map/ppermute | solution.py:490
  33.2 3.1 %collective-permute-start.79 = (bf16[2,32,1024]{2,1,0:T(8,128)(2,1)}, bf16[2,32,1024]{2,1,0:T(8,128)(2,1)S(1)}, u32[]{:S(2)}, u32[]{:S(2)}) collective-permute-start(bf16[2,32,1024]{2,1,0:T(8,128)(2,1)} %get-tuple-element.222.refs_0_), channel_id=1, source_target_pairs={{0,1},{1,0},{2,3},{3,2},{4,5},{5,4},{6,7},{7,6},{8,9},{9,8},{10,11... | collective-permute-start | bytes 393224 | tf_op jit(solution)/shard_map/ppermute | solution.py:460
  33.3 10.3 %collective-permute-start.77 = (bf16[2,32,1024]{2,1,0:T(8,128)(2,1)}, bf16[2,32,1024]{2,1,0:T(8,128)(2,1)S(1)}, u32[]{:S(2)}, u32[]{:S(2)}) collective-permute-start(bf16[2,32,1024]{2,1,0:T(8,128)(2,1)} %get-tuple-element.222.refs_0_), channel_id=1, source_target_pairs={{0,4},{1,5},{2,6},{3,7},{4,0},{5,1},{6,2},{7,3},{8,12},{9,13},{10,... | collective-permute-start | bytes 393224 | tf_op jit(solution)/shard_map/ppermute | solution.py:455
  33.4 17.3 %collective-permute-start.76 = (bf16[2,32,1024]{2,1,0:T(8,128)(2,1)}, bf16[2,32,1024]{2,1,0:T(8,128)(2,1)S(1)}, u32[]{:S(2)}, u32[]{:S(2)}) collective-permute-start(bf16[2,32,1024]{2,1,0:T(8,128)(2,1)} %get-tuple-element.222.refs_0_), channel_id=1, source_target_pairs={{0,2},{1,3},{2,0},{3,1},{4,6},{5,7},{6,4},{7,5},{8,10},{9,11},{10,... | collective-permute-start | bytes 393224 | tf_op jit(solution)/shard_map/ppermute | solution.py:455
  36.3 22.5 %copy-start.19 = (bf16[2,32,1024]{2,1,0:T(8,128)(2,1)}, bf16[2,32,1024]{2,1,0:T(8,128)(2,1)S(1)}, u32[]{:S(2)}) copy-start(bf16[2,32,1024]{2,1,0:T(8,128)(2,1)S(1)} %collective-permute-done.78.refs_3_) | copy-start | bytes 393220
  36.3 20.9 %collective-permute-start.82 = (bf16[2,32,1024]{2,1,0:T(8,128)(2,1)S(1)}, bf16[2,32,1024]{2,1,0:T(8,128)(2,1)S(1)}, u32[]{:S(2)}, u32[]{:S(2)}) collective-permute-start(bf16[2,32,1024]{2,1,0:T(8,128)(2,1)S(1)} %collective-permute-done.78.refs_3_), channel_id=1, source_target_pairs={{0,1},{1,0},{2,3},{3,2},{4,5},{5,4},{6,7},{7,6},{8,9},{9,8},{10,11... | collective-permute-start | bytes 393224 | tf_op jit(solution)/shard_map/ppermute | solution.py:460
  36.4 22.4 %copy-start.20 = (bf16[2,32,1024]{2,1,0:T(8,128)(2,1)}, bf16[2,32,1024]{2,1,0:T(8,128)(2,1)S(1)}, u32[]{:S(2)}) copy-start(bf16[2,32,1024]{2,1,0:T(8,128)(2,1)S(1)} %collective-permute-done.79.refs_4_) | copy-start | bytes 393220
  36.4 28.0 %collective-permute-start.75 = (bf16[2,64,1024]{2,1,0:T(8,128)(2,1)S(1)}, bf16[2,64,1024]{2,1,0:T(8,128)(2,1)S(1)}, u32[]{:S(2)}, u32[]{:S(2)}) collective-permute-start(bf16[2,64,1024]{2,1,0:T(8,128)(2,1)S(1)} %copy-done.7), channel_id=1, source_target_pairs={{0,1},{1,2},{2,3},{3,4},{4,5},{5,6},{6,7},{8,9},{9,10},{10,11},{11... | collective-permute-start | bytes 786440 | tf_op jit(solution)/shard_map/ppermute | solution.py:526
  43.6 15.2 %copy-start.21 = (bf16[2,32,1024]{2,1,0:T(8,128)(2,1)}, bf16[2,32,1024]{2,1,0:T(8,128)(2,1)S(1)}, u32[]{:S(2)}) copy-start(bf16[2,32,1024]{2,1,0:T(8,128)(2,1)S(1)} %collective-permute-done.77.refs_2_) | copy-start | bytes 393220
  43.6 21.5 %collective-permute-start.83 = (bf16[32,4096]{1,0:T(8,128)(2,1)}, bf16[32,4096]{1,0:T(8,128)(2,1)S(1)}, u32[]{:S(2)}, u32[]{:S(2)}) collective-permute-start(bf16[32,4096]{1,0:T(8,128)(2,1)} %get-tuple-element.194), channel_id=1, source_target_pairs={{0,1},{1,2},{2,6},{8,9},{9,10},{10,14},{16,17},{17,18},{18,22},{24... | collective-permute-start | bytes 786440 | tf_op jit(solution)/shard_map/ppermute | solution.py:435
  50.7 8.2 %copy-start.22 = (bf16[2,32,1024]{2,1,0:T(8,128)(2,1)}, bf16[2,32,1024]{2,1,0:T(8,128)(2,1)S(1)}, u32[]{:S(2)}) copy-start(bf16[2,32,1024]{2,1,0:T(8,128)(2,1)S(1)} %collective-permute-done.76.refs_1_) | copy-start | bytes 393220
  50.7 13.0 %copy-start.10 = (bf16[32,4096]{1,0:T(8,128)(2,1)S(1)}, bf16[32,4096]{1,0:T(8,128)(2,1)}, u32[]{:S(2)}) copy-start(bf16[32,4096]{1,0:T(8,128)(2,1)} %get-tuple-element.197) | copy-start | bytes 786436
  50.7 13.7 %copy-start.9 = (bf16[32,4096]{1,0:T(8,128)(2,1)S(1)}, bf16[32,4096]{1,0:T(8,128)(2,1)}, u32[]{:S(2)}) copy-start(bf16[32,4096]{1,0:T(8,128)(2,1)} %get-tuple-element.198) | copy-start | bytes 786436
  50.7 14.4 %copy-start.8 = (bf16[32,4096]{1,0:T(8,128)(2,1)S(1)}, bf16[32,4096]{1,0:T(8,128)(2,1)}, u32[]{:S(2)}) copy-start(bf16[32,4096]{1,0:T(8,128)(2,1)} %get-tuple-element.199) | copy-start | bytes 786436
  50.7 15.1 %collective-permute-start.84 = (bf16[32,4096]{1,0:T(8,128)(2,1)}, bf16[32,4096]{1,0:T(8,128)(2,1)S(1)}, u32[]{:S(2)}, u32[]{:S(2)}) collective-permute-start(bf16[32,4096]{1,0:T(8,128)(2,1)} %get-tuple-element.195), channel_id=1, source_target_pairs={{0,2},{1,3},{2,7},{8,10},{9,11},{10,15},{16,18},{17,19},{18,23},{2... | collective-permute-start | bytes 786440 | tf_op jit(solution)/shard_map/ppermute | solution.py:435
  57.2 1.7 %copy-start.23 = (bf16[2,32,1024]{2,1,0:T(8,128)(2,1)}, bf16[2,32,1024]{2,1,0:T(8,128)(2,1)S(1)}, u32[]{:S(2)}) copy-start(bf16[2,32,1024]{2,1,0:T(8,128)(2,1)S(1)} %collective-permute-done.82.refs_7_) | copy-start | bytes 393220
  57.2 1.7 %collective-permute-start.81 = (bf16[2,32,1024]{2,1,0:T(8,128)(2,1)S(1)}, bf16[2,32,1024]{2,1,0:T(8,128)(2,1)S(1)}, u32[]{:S(2)}, u32[]{:S(2)}) collective-permute-start(bf16[2,32,1024]{2,1,0:T(8,128)(2,1)S(1)} %collective-permute-done.77.refs_2_), channel_id=1, source_target_pairs={{0,1},{1,0},{2,3},{3,2},{4,5},{5,4},{6,7},{7,6},{8,9},{9,8},{10,11... | collective-permute-start | bytes 393224 | tf_op jit(solution)/shard_map/ppermute | solution.py:460
  57.7 5.4 %collective-permute-start.80 = (bf16[2,32,1024]{2,1,0:T(8,128)(2,1)S(1)}, bf16[2,32,1024]{2,1,0:T(8,128)(2,1)S(1)}, u32[]{:S(2)}, u32[]{:S(2)}) collective-permute-start(bf16[2,32,1024]{2,1,0:T(8,128)(2,1)S(1)} %collective-permute-done.76.refs_1_), channel_id=1, source_target_pairs={{0,1},{1,0},{2,3},{3,2},{4,5},{5,4},{6,7},{7,6},{8,9},{9,8},{10,11... | collective-permute-start | bytes 393224 | tf_op jit(solution)/shard_map/ppermute | solution.py:460
  58.9 14.2 %copy-start.2 = (bf16[2,64,1024]{2,1,0:T(8,128)(2,1)}, bf16[2,64,1024]{2,1,0:T(8,128)(2,1)S(1)}, u32[]{:S(2)}) copy-start(bf16[2,64,1024]{2,1,0:T(8,128)(2,1)S(1)} %add.36.text_ref) | copy-start | bytes 786436
  59.6 12.4 %collective-permute-start.85 = (bf16[32,4096]{1,0:T(8,128)(2,1)}, bf16[32,4096]{1,0:T(8,128)(2,1)S(1)}, u32[]{:S(2)}, u32[]{:S(2)}) collective-permute-start(bf16[32,4096]{1,0:T(8,128)(2,1)} %get-tuple-element.196), channel_id=1, source_target_pairs={{0,3},{1,4},{8,11},{9,12},{16,19},{17,20},{24,27},{25,28}} | collective-permute-start | bytes 786440 | tf_op jit(solution)/shard_map/ppermute | solution.py:435
  63.7 8.2 %collective-permute-start.86 = (bf16[32,4096]{1,0:T(8,128)(2,1)S(1)}, bf16[32,4096]{1,0:T(8,128)(2,1)S(1)}, u32[]{:S(2)}, u32[]{:S(2)}) collective-permute-start(bf16[32,4096]{1,0:T(8,128)(2,1)S(1)} %copy-done.10), channel_id=1, source_target_pairs={{1,5},{9,13},{17,21},{25,29}} | collective-permute-start | bytes 786440 | tf_op jit(solution)/shard_map/ppermute | solution.py:435
  64.4 8.6 %copy-start.11 = (bf16[2,64,1024]{2,1,0:T(8,128)(2,1)}, bf16[2,64,1024]{2,1,0:T(8,128)(2,1)S(1)}, u32[]{:S(2)}) copy-start(bf16[2,64,1024]{2,1,0:T(8,128)(2,1)S(1)} %collective-permute-done.75.halo_ref) | copy-start | bytes 786436
  64.4 7.5 %collective-permute-start.87 = (bf16[32,4096]{1,0:T(8,128)(2,1)S(1)}, bf16[32,4096]{1,0:T(8,128)(2,1)S(1)}, u32[]{:S(2)}, u32[]{:S(2)}) collective-permute-start(bf16[32,4096]{1,0:T(8,128)(2,1)S(1)} %copy-done.9), channel_id=1, source_target_pairs={{1,6},{9,14},{17,22},{25,30}} | collective-permute-start | bytes 786440 | tf_op jit(solution)/shard_map/ppermute | solution.py:435
  65.1 7.9 %copy-start.12 = (bf16[32,4096]{1,0:T(8,128)(2,1)}, bf16[32,4096]{1,0:T(8,128)(2,1)S(1)}, u32[]{:S(2)}) copy-start(bf16[32,4096]{1,0:T(8,128)(2,1)S(1)} %collective-permute-done.83.refs_9_) | copy-start | bytes 786436
  65.1 6.8 %collective-permute-start.88 = (bf16[32,4096]{1,0:T(8,128)(2,1)S(1)}, bf16[32,4096]{1,0:T(8,128)(2,1)S(1)}, u32[]{:S(2)}, u32[]{:S(2)}) collective-permute-start(bf16[32,4096]{1,0:T(8,128)(2,1)S(1)} %copy-done.8), channel_id=1, source_target_pairs={{1,7},{9,15},{17,23},{25,31}} | collective-permute-start | bytes 786440 | tf_op jit(solution)/shard_map/ppermute | solution.py:435
  65.8 7.2 %copy-start.13 = (bf16[32,4096]{1,0:T(8,128)(2,1)}, bf16[32,4096]{1,0:T(8,128)(2,1)S(1)}, u32[]{:S(2)}) copy-start(bf16[32,4096]{1,0:T(8,128)(2,1)S(1)} %collective-permute-done.84.refs_10_) | copy-start | bytes 786436
  65.8 7.2 %collective-permute-start.74 = (bf16[2,64,1024]{2,1,0:T(8,128)(2,1)S(1)}, bf16[2,64,1024]{2,1,0:T(8,128)(2,1)S(1)}, u32[]{:S(2)}, u32[]{:S(2)}) collective-permute-start(bf16[2,64,1024]{2,1,0:T(8,128)(2,1)S(1)} %add.36.text_ref), channel_id=1, source_target_pairs={{0,1},{2,3},{4,5},{6,7},{8,9},{10,11},{12,13},{14,15},{16,17},{18,... | collective-permute-start | bytes 786440 | tf_op jit(solution)/shard_map/ppermute | solution.py:492
  71.9 1.2 copy-start.14
  71.9 1.1 copy-start.15
  72.0 1.1 copy-start.16
  72.0 1.1 copy-start.17
  89.9 2.6 %collective-permute-start.89 = (bf16[2,192,1024]{2,1,0:T(8,128)(2,1)}, bf16[2,192,1024]{2,1,0:T(8,128)(2,1)S(1)}, u32[]{:S(2)}, u32[]{:S(2)}) collective-permute-start(bf16[2,192,1024]{2,1,0:T(8,128)(2,1)} %get-tuple-element.202), channel_id=1, source_target_pairs={{0,1},{1,0},{2,3},{3,2},{4,5},{5,4},{6,7},{7,6},{8,9},{9,8},{10,11... | collective-permute-start | bytes 2359304 | tf_op jit(solution)/shard_map/ppermute | solution.py:465
  93.8 10.9 %collective-permute-start.41 = (bf16[32,4096]{1,0:T(8,128)(2,1)S(1)}, bf16[32,4096]{1,0:T(8,128)(2,1)}, u32[]{:S(2)}, u32[]{:S(2)}) collective-permute-start(bf16[32,4096]{1,0:T(8,128)(2,1)S(1)} %param.41), channel_id=1, source_target_pairs={{0,16},{8,24},{16,8},{24,0},{1,17},{9,25},{17,9},{25,1},{2,18},{10... | collective-permute-start | bytes 786440 | tf_op jit(solution)/shard_map/cond/branch_17_fun/ppermute | solution.py:410
  104.6 4.5 %copy-start.6 = (bf16[2,64,1024]{2,1,0:T(8,128)(2,1)S(1)}, bf16[2,64,1024]{2,1,0:T(8,128)(2,1)}, u32[]{:S(2)}) copy-start(bf16[2,64,1024]{2,1,0:T(8,128)(2,1)} %get-tuple-element.207) | copy-start | bytes 786436
  104.6 17.5 %collective-permute-start.93 = (bf16[2,32,1024]{2,1,0:T(8,128)(2,1)S(1)}, bf16[2,32,1024]{2,1,0:T(8,128)(2,1)S(1)}, u32[]{:S(2)}, u32[]{:S(2)}) collective-permute-start(bf16[2,32,1024]{2,1,0:T(8,128)(2,1)S(1)} %get-tuple-element.209), channel_id=1, source_target_pairs={{0,2},{1,3},{2,0},{3,1},{4,6},{5,7},{6,4},{7,5},{8,10},{9,11},{10,... | collective-permute-start | bytes 393224 | tf_op jit(solution)/shard_map/ppermute | solution.py:476
  106.3 15.9 %collective-permute-start.94 = (bf16[2,32,1024]{2,1,0:T(8,128)(2,1)S(1)}, bf16[2,32,1024]{2,1,0:T(8,128)(2,1)S(1)}, u32[]{:S(2)}, u32[]{:S(2)}) collective-permute-start(bf16[2,32,1024]{2,1,0:T(8,128)(2,1)S(1)} %get-tuple-element.210), channel_id=1, source_target_pairs={{0,4},{1,5},{2,6},{3,7},{4,0},{5,1},{6,2},{7,3},{8,12},{9,13},{10,... | collective-permute-start | bytes 393224 | tf_op jit(solution)/shard_map/ppermute | solution.py:476
  107.8 14.4 %collective-permute-start.95 = (bf16[2,32,1024]{2,1,0:T(8,128)(2,1)S(1)}, bf16[2,32,1024]{2,1,0:T(8,128)(2,1)S(1)}, u32[]{:S(2)}, u32[]{:S(2)}) collective-permute-start(bf16[2,32,1024]{2,1,0:T(8,128)(2,1)S(1)} %get-tuple-element.211), channel_id=1, source_target_pairs={{0,6},{1,7},{2,4},{3,5},{4,2},{5,3},{6,0},{7,1},{8,14},{9,15},{10,... | collective-permute-start | bytes 393224 | tf_op jit(solution)/shard_map/ppermute | solution.py:476
  109.1 32.6 %collective-permute-start.90 = (bf16[2,64,1024]{2,1,0:T(8,128)(2,1)S(1)}, bf16[2,64,1024]{2,1,0:T(8,128)(2,1)S(1)}, u32[]{:S(2)}, u32[]{:S(2)}) collective-permute-start(bf16[2,64,1024]{2,1,0:T(8,128)(2,1)S(1)} %copy-done.6), channel_id=1, source_target_pairs={{1,0},{2,1},{3,2},{4,3},{5,4},{6,5},{7,6},{9,8},{10,9},{11,10},{12... | collective-permute-start | bytes 786440 | tf_op jit(solution)/shard_map/ppermute | solution.py:537
  119.9 8.3 %collective-permute-start.91 = (bf16[2,64,1024]{2,1,0:T(8,128)(2,1)S(1)}, bf16[2,64,1024]{2,1,0:T(8,128)(2,1)S(1)}, u32[]{:S(2)}, u32[]{:S(2)}) collective-permute-start(bf16[2,64,1024]{2,1,0:T(8,128)(2,1)S(1)} %add_convert_fusion.2), channel_id=1, source_target_pairs={{4,0},{6,2},{12,8},{14,10},{20,16},{22,18},{28,24},{30,26}} | collective-permute-start | bytes 786440 | tf_op jit(solution)/shard_map/ppermute | solution.py:499
  122.3 19.5 %copy-start = (f32[2,128,1024]{2,1,0:T(8,128)S(1)}, f32[2,128,1024]{2,1,0:T(8,128)}, u32[]{:S(2)}) copy-start(f32[2,128,1024]{2,1,0:T(8,128)} %get-tuple-element.201) | copy-start | bytes 3145732
  128.2 12.8 %collective-permute-start.92 = (bf16[2,64,1024]{2,1,0:T(8,128)(2,1)S(1)}, bf16[2,64,1024]{2,1,0:T(8,128)(2,1)S(1)}, u32[]{:S(2)}, u32[]{:S(2)}) collective-permute-start(bf16[2,64,1024]{2,1,0:T(8,128)(2,1)S(1)} %add_convert_fusion.1), channel_id=1, source_target_pairs={{0,2},{2,0},{8,10},{10,8},{16,18},{18,16},{24,26},{26,24}} | collective-permute-start | bytes 786440 | tf_op jit(solution)/shard_map/ppermute | solution.py:482
  133.0 7.0 %collective-permute-start.65 = (bf16[32,2048]{1,0:T(8,128)(2,1)S(1)}, bf16[32,2048]{1,0:T(8,128)(2,1)}, u32[]{:S(2)}, u32[]{:S(2)}) collective-permute-start(bf16[32,2048]{1,0:T(8,128)(2,1)S(1)} %param.65), channel_id=1, source_target_pairs={{0,16},{8,24},{16,8},{24,0},{1,17},{9,25},{17,9},{25,1},{2,18},{10... | collective-permute-start | bytes 393224 | tf_op jit(solution)/shard_map/cond/branch_17_fun/ppermute | solution.py:410
  (6 other events, 4.1 us)
Sparse Core Ops, SparseCore 0:
  10.1 30.6 all-gather.2

commit v2 on v1

--- a/solution.py
+++ b/solution.py
@@ -111,9 +111,9 @@
 
 
 def second_kernel(
-    rounds, tok_rows, image_rows, halo, vis_ref, length_ref, d_ref, t_ref, r_ref, *out_refs
+    rounds, tok_rows, image_rows, halo, vis_ref, length_ref, d_ref, *out_refs
 ):
-    *window_refs, near_ref, whole_ref, image_ref, text_ref = out_refs
+    *window_refs, near_ref, whole_ref, image_ref = out_refs
     here = lax.axis_index("ctx")
     ctx_size = lax.axis_size("ctx")
     row = lax.broadcasted_iota(jnp.int32, (IMAGE_BLOCK, tok_rows), 0)
@@ -133,8 +133,6 @@
     @pl.when(pl.program_id(0) == 0)
     def _():
         vis = vis_ref[0]
-        text = t_ref[...].astype(jnp.float32) + r_ref[...].astype(jnp.float32)
-        text_ref[...] = text.astype(jnp.bfloat16)
         own_at = lax.broadcasted_iota(jnp.int32, (8, tok_rows), 1) + here * tok_rows
         own_segment = segments(own_at, length_ref)[:1]
         placeholder = (own_at >= vis) & (own_at < vis + VIS)
@@ -162,11 +160,11 @@
         image_ref[VIS:] = hide(text_at <= image_row)
 
 
-def second_arrays(vis_start, lengths, cotangent, text, received, image_rows, halo):
+def second_arrays(vis_start, lengths, cotangent, image_rows, halo):
     tok_rows, width = cotangent.shape
     rounds = window_rounds(lax.axis_size("ctx"), tok_rows, image_rows)
     count = len(rounds) + 1
-    block = 1024
+    block = 2048
     spec = pl.BlockSpec
     smem = spec(memory_space=pltpu.SMEM)
     lanes = RATIO * IMAGE_BLOCK
@@ -175,29 +173,22 @@
     out = pl.pallas_call(
         functools.partial(second_kernel, rounds, tok_rows, image_rows, halo),
         grid=(width // block,),
-        in_specs=[
-            smem,
-            smem,
-            spec((tok_rows, block), lambda at: (0, at)),
-            whole(2, PROMPT, KV_WIDTH),
-            whole(2, PROMPT, KV_WIDTH),
-        ],
+        in_specs=[smem, smem, spec((tok_rows, block), lambda at: (0, at))],
         out_specs=[spec((IMAGE_BLOCK, block), lambda at: (0, at)) for _ in range(count)]
-        + [
-            whole(near, tok_rows),
-            whole(8, tok_rows),
-            whole(PREFIX, lanes),
-            whole(2, PROMPT, KV_WIDTH),
-        ],
+        + [whole(near, tok_rows), whole(8, tok_rows), whole(PREFIX, lanes)],
         out_shape=[jax.ShapeDtypeStruct((IMAGE_BLOCK, width), jnp.bfloat16) for _ in range(count)]
         + [
             jax.ShapeDtypeStruct((near, tok_rows), jnp.float32),
             jax.ShapeDtypeStruct((8, tok_rows), jnp.float32),
             jax.ShapeDtypeStruct((PREFIX, lanes), jnp.float32),
-            jax.ShapeDtypeStruct((2, PROMPT, KV_WIDTH), jnp.bfloat16),
         ],
-    )(vis_start, lengths, cotangent, text, received)
-    return out[:count], rounds, out[count:]
+        cost_estimate=pl.CostEstimate(
+            flops=2 * count * IMAGE_BLOCK * tok_rows * width,
+            bytes_accessed=8 * 1024 * 1024,
+            transcendentals=0,
+        ),
+    )(vis_start, lengths, cotangent)
+    return out[:count], rounds, list(out[count:])
 
 
 def rows_backward(parts, q_rows, d_rows):
@@ -231,14 +222,16 @@
     return outcome
 
 
-def total_of(refs, at=slice(None)):
-    if len(refs) == 1:
-        return refs[0][at]
-    return sum(ref[at].astype(jnp.float32) for ref in refs).astype(jnp.bfloat16)
+def total_of(values):
+    if len(values) == 1:
+        return values[0]
+    return sum(value.astype(jnp.float32) for value in values).astype(jnp.bfloat16)
 
 
 def attend_kernel(
+    block_rows,
     block_count,
+    text_count,
     window_count,
     heads,
     halo,
@@ -250,20 +243,18 @@
     q_ref,
     d_ref,
     iq_ref,
-    text_ref,
-    other_text_ref,
     halo_ref,
     own_ref,
     *refs,
 ):
-    block_refs = refs[:block_count]
-    window_refs = refs[block_count : block_count + window_count]
-    dq_ref, diq_ref, dmine_ref, dpair_ref, dhalo_ref, down_ref = refs[
-        block_count + window_count :
-    ]
+    block_refs, refs = refs[:block_count], refs[block_count:]
+    text_refs, refs = refs[:text_count], refs[text_count:]
+    window_refs, refs = refs[:window_count], refs[window_count:]
+    dq_ref, diq_ref, dmine_ref, dpair_ref, dhalo_ref, down_ref = refs
+    text_refs = text_refs or [ref for ref in block_refs if ref.shape[1] > block_rows]
     near_bias = jnp.concatenate([near_ref[...]] * 2, axis=1)
     whole_bias = jnp.concatenate([whole_ref[:1]] * 2, axis=1)
-    image_cotangent = total_of(window_refs)
+    image_cotangent = total_of([ref[...] for ref in window_refs])
     for head in range(heads):
         lanes = slice(head * HEAD_DIM, (head + 1) * HEAD_DIM)
         spans = [
@@ -272,8 +263,10 @@
         ]
         visual, text, near = [], [], []
         for part in range(2):
-            visual.append(jnp.concatenate([ref[part, :, lanes] for ref in block_refs], axis=0))
-            text.append(total_of([text_ref, other_text_ref], (part, slice(None), lanes)))
+            visual.append(
+                jnp.concatenate([ref[part, :block_rows, lanes] for ref in block_refs], axis=0)
+            )
+            text.append(total_of([ref[part, -PROMPT:, lanes] for ref in text_refs]))
             near.append(
                 jnp.concatenate(
                     [text[part], halo_ref[part, :, lanes], own_ref[0, part, :, lanes]], axis=0
@@ -330,7 +323,7 @@
 
 
 def attend(
-    number, masks, queries, cotangent, every_q, text, other_text, halo_kv, own_kv, blocks, windows
+    number, masks, queries, cotangent, every_q, halo_kv, own_kv, blocks, texts, windows
 ):
     heads = 2
     near_bias, whole_bias, image_bias = masks
@@ -344,7 +337,16 @@
     q_spec = lambda rows: spec((rows, heads * GROUP_WIDTH), lambda at: (0, at))
     whole = lambda rows: spec((rows, 128), lambda at: (0, 0))
     return pl.pallas_call(
-        functools.partial(attend_kernel, len(blocks), len(windows), heads, halo, own),
+        functools.partial(
+            attend_kernel,
+            VIS // len(blocks),
+            len(blocks),
+            len(texts),
+            len(windows),
+            heads,
+            halo,
+            own,
+        ),
         grid=(KV_HEADS // heads,),
         in_specs=[
             spec(memory_space=pltpu.SMEM),
@@ -354,12 +356,10 @@
             q_spec(own),
             q_spec(own),
             spec((groups, IMAGE_BLOCK, heads * GROUP_WIDTH), lambda at: (0, 0, at)),
-            kv_spec(PROMPT),
-            kv_spec(PROMPT),
             kv_spec(halo),
             spec((1, 2, own, heads * HEAD_DIM), lambda at: (0, 0, 0, at)),
         ]
-        + [kv_spec(block.shape[1]) for block in blocks]
+        + [kv_spec(block.shape[1]) for block in [*blocks, *texts]]
         + [q_spec(IMAGE_BLOCK) for _ in windows],
         out_specs=[
             q_spec(own),
@@ -390,27 +390,34 @@
         queries,
         cotangent,
         every_q,
-        text,
-        other_text,
         halo_kv,
         own_kv,
         *blocks,
+        *texts,
         *windows,
     )
 
 
-def route(rows, number, back):
+def route(rows, number, back, beside=()):
     groups = lax.axis_size("rollout")
+    arrays = [array for array, _ in beside]
+
+    def move_beside(arrays):
+        return [lax.ppermute(array, "ctx", pairs) for array, (_, pairs) in zip(arrays, beside)]
+
     if groups != 4:
         every = lax.all_gather(rows, "rollout", axis=0)
-        return lax.dynamic_index_in_dim(every, number[2 if back else 1], 0, keepdims=False)
+        picked = lax.dynamic_index_in_dim(every, number[2 if back else 1], 0, keepdims=False)
+        return [picked] + move_beside(arrays)
 
     def branch(images):
         pairs = [(g, i) if back else (i, g) for g, i in enumerate(images)]
-        return lambda moved: lax.ppermute(moved, "rollout", pairs)
+        if all(source == target for source, target in pairs):
+            return lambda rows, arrays: [rows] + move_beside(arrays)
+        return lambda rows, arrays: [lax.ppermute(rows, "rollout", pairs)] + move_beside(arrays)
 
     orders = itertools.permutations(range(groups))
-    return lax.switch(number[0], [branch(images) for images in orders], rows)
+    return lax.switch(number[0], [branch(images) for images in orders], rows, arrays)
 
 
 def window_rounds(ctx_size, tok_rows, image_rows):
@@ -430,15 +437,51 @@
     return rounds
 
 
-def image_windows(windows, rounds):
-    parts = [windows[0]] + [
-        lax.ppermute(rows, "ctx", pairs) for rows, pairs in zip(windows[1:], rounds)
-    ]
+def window_beside(ctx_size, rounds):
+    return [2, 3, 4] if ctx_size == 8 and len(rounds) == 6 else []
+
+
+def image_windows(windows, rounds, beside, moved):
+    moved = dict(zip(beside, moved))
+    parts = [windows[0]]
+    for at, (rows, pairs) in enumerate(zip(windows[1:], rounds)):
+        parts.append(moved[at] if at in moved else lax.ppermute(rows, "ctx", pairs))
     if len(parts) > 8:
         parts = [sum(part.astype(jnp.float32) for part in parts).astype(jnp.bfloat16)]
     return parts
 
 
+def xor_pairs(step):
+    return [(at, at ^ step) for at in range(lax.axis_size("ctx"))]
+
+
+def xor_permute(rows, step):
+    return lax.ppermute(rows, "ctx", xor_pairs(step))
+
+
+def on_device(function, *arrays):
+    if lax.axis_size("ctx") != 8:
+        return function(*arrays)
+    block = KV_WIDTH // 2
+    shapes = jax.eval_shape(function, *arrays)
+
+    def kernel(*refs):
+        for out_ref, value in zip(
+            refs[len(arrays) :], function(*[ref[...] for ref in refs[: len(arrays)]])
+        ):
+            out_ref[...] = value
+
+    spec = lambda array: pl.BlockSpec(array.shape[:2] + (block,), lambda at: (0, 0, at))
+    return pl.pallas_call(
+        kernel,
+        grid=(2,),
+        in_specs=[spec(array) for array in arrays],
+        out_specs=[spec(shape) for shape in shapes],
+        out_shape=[jax.ShapeDtypeStruct(shape.shape, shape.dtype) for shape in shapes],
+        cost_estimate=pl.CostEstimate(flops=1, bytes_accessed=1, transcendentals=0),
+    )(*arrays)
+
+
 def text_strides(ctx_size, late_shard):
     strides = [1 << at for at in range(1, ctx_size.bit_length() - 1)]
     return [stride for stride in reversed(strides) if stride != late_shard]
@@ -448,64 +491,66 @@
     return list(range(2, ctx_size, 2))
 
 
-def gather_prefix(image_kv):
+def join_text(image_kv, text, received):
+    return [jnp.concatenate([image_kv, add_text(text, received)], axis=1)]
+
+
+def add_text(text, received):
+    return (text.astype(jnp.float32) + received.astype(jnp.float32)).astype(jnp.bfloat16)
+
+
+def gather_prefix(image_kv, text, received, late_shard):
     ctx_size = lax.axis_size("ctx")
-    swap = [(at, at ^ 1) for at in range(ctx_size)]
-    mine = [image_kv] + [
-        lax.ppermute(image_kv, "ctx", [(at, at ^ step) for at in range(ctx_size)])
-        for step in chip_steps(ctx_size)
-    ]
-    if len(mine) > 4:
-        mine = [jnp.concatenate(mine, axis=1)]
-    return mine + [lax.ppermute(block, "ctx", swap) for block in mine]
-
-
-def reduce_prefix(d_mine, d_pair, image_rows, later):
-    ctx_size = lax.axis_size("ctx")
-    other = lax.ppermute(d_pair, "ctx", [(at, at ^ 1) for at in range(ctx_size)])
-    chip = d_mine.astype(jnp.float32) + other[:, : VIS // 2].astype(jnp.float32)
-    text = d_pair[:, VIS // 2 :].astype(jnp.float32) + other[:, VIS // 2 :].astype(jnp.float32)
     steps = chip_steps(ctx_size)
-    rows = [
-        chip[:, place * image_rows : (place + 1) * image_rows].astype(jnp.bfloat16)
-        for place in range(1, len(steps) + 1)
-    ]
-    rows, later = lax.optimization_barrier((rows, later))
-    total = chip[:, :image_rows]
-    for step, part in zip(steps, rows):
-        moved = lax.ppermute(part, "ctx", [(at, at ^ step) for at in range(ctx_size)])
-        total = total + moved.astype(jnp.float32)
-    return total, text.astype(jnp.bfloat16), later
-
-
-def swap_text(text, late_shard):
-    return lax.ppermute(text, "ctx", [(0, late_shard), (late_shard, 0)])
+    if ctx_size == 8:
+        (text,) = on_device(join_text, image_kv, text, received)
+        mine = [text, xor_permute(image_kv, 2), xor_permute(text, 4), xor_permute(image_kv, 6)]
+        pair = [xor_permute(mine[0], 1)]
+        for at, earlier in ((1, None), (3, 0), (2, 1)):
+            block = mine[at]
+            if earlier is not None:
+                block, pair[earlier] = lax.optimization_barrier((block, pair[earlier]))
+            pair.append(xor_permute(block, 1))
+        return mine + [pair[0], pair[1], pair[3], pair[2]], []
+    mine = jnp.concatenate(
+        [image_kv] + [xor_permute(image_kv, step) for step in steps], axis=1
+    )
+    return [mine, xor_permute(mine, 1)], list(spread_text(add_text(text, received), late_shard))
+
+
+def split_sums(image_rows, steps, d_mine, d_pair, other):
+    half = VIS // 2
+    add = lambda one, two: one.astype(jnp.float32) + two.astype(jnp.float32)
+    text = add(d_pair[:, half:], other[:, half:])
+    out = []
+    for at in range(len(steps) + 1):
+        rows = slice(at * image_rows, (at + 1) * image_rows)
+        sums = add(d_mine[:, rows], other[:, rows])
+        if len(steps) == 3 and steps[at - 1] == 4 and at:
+            sums = jnp.concatenate([sums, text], axis=1)
+        out.append(sums.astype(jnp.bfloat16) if at else sums)
+    return out + [text]
+
+
+def add_sums(image_rows, own, text, *parts):
+    for part in parts:
+        own = own + part[:, :image_rows].astype(jnp.float32)
+        if part.shape[1] > image_rows:
+            text = text + part[:, image_rows:].astype(jnp.float32)
+    return [own.astype(jnp.bfloat16), text.astype(jnp.bfloat16)]
 
 
 def spread_text(text, late_shard):
-    ctx_size = lax.axis_size("ctx")
-    holders = [0, late_shard]
-    for stride in text_strides(ctx_size, late_shard):
-        pairs = [(at, at + stride) for at in holders]
-        text = text + lax.ppermute(text, "ctx", pairs)
-        holders += [at + stride for at in holders]
-    return text, lax.ppermute(text, "ctx", [(at, at + 1) for at in holders])
+    for stride in text_strides(lax.axis_size("ctx"), late_shard):
+        text = text + xor_permute(text, stride)
+    return text, xor_permute(text, 1)
 
 
 def collect_text(text, late_shard):
-    ctx_size = lax.axis_size("ctx")
-
-    def add(text, pairs):
-        moved = lax.ppermute(text, "ctx", pairs)
-        return (text.astype(jnp.float32) + moved.astype(jnp.float32)).astype(jnp.bfloat16)
-
-    strides = text_strides(ctx_size, late_shard)
-    for place in range(len(strides) - 1, -1, -1):
-        holders = [0, late_shard]
-        for stride in strides[:place]:
-            holders += [at + stride for at in holders]
-        text = add(text, [(at + strides[place], at) for at in holders])
-    return text.astype(jnp.float32) + swap_text(text, late_shard).astype(jnp.float32)
+    for stride in reversed(text_strides(lax.axis_size("ctx"), late_shard)):
+        moved = xor_permute(text.astype(jnp.bfloat16), stride)
+        text = text.astype(jnp.float32) + moved.astype(jnp.float32)
+    return text.astype(jnp.bfloat16)
 
 
 def halo_cuts(tok_rows, halo):
@@ -527,18 +572,68 @@
     return jnp.concatenate(parts, axis=1) if len(parts) > 1 else parts[0]
 
 
-def halo_return(d_halo, tok_rows):
-    halo = d_halo.shape[1]
+def halo_parts(d_halo, tok_rows):
     ctx_size = lax.axis_size("ctx")
-    total = None
-    end = halo
-    for step, count in enumerate(halo_cuts(tok_rows, halo), 1):
-        pairs = [(at + step, at) for at in range(ctx_size - step)]
-        part = lax.ppermute(d_halo[:, end - count : end], "ctx", pairs).astype(jnp.float32)
-        part = jnp.pad(part, ((0, 0), (tok_rows - count, 0), (0, 0)))
-        total = part if total is None else total + part
+    cuts = halo_cuts(tok_rows, d_halo.shape[1])
+    parts = []
+    end = d_halo.shape[1]
+    for step, count in enumerate(cuts, 1):
+        rows = d_halo if len(cuts) == 1 else d_halo[:, end - count : end]
+        parts.append((rows, [(at + step, at) for at in range(ctx_size - step)]))
         end -= count
-    return total
+    return parts
+
+
+def last_kernel(
+    number_ref, vis_ref, dq_ref, dkv_ref, down_ref, text_ref, other_ref, *refs
+):
+    *part_refs, image_ref, kv_ref = refs
+    here = lax.axis_index("ctx")
+    tok_rows = down_ref.shape[1]
+    image_ref[0, :, :Q_WIDTH] = dq_ref[0]
+    image_ref[0, :, Q_WIDTH : Q_WIDTH + KV_WIDTH] = dkv_ref[0]
+    image_ref[0, :, Q_WIDTH + KV_WIDTH :] = dkv_ref[1]
+    at = lax.broadcasted_iota(jnp.int32, (PROMPT, KV_WIDTH), 0)
+    ahead = jnp.where(here == 0, 1, 0)
+    behind = jnp.where(here == VIS // tok_rows, 1, 0)
+    kept = jnp.where(at < vis_ref[0], ahead, behind) == 1
+    for part in range(2):
+        text = text_ref[part].astype(jnp.float32) + other_ref[part].astype(jnp.float32)
+        text = jnp.where(kept, text, 0.0)
+        sums = down_ref[part] + jnp.concatenate(
+            [text, jnp.zeros((tok_rows - PROMPT, KV_WIDTH), jnp.float32)], axis=0
+        )
+        for part_ref in part_refs:
+            back = part_ref[part].astype(jnp.float32)
+            if back.shape[0] < tok_rows:
+                missing = jnp.zeros((tok_rows - back.shape[0], KV_WIDTH), jnp.float32)
+                back = jnp.concatenate([missing, back], axis=0)
+            sums = sums + back
+        kv_ref[0, part] = sums.astype(jnp.bfloat16)
+
+
+def last_arrays(number, vis_start, every_dq, image_dkv, d_own_kv, text, other_text, parts):
+    rows = image_dkv.shape[1]
+    whole = lambda array: pl.BlockSpec(array.shape, lambda at, number: (0,) * len(array.shape))
+    kept = [image_dkv, d_own_kv, text, other_text, *parts]
+    shapes = [
+        jax.ShapeDtypeStruct((1, rows, Q_WIDTH + 2 * KV_WIDTH), jnp.bfloat16),
+        jax.ShapeDtypeStruct((1,) + d_own_kv.shape, jnp.bfloat16),
+    ]
+    return pl.pallas_call(
+        last_kernel,
+        grid_spec=pltpu.PrefetchScalarGridSpec(
+            num_scalar_prefetch=1,
+            grid=(1,),
+            in_specs=[
+                pl.BlockSpec(memory_space=pltpu.SMEM),
+                pl.BlockSpec((1, rows, Q_WIDTH), lambda at, number: (number[2], 0, 0)),
+            ]
+            + [whole(array) for array in kept],
+            out_specs=[whole(shape) for shape in shapes],
+        ),
+        out_shape=shapes,
+    )(number, vis_start, every_dq, *kept)
 
 
 def gather_queries(image_q):
@@ -551,7 +646,6 @@
     tok_rows = queries.shape[1]
     image_count = image_rows.shape[1]
     ctx_size = lax.axis_size("ctx")
-    here = lax.axis_index("ctx")
     seq_len = tok_rows * ctx_size
     late_shard = VIS // tok_rows
     longest = 4 * (seq_len - PREFIX) // (3 * NCOMP)
@@ -562,15 +656,16 @@
         seq_image, vis_start, image_rows, keys_values, halo
     )
     every_q = gather_queries(image_q)
-    swapped = swap_text(text, late_shard)
-    image_kv = route(image_kv, number, False)
-    blocks = gather_prefix(image_kv)
-    image_kv, d_later = lax.optimization_barrier((image_kv, d_own))
-    windows, rounds, (*masks, text) = second_arrays(
-        vis_start, comp_lengths, d_later, text, swapped, image_count, halo
-    )
-    windows = image_windows(windows, rounds)
-    text, other_text = spread_text(text, late_shard)
+    windows, rounds, masks = second_arrays(vis_start, comp_lengths, d_own, image_count, halo)
+    beside = window_beside(ctx_size, rounds)
+    image_kv, received, *moved = route(
+        image_kv,
+        number,
+        False,
+        [(text, xor_pairs(late_shard))] + [(windows[at + 1], rounds[at]) for at in beside],
+    )
+    windows = image_windows(windows, rounds, beside, moved)
+    blocks, texts = gather_prefix(image_kv, text, received, late_shard)
     halo_kv = halo_rows(tail, halo, tok_rows)
 
     grad_q, d_image_q, d_mine, d_pair, d_halo, d_own_kv = attend(
@@ -579,28 +674,31 @@
         q_own,
         d_own,
         every_q,
-        text,
-        other_text,
         halo_kv,
         keys_values,
         blocks,
+        texts,
         windows,
     )
 
-    sums, d_text, d_image_q = reduce_prefix(d_mine, d_pair, image_count, d_image_q)
-    image_dq = route(d_image_q[:image_count], number, True)
-    d_text, d_halo, image_dq = lax.optimization_barrier((d_text, d_halo, image_dq))
-    text_at = jnp.arange(PROMPT, dtype=jnp.int32)
-    text_here = jnp.where(text_at < vis_start[0], here == 0, here == late_shard)[None, :, None]
-    text_part = jnp.where(text_here, collect_text(d_text, late_shard), 0.0)
-    text_part = jnp.pad(text_part, ((0, 0), (0, tok_rows - PROMPT), (0, 0)))
-    grad_kv = (d_own_kv + halo_return(d_halo, tok_rows) + text_part).astype(jnp.bfloat16)
-    grad_image = jnp.pad(image_dq, ((0, 0), (0, 2 * KV_WIDTH)))
-    sums, grad_image = lax.optimization_barrier((sums, grad_image))
-    sums = jnp.concatenate([sums[0], sums[1]], axis=1).astype(jnp.bfloat16)
-    image_dkv = route(sums, number, True)
-    grad_image = lax.dynamic_update_slice(grad_image, image_dkv, (0, Q_WIDTH))
-    return (grad_q[None], grad_kv[None], grad_image[None])
+    every_dq = lax.all_gather(d_image_q[:image_count], "rollout", axis=0)
+    steps = chip_steps(ctx_size)
+    other = xor_permute(d_pair, 1)
+    own, *sent, d_text = on_device(
+        functools.partial(split_sums, image_count, steps), d_mine, d_pair, other
+    )
+    moved = [xor_permute(rows, step) for rows, step in zip(sent, steps)]
+    halo_back = [
+        lax.ppermute(rows, "ctx", pairs) for rows, pairs in halo_parts(d_halo, tok_rows)
+    ]
+    sums, d_text = on_device(functools.partial(add_sums, image_count), own, d_text, *moved)
+    if ctx_size != 8:
+        d_text = collect_text(d_text, late_shard)
+    image_dkv, other_text = route(sums, number, True, [(d_text, xor_pairs(late_shard))])
+    grad_image, grad_kv = last_arrays(
+        number, vis_start, every_dq, image_dkv, d_own_kv, d_text, other_text, halo_back
+    )
+    return (grad_q[None], grad_kv, grad_image)
 
 
 def solution(mesh):

time: 150 us -> 129 us (0.86); the launches traced: 150 us -> 132 us
  starting transfers between devices: 73.1 us -> 50.9 us
  Pallas kernels: 23 us -> 29.8 us
  other arithmetic: 4.51 us -> 0 us
  waiting for transfers between devices: 26.7 us -> 31 us
  local copies, waits for them, and re-layouts: 6.85 us -> 4.58 us
    ppermute x26 -> x22, starting transfers between devices: 65.8 us -> 49.2 us  [the longest x11 20.6 us: xor_permute(): return lax.ppermute(rows, 'ctx', xor_pairs(step))]
    pallas_call x1 -> x5, Pallas kernels: 16.1 us -> 24.8 us  [the longest x1 16.1 us: attend(): pl.pallas_call(functools.partial(attend_kernel, VIS // len(blocks), len(b...]
    ppermute x1, starting transfers between devices: 7.23 us -> 1.63 us  [halo_rows(): parts.insert(0, lax.ppermute(rows, 'ctx', pairs))]
    ppermute x26 -> x22, waiting for transfers between devices: 26.7 us -> 31 us  [the longest x11 13.7 us: xor_permute(): return lax.ppermute(rows, 'ctx', xor_pairs(step))]
    add x3 -> x0, other arithmetic: 2.34 us -> none  [the longest x1 1.25 us: reduce_prefix(): chip = d_mine.astype(jnp.float32) + other[:, :VIS // 2].astype(jnp.float32)]
    pallas_call x1, Pallas kernels: 4.76 us -> 3.08 us  [second_arrays(): pl.pallas_call(functools.partial(second_kernel, rounds, tok_rows, image_r...]
    unnamed x52 -> x44, local copies, waits for them, and re-layouts: 4.91 us -> 4.56 us
  transfers between devices with their start and end apart: 28 -> 25, of which waited for: 6 -> 8; matrix products, arithmetic and copies ran while one was open for 3% -> 0% of each run, Pallas kernels for 3% -> 7%
where the time goes in v2:
time: 129 us; the launch traced here: 132 us
  starting transfers between devices  50.9 us (39%)
  waiting for transfers between devices  31 us (24%)
  Pallas kernels  29.8 us (23%)
  between operations  15.1 us (12%)
  local copies, waits for them, and re-layouts  4.58 us (4%)
    ppermute x11, starting transfers between devices, xor_permute(): return lax.ppermute(rows, 'ctx', xor_pairs(step))  20.6 us
    pallas_call x1, Pallas kernels, attend(): pl.pallas_call(functools.partial(attend_kernel, VIS // len(blocks), len(b...  16.1 us
    ppermute x11, waiting for transfers between devices, xor_permute(): return lax.ppermute(rows, 'ctx', xor_pairs(step))  13.7 us
    ppermute x2, waiting for transfers between devices, branch(): lax.ppermute(rows, 'rollout', pairs)  12.2 us
    ppermute x5, starting transfers between devices, move_beside(): lax.ppermute(array, 'ctx', pairs)  11.9 us
    ppermute x2, starting transfers between devices, branch(): lax.ppermute(rows, 'rollout', pairs)  11.4 us
    pallas_call x3, Pallas kernels, on_device(): pl.pallas_call(kernel, grid=(2,), in_specs=[spec(array) for array in arra...  5.66 us
    ppermute x3, waiting for transfers between devices, image_windows(): parts.append(moved[at] if at in moved else lax.ppermute(rows, 'ctx', pairs))  5.12 us
  transfers between devices with their start and end apart: 25, of which 8 were waited for; matrix products, arithmetic and copies ran while one was open for 0% of the time, Pallas kernels for 7%

profile of v2, /device:TPU:0, one launch (start us, length us, event | category | flops | bytes accessed | tf_op | source)
XLA Modules:
  0.0 131.7 jit_solution(9186615692043128226)
XLA Ops:
  7.9 2.0 %shard_map.94 = (s32[3]{0:T(128)}, bf16[2,32,1024]{2,1,0:T(8,128)(2,1)S(1)}, bf16[32,4096]{1,0:T(8,128)(2,1)}, bf16[2,64,1024]{2,1,0:T(8,128)(2,1)S(1)}, bf16[2,64,1024]{2,1,0:T(8,128)(2,1)}) custom-call(s32[4]{0:T(128)} %seq_ref.1, s32[1]{0:T(128)S(6)} %copy.178.vis_ref, bf16[1,32,6144]{2,1,0:T(8,128)(2,1)} %image_ref.1, bf16[1,2,128,1024]{3,2,1,0:T(8,128)(2,1)} %own_ref.1), custom_call_target="tpu_custom_call" | custom-call | tf_op jit(solution)/shard_map/pallas_call | solution.py:86
  9.9 0.0 all-gather.7.cloned.1.call-start
  9.9 3.1 %shard_map.95 = (bf16[32,4096]{1,0:T(8,128)(2,1)}, bf16[32,4096]{1,0:T(8,128)(2,1)}, bf16[32,4096]{1,0:T(8,128)(2,1)}, bf16[32,4096]{1,0:T(8,128)(2,1)S(1)}, bf1...) custom-call(s32[1]{0:T(128)S(6)} %copy.178.vis_ref, ...), custom_call_target="tpu_custom_call" | custom-call | flops 234881024 | bytes 8388608 | tf_op jit(solution)/shard_map/pallas_call | solution.py:173
  13.0 0.6 copy-done.5
  13.7 18.0 %conditional.2 = (bf16[2,32,1024]{2,1,0:T(8,128)(2,1)S(1)}, bf16[2,64,1024]{2,1,0:T(8,128)(2,1)}, bf16[32,4096]{1,0:T(8,128)(2,1)}, bf16[32,4096]{1,0:T(8,128)(2,1)}, bf16[32,4096]{1,0:T(8,128)(2,1)}) conditional(s32[]{:T(128)} %bitcast.3, (bf16[2,64,1024]{2,1,0:T(8,128)(2,1)S(1)}, bf16[32,4096]{1,0:T(8,128)(2,1)S(1)}, ...), branch_computations={%region_0.0_spmd, %region_1.0_spmd, %region_2.0_spmd, %region_3.0_... | conditional | bytes 4980976 | solution.py:420
  13.8 3.0 %collective-permute-start.110 = (bf16[2,64,1024]{2,1,0:T(8,128)(2,1)S(1)}, bf16[2,64,1024]{2,1,0:T(8,128)(2,1)}, u32[]{:S(2)}, u32[]{:S(2)}) collective-permute-start(bf16[2,64,1024]{2,1,0:T(8,128)(2,1)S(1)} %get-tuple-element.447), channel_id=1, source_target_pairs={{0,2},{1,3},{2,0},{3,1},{4,6},{5,7},{6,4},{7,5},{8,10},{9,11},{10,... | collective-permute-start | bytes 786440 | tf_op jit(solution)/shard_map/cond/branch_22_fun/ppermute | solution.py:406
  16.8 2.1 %collective-permute-start.111 = (bf16[32,4096]{1,0:T(8,128)(2,1)S(1)}, bf16[32,4096]{1,0:T(8,128)(2,1)}, u32[]{:S(2)}, u32[]{:S(2)}) collective-permute-start(bf16[32,4096]{1,0:T(8,128)(2,1)S(1)} %get-tuple-element.448), channel_id=1, source_target_pairs={{0,3},{1,4},{8,11},{9,12},{16,19},{17,20},{24,27},{25,28}} | collective-permute-start | bytes 786440 | tf_op jit(solution)/shard_map/cond/branch_22_fun/ppermute | solution.py:406
  18.8 1.4 %collective-permute-start.112 = (bf16[32,4096]{1,0:T(8,128)(2,1)S(1)}, bf16[32,4096]{1,0:T(8,128)(2,1)}, u32[]{:S(2)}, u32[]{:S(2)}) collective-permute-start(bf16[32,4096]{1,0:T(8,128)(2,1)S(1)} %get-tuple-element.449), channel_id=1, source_target_pairs={{1,5},{9,13},{17,21},{25,29}} | collective-permute-start | bytes 786440 | tf_op jit(solution)/shard_map/cond/branch_22_fun/ppermute | solution.py:406
  20.2 1.4 %collective-permute-start.113 = (bf16[32,4096]{1,0:T(8,128)(2,1)S(1)}, bf16[32,4096]{1,0:T(8,128)(2,1)}, u32[]{:S(2)}, u32[]{:S(2)}) collective-permute-start(bf16[32,4096]{1,0:T(8,128)(2,1)S(1)} %get-tuple-element.450), channel_id=1, source_target_pairs={{1,6},{9,14},{17,22},{25,30}} | collective-permute-start | bytes 786440 | tf_op jit(solution)/shard_map/cond/branch_22_fun/ppermute | solution.py:406
  21.5 2.8 %collective-permute-start.109 = (bf16[2,32,1024]{2,1,0:T(8,128)(2,1)S(1)}, bf16[2,32,1024]{2,1,0:T(8,128)(2,1)S(1)}, u32[]{:S(2)}, u32[]{:S(2)}) collective-permute-start(bf16[2,32,1024]{2,1,0:T(8,128)(2,1)S(1)} %get-tuple-element.446), channel_id=1, source_target_pairs={{24,0},{16,8},{0,16},{8,24},{25,1},{17,9},{1,17},{9,25},{26,2},{18... | collective-permute-start | bytes 393224 | tf_op jit(solution)/shard_map/cond/branch_22_fun/ppermute | solution.py:417
  24.4 7.3 %collective-permute-done.109 = bf16[2,32,1024]{2,1,0:T(8,128)(2,1)S(1)} collective-permute-done((bf16[2,32,1024]{2,1,0:T(8,128)(2,1)S(1)}, bf16[2,32,1024]{2,1,0:T(8,128)(2,1)S(1)}, u32[]{:S(2)}, u32[]{:S(2)}) %collective-permute-start.109) | collective-permute-done | bytes 131104 | tf_op jit(solution)/shard_map/cond/branch_22_fun/ppermute | solution.py:417
  31.8 1.8 %shard_map.96.refs_0_ = bf16[2,96,1024]{2,1,0:T(8,128)(2,1)} custom-call(bf16[2,32,1024]{2,1,0:T(8,128)(2,1)S(1)} %get-tuple-element.559.refs_0_, bf16[2,64,1024]{2,1,0:T(8,128)(2,1)S(1)} %get-tuple-element.554.refs_1_, bf16[2,64,1024]{2,1,0:T(8,128)(2,1)} %get-tuple-element.560.refs_2_), custom_call_target="tpu_custom_call" | custom-call | flops 1 | bytes 1 | tf_op jit(solution)/shard_map/pallas_call | solution.py:475
  33.6 0.9 collective-permute-start.168
  34.4 1.5 %collective-permute-start.170 = (bf16[2,96,1024]{2,1,0:T(8,128)(2,1)}, bf16[2,96,1024]{2,1,0:T(8,128)(2,1)S(1)}, u32[]{:S(2)}, u32[]{:S(2)}) collective-permute-start(bf16[2,96,1024]{2,1,0:T(8,128)(2,1)} %shard_map.96.refs_0_), channel_id=1, source_target_pairs={{0,1},{1,0},{2,3},{3,2},{4,5},{5,4},{6,7},{7,6},{8,9},{9,8},{10,11... | collective-permute-start | bytes 1179656 | tf_op jit(solution)/shard_map/ppermute | solution.py:459
  36.0 4.4 %collective-permute-done.167.refs_1_ = bf16[2,32,1024]{2,1,0:T(8,128)(2,1)S(1)} collective-permute-done((bf16[2,32,1024]{2,1,0:T(8,128)(2,1)S(1)}, bf16[2,32,1024]{2,1,0:T(8,128)(2,1)S(1)}, u32[]{:S(2)}, u32[]{:S(2)}) %collective-permute-start.167) | collective-permute-done | bytes 131104 | tf_op jit(solution)/shard_map/ppermute | solution.py:459
  40.3 0.7 collective-permute-start.171
  41.0 0.6 collective-permute-start.169
  41.6 1.6 %collective-permute-start.166 = (bf16[2,64,1024]{2,1,0:T(8,128)(2,1)S(1)}, bf16[2,64,1024]{2,1,0:T(8,128)(2,1)S(1)}, u32[]{:S(2)}, u32[]{:S(2)}) collective-permute-start(bf16[2,64,1024]{2,1,0:T(8,128)(2,1)S(1)} %copy-done.9), channel_id=1, source_target_pairs={{0,1},{1,2},{2,3},{3,4},{4,5},{5,6},{6,7},{8,9},{9,10},{10,11},{11... | collective-permute-start | bytes 786440 | tf_op jit(solution)/shard_map/ppermute | solution.py:571
  43.3 0.6 copy-done.19
  43.9 0.4 collective-permute-done.168.refs_2_
  44.3 5.7 %collective-permute-start.172 = (bf16[2,96,1024]{2,1,0:T(8,128)(2,1)S(1)}, bf16[2,96,1024]{2,1,0:T(8,128)(2,1)S(1)}, u32[]{:S(2)}, u32[]{:S(2)}) collective-permute-start(bf16[2,96,1024]{2,1,0:T(8,128)(2,1)S(1)} %collective-permute-done.168.refs_2_), channel_id=1, source_target_pairs={{0,1},{1,0},{2,3},{3,2},{4,5},{5,4},{6,7},{7,6},{8,9},{9,8},{10,11... | collective-permute-start | bytes 1179656 | tf_op jit(solution)/shard_map/ppermute | solution.py:459
  50.0 1.9 %collective-permute-start.174 = (bf16[32,4096]{1,0:T(8,128)(2,1)S(1)}, bf16[32,4096]{1,0:T(8,128)(2,1)S(1)}, u32[]{:S(2)}, u32[]{:S(2)}) collective-permute-start(bf16[32,4096]{1,0:T(8,128)(2,1)S(1)} %copy-done.12), channel_id=1, source_target_pairs={{0,1},{1,2},{2,6},{8,9},{9,10},{10,14},{16,17},{17,18},{18,22},{24... | collective-permute-start | bytes 786440 | tf_op jit(solution)/shard_map/ppermute | solution.py:448
  51.9 1.3 collective-permute-start.175
  53.3 0.9 collective-permute-start.176
  54.2 0.7 collective-permute-start.173
  54.9 5.1 %collective-permute-done.175.refs_10_ = bf16[32,4096]{1,0:T(8,128)(2,1)S(1)} collective-permute-done((bf16[32,4096]{1,0:T(8,128)(2,1)S(1)}, bf16[32,4096]{1,0:T(8,128)(2,1)S(1)}, u32[]{:S(2)}, u32[]{:S(2)}) %collective-permute-start.175) | collective-permute-done | bytes 262176 | tf_op jit(solution)/shard_map/ppermute | solution.py:448
  60.1 0.6 copy-done.16
  60.7 0.1 copy-done.17
  60.9 0.1 copy-done.8
  61.0 16.1 %shard_map.97 = (bf16[128,4096]{1,0:T(8,128)(2,1)}, bf16[32,4096]{1,0:T(8,128)(2,1)}, bf16[2,128,1024]{2,1,0:T(8,128)(2,1)}, bf16[2,192,1024]{2,1,0:T(8,128)(2,1...) custom-call(s32[3]{0:T(128)} %get-tuple-element.548.number_ref, f32[256,128]{1,0:T(8,128)} %get-tuple-element.549.near_ref, ...), custom_call_target="tpu_custom_call" | custom-call | flops 3103784960 | bytes 12582912 | tf_op jit(solution)/shard_map/pallas_call | solution.py:339
  77.1 3.6 %collective-permute-start.177 = (bf16[2,192,1024]{2,1,0:T(8,128)(2,1)}, bf16[2,192,1024]{2,1,0:T(8,128)(2,1)S(1)}, u32[]{:S(2)}, u32[]{:S(2)}) collective-permute-start(bf16[2,192,1024]{2,1,0:T(8,128)(2,1)} %get-tuple-element.575.refs_1_), channel_id=1, source_target_pairs={{0,1},{1,0},{2,3},{3,2},{4,5},{5,4},{6,7},{7,6},{8,9},{9,8},{10,11... | collective-permute-start | bytes 2359304 | tf_op jit(solution)/shard_map/ppermute | solution.py:459
  80.7 2.1 %collective-permute-done.177.refs_2_ = bf16[2,192,1024]{2,1,0:T(8,128)(2,1)S(1)} collective-permute-done((bf16[2,192,1024]{2,1,0:T(8,128)(2,1)}, bf16[2,192,1024]{2,1,0:T(8,128)(2,1)S(1)}, u32[]{:S(2)}, u32[]{:S(2)}) %collective-permute-start.177) | collective-permute-done | bytes 786464 | tf_op jit(solution)/shard_map/ppermute | solution.py:459
  82.8 0.9 copy-done
  83.7 2.4 %shard_map.98 = (f32[2,32,1024]{2,1,0:T(8,128)}, bf16[2,32,1024]{2,1,0:T(8,128)(2,1)}, bf16[2,96,1024]{2,1,0:T(8,128)(2,1)}, bf16[2,32,1024]{2,1,0:T(8,128)(2,1)}, f32[2,64,1024]{2,1,0:T(8,128)}) custom-call(bf16[2,128,1024]{2,1,0:T(8,128)(2,1)} %get-tuple-element.574.refs_0_, bf16[2,192,1024]{2,1,0:T(8,128)(2,1)} %get-tuple-element.575.refs_1_, ...), custom_call_target="tpu_custom_call" | custom-call | flops 1 | bytes 1 | tf_op jit(solution)/shard_map/pallas_call | solution.py:475
  86.1 1.3 collective-permute-start.181
  87.4 4.3 %collective-permute-start.178 = (bf16[2,32,1024]{2,1,0:T(8,128)(2,1)}, bf16[2,32,1024]{2,1,0:T(8,128)(2,1)S(1)}, u32[]{:S(2)}, u32[]{:S(2)}) collective-permute-start(bf16[2,32,1024]{2,1,0:T(8,128)(2,1)} %get-tuple-element.578), channel_id=1, source_target_pairs={{0,2},{1,3},{2,0},{3,1},{4,6},{5,7},{6,4},{7,5},{8,10},{9,11},{10,... | collective-permute-start | bytes 393224 | tf_op jit(solution)/shard_map/ppermute | solution.py:459
  91.8 2.6 %collective-permute-start.180 = (bf16[2,32,1024]{2,1,0:T(8,128)(2,1)}, bf16[2,32,1024]{2,1,0:T(8,128)(2,1)S(1)}, u32[]{:S(2)}, u32[]{:S(2)}) collective-permute-start(bf16[2,32,1024]{2,1,0:T(8,128)(2,1)} %get-tuple-element.580), channel_id=1, source_target_pairs={{0,6},{1,7},{2,4},{3,5},{4,2},{5,3},{6,0},{7,1},{8,14},{9,15},{10,... | collective-permute-start | bytes 393224 | tf_op jit(solution)/shard_map/ppermute | solution.py:459
  94.4 5.9 %collective-permute-done.178.refs_2_ = bf16[2,32,1024]{2,1,0:T(8,128)(2,1)S(1)} collective-permute-done((bf16[2,32,1024]{2,1,0:T(8,128)(2,1)}, bf16[2,32,1024]{2,1,0:T(8,128)(2,1)S(1)}, u32[]{:S(2)}, u32[]{:S(2)}) %collective-permute-start.178) | collective-permute-done | bytes 131104 | tf_op jit(solution)/shard_map/ppermute | solution.py:459
  100.2 0.9 collective-permute-done.180.refs_4_
  101.2 0.6 copy-done.4
  101.8 0.1 copy-done.1
  101.9 1.4 %shard_map.99 = (bf16[2,32,1024]{2,1,0:T(8,128)(2,1)S(1)}, bf16[2,64,1024]{2,1,0:T(8,128)(2,1)S(1)}) custom-call(f32[2,32,1024]{2,1,0:T(8,128)} %get-tuple-element.576.refs_0_, f32[2,64,1024]{2,1,0:T(8,128)} %get-tuple-element.577.refs_1_, bf16[2,32,1024]{2,1,0:T(8,128)(2,1)} %copy-done.3, bf16[2,96,1024]{2,1,0:T(8,128)(2,1)} %copy-done.1, ...), custom_call_target="tpu_custom_call" | custom-call | flops 1 | bytes 1 | tf_op jit(solution)/shard_map/pallas_call | solution.py:475
  103.4 17.6 %conditional.3 = (bf16[2,32,1024]{2,1,0:T(8,128)(2,1)S(1)}, bf16[2,64,1024]{2,1,0:T(8,128)(2,1)}) conditional(s32[]{:T(128)} %bitcast.3, (bf16[2,64,1024]{2,1,0:T(8,128)(2,1)S(1)}, bf16[2,32,1024]{2,1,0:T(8,128)(2,1)S(1)}) %tuple.183, (bf16[2,32,1024]{2,1,0:T(8,128)(2,1)S(1)}, ...), branch_computations={%region_24.0_spmd, %region_25.0_spmd, %region_26.0_spmd, %region_2... | conditional | bytes 1835104 | solution.py:420
  103.5 4.1 %collective-permute-start.163 = (bf16[2,64,1024]{2,1,0:T(8,128)(2,1)S(1)}, bf16[2,64,1024]{2,1,0:T(8,128)(2,1)}, u32[]{:S(2)}, u32[]{:S(2)}) collective-permute-start(bf16[2,64,1024]{2,1,0:T(8,128)(2,1)S(1)} %get-tuple-element.501), channel_id=1, source_target_pairs={{0,2},{1,3},{2,0},{3,1},{4,6},{5,7},{6,4},{7,5},{8,10},{9,11},{10,... | collective-permute-start | bytes 786440 | tf_op jit(solution)/shard_map/cond/branch_22_fun/ppermute | solution.py:406
  107.6 8.6 %collective-permute-start.162 = (bf16[2,32,1024]{2,1,0:T(8,128)(2,1)S(1)}, bf16[2,32,1024]{2,1,0:T(8,128)(2,1)S(1)}, u32[]{:S(2)}, u32[]{:S(2)}) collective-permute-start(bf16[2,32,1024]{2,1,0:T(8,128)(2,1)S(1)} %get-tuple-element.500), channel_id=1, source_target_pairs={{0,24},{8,16},{16,0},{24,8},{1,25},{9,17},{17,1},{25,9},{2,26},{10... | collective-permute-start | bytes 393224 | tf_op jit(solution)/shard_map/cond/branch_22_fun/ppermute | solution.py:417
  116.1 4.9 %collective-permute-done.162 = bf16[2,32,1024]{2,1,0:T(8,128)(2,1)S(1)} collective-permute-done((bf16[2,32,1024]{2,1,0:T(8,128)(2,1)S(1)}, bf16[2,32,1024]{2,1,0:T(8,128)(2,1)S(1)}, u32[]{:S(2)}, u32[]{:S(2)}) %collective-permute-start.162) | collective-permute-done | bytes 131104 | tf_op jit(solution)/shard_map/cond/branch_22_fun/ppermute | solution.py:417
  121.1 0.7 copy-done.2
  121.8 3.0 %shard_map.100 = (bf16[1,32,6144]{2,1,0:T(8,128)(2,1)}, bf16[1,2,128,1024]{3,2,1,0:T(8,128)(2,1)}) custom-call(s32[3]{0:T(128)} %get-tuple-element.548.number_ref, s32[1]{0:T(128)S(6)} %copy.178.vis_ref, bf16[4,32,4096]{2,1,0:T(8,128)(2,1)} %bitcast.9, bf16[2,32,1024]{2,1,0:T(8,128)(2,1)S(1)} %get-tuple-element.583.dkv_ref, ...), custom_call_target="tpu_custom_call" | custom-call | tf_op jit(solution)/shard_map/pallas_call | solution.py:623
  (59 shorter events, 0.3 us)
Async XLA Ops:
  7.2 52.9 %all-gather.5.cloned.1.call-start = ((), (), s32[]{:S(2)}) async-start(), calls=%async_computation | async-start | bytes 1310720 | tf_op jit(solution)/shard_map/all_gather | solution.py:640
  9.9 111.2 %all-gather.7.cloned.1.call-start = ((), (), s32[]{:S(2)}) async-start(), calls=%async_computation.1 | async-start | bytes 1310720 | tf_op jit(solution)/shard_map/all_gather | solution.py:684
  13.0 0.6 copy-start.5
  13.8 17.9 %collective-permute-start.110 = (bf16[2,64,1024]{2,1,0:T(8,128)(2,1)S(1)}, bf16[2,64,1024]{2,1,0:T(8,128)(2,1)}, u32[]{:S(2)}, u32[]{:S(2)}) collective-permute-start(bf16[2,64,1024]{2,1,0:T(8,128)(2,1)S(1)} %get-tuple-element.447), channel_id=1, source_target_pairs={{0,2},{1,3},{2,0},{3,1},{4,6},{5,7},{6,4},{7,5},{8,10},{9,11},{10,... | collective-permute-start | bytes 786440 | tf_op jit(solution)/shard_map/cond/branch_22_fun/ppermute | solution.py:406
  16.8 14.9 %collective-permute-start.111 = (bf16[32,4096]{1,0:T(8,128)(2,1)S(1)}, bf16[32,4096]{1,0:T(8,128)(2,1)}, u32[]{:S(2)}, u32[]{:S(2)}) collective-permute-start(bf16[32,4096]{1,0:T(8,128)(2,1)S(1)} %get-tuple-element.448), channel_id=1, source_target_pairs={{0,3},{1,4},{8,11},{9,12},{16,19},{17,20},{24,27},{25,28}} | collective-permute-start | bytes 786440 | tf_op jit(solution)/shard_map/cond/branch_22_fun/ppermute | solution.py:406
  18.8 12.9 %collective-permute-start.112 = (bf16[32,4096]{1,0:T(8,128)(2,1)S(1)}, bf16[32,4096]{1,0:T(8,128)(2,1)}, u32[]{:S(2)}, u32[]{:S(2)}) collective-permute-start(bf16[32,4096]{1,0:T(8,128)(2,1)S(1)} %get-tuple-element.449), channel_id=1, source_target_pairs={{1,5},{9,13},{17,21},{25,29}} | collective-permute-start | bytes 786440 | tf_op jit(solution)/shard_map/cond/branch_22_fun/ppermute | solution.py:406
  20.2 11.5 %collective-permute-start.113 = (bf16[32,4096]{1,0:T(8,128)(2,1)S(1)}, bf16[32,4096]{1,0:T(8,128)(2,1)}, u32[]{:S(2)}, u32[]{:S(2)}) collective-permute-start(bf16[32,4096]{1,0:T(8,128)(2,1)S(1)} %get-tuple-element.450), channel_id=1, source_target_pairs={{1,6},{9,14},{17,22},{25,30}} | collective-permute-start | bytes 786440 | tf_op jit(solution)/shard_map/cond/branch_22_fun/ppermute | solution.py:406
  21.5 10.1 %collective-permute-start.109 = (bf16[2,32,1024]{2,1,0:T(8,128)(2,1)S(1)}, bf16[2,32,1024]{2,1,0:T(8,128)(2,1)S(1)}, u32[]{:S(2)}, u32[]{:S(2)}) collective-permute-start(bf16[2,32,1024]{2,1,0:T(8,128)(2,1)S(1)} %get-tuple-element.446), channel_id=1, source_target_pairs={{24,0},{16,8},{0,16},{8,24},{25,1},{17,9},{1,17},{9,25},{26,2},{18... | collective-permute-start | bytes 393224 | tf_op jit(solution)/shard_map/cond/branch_22_fun/ppermute | solution.py:417
  31.7 9.9 %copy-start.9 = (bf16[2,64,1024]{2,1,0:T(8,128)(2,1)S(1)}, bf16[2,64,1024]{2,1,0:T(8,128)(2,1)}, u32[]{:S(2)}) copy-start(bf16[2,64,1024]{2,1,0:T(8,128)(2,1)} %get-tuple-element.553) | copy-start | bytes 786436
  31.7 18.3 %copy-start.12 = (bf16[32,4096]{1,0:T(8,128)(2,1)S(1)}, bf16[32,4096]{1,0:T(8,128)(2,1)}, u32[]{:S(2)}) copy-start(bf16[32,4096]{1,0:T(8,128)(2,1)} %get-tuple-element.566) | copy-start | bytes 786436
  31.7 20.2 %copy-start.11 = (bf16[32,4096]{1,0:T(8,128)(2,1)S(1)}, bf16[32,4096]{1,0:T(8,128)(2,1)}, u32[]{:S(2)}) copy-start(bf16[32,4096]{1,0:T(8,128)(2,1)} %get-tuple-element.567) | copy-start | bytes 786436
  31.8 21.5 %copy-start.10 = (bf16[32,4096]{1,0:T(8,128)(2,1)S(1)}, bf16[32,4096]{1,0:T(8,128)(2,1)}, u32[]{:S(2)}) copy-start(bf16[32,4096]{1,0:T(8,128)(2,1)} %get-tuple-element.571) | copy-start | bytes 786436
  33.6 10.8 %collective-permute-start.168 = (bf16[2,96,1024]{2,1,0:T(8,128)(2,1)}, bf16[2,96,1024]{2,1,0:T(8,128)(2,1)S(1)}, u32[]{:S(2)}, u32[]{:S(2)}) collective-permute-start(bf16[2,96,1024]{2,1,0:T(8,128)(2,1)} %shard_map.96.refs_0_), channel_id=1, source_target_pairs={{0,4},{1,5},{2,6},{3,7},{4,0},{5,1},{6,2},{7,3},{8,12},{9,13},{10,... | collective-permute-start | bytes 1179656 | tf_op jit(solution)/shard_map/ppermute | solution.py:459
  34.4 5.9 %collective-permute-start.167 = (bf16[2,32,1024]{2,1,0:T(8,128)(2,1)S(1)}, bf16[2,32,1024]{2,1,0:T(8,128)(2,1)S(1)}, u32[]{:S(2)}, u32[]{:S(2)}) collective-permute-start(bf16[2,32,1024]{2,1,0:T(8,128)(2,1)S(1)} %get-tuple-element.559.refs_0_), channel_id=1, source_target_pairs={{0,2},{1,3},{2,0},{3,1},{4,6},{5,7},{6,4},{7,5},{8,10},{9,11},{10,... | collective-permute-start | bytes 393224 | tf_op jit(solution)/shard_map/ppermute | solution.py:459
  34.4 18.8 %collective-permute-start.170 = (bf16[2,96,1024]{2,1,0:T(8,128)(2,1)}, bf16[2,96,1024]{2,1,0:T(8,128)(2,1)S(1)}, u32[]{:S(2)}, u32[]{:S(2)}) collective-permute-start(bf16[2,96,1024]{2,1,0:T(8,128)(2,1)} %shard_map.96.refs_0_), channel_id=1, source_target_pairs={{0,1},{1,0},{2,3},{3,2},{4,5},{5,4},{6,7},{7,6},{8,9},{9,8},{10,11... | collective-permute-start | bytes 1179656 | tf_op jit(solution)/shard_map/ppermute | solution.py:459
  40.3 19.7 %copy-start.18 = (bf16[2,32,1024]{2,1,0:T(8,128)(2,1)}, bf16[2,32,1024]{2,1,0:T(8,128)(2,1)S(1)}, u32[]{:S(2)}) copy-start(bf16[2,32,1024]{2,1,0:T(8,128)(2,1)S(1)} %collective-permute-done.167.refs_1_) | copy-start | bytes 393220
  40.3 2.9 %collective-permute-start.171 = (bf16[2,32,1024]{2,1,0:T(8,128)(2,1)S(1)}, bf16[2,32,1024]{2,1,0:T(8,128)(2,1)S(1)}, u32[]{:S(2)}, u32[]{:S(2)}) collective-permute-start(bf16[2,32,1024]{2,1,0:T(8,128)(2,1)S(1)} %collective-permute-done.167.refs_1_), channel_id=1, source_target_pairs={{0,1},{1,0},{2,3},{3,2},{4,5},{5,4},{6,7},{7,6},{8,9},{9,8},{10,11... | collective-permute-start | bytes 393224 | tf_op jit(solution)/shard_map/ppermute | solution.py:459
  41.0 10.9 %collective-permute-start.169 = (bf16[2,32,1024]{2,1,0:T(8,128)(2,1)S(1)}, bf16[2,32,1024]{2,1,0:T(8,128)(2,1)S(1)}, u32[]{:S(2)}, u32[]{:S(2)}) collective-permute-start(bf16[2,32,1024]{2,1,0:T(8,128)(2,1)S(1)} %get-tuple-element.559.refs_0_), channel_id=1, source_target_pairs={{0,6},{1,7},{2,4},{3,5},{4,2},{5,3},{6,0},{7,1},{8,14},{9,15},{10,... | collective-permute-start | bytes 393224 | tf_op jit(solution)/shard_map/ppermute | solution.py:459
  41.6 12.5 %collective-permute-start.166 = (bf16[2,64,1024]{2,1,0:T(8,128)(2,1)S(1)}, bf16[2,64,1024]{2,1,0:T(8,128)(2,1)S(1)}, u32[]{:S(2)}, u32[]{:S(2)}) collective-permute-start(bf16[2,64,1024]{2,1,0:T(8,128)(2,1)S(1)} %copy-done.9), channel_id=1, source_target_pairs={{0,1},{1,2},{2,3},{3,4},{4,5},{5,6},{6,7},{8,9},{9,10},{10,11},{11... | collective-permute-start | bytes 786440 | tf_op jit(solution)/shard_map/ppermute | solution.py:571
  43.3 0.7 copy-start.19
  44.3 15.8 %copy-start.6 = (bf16[2,96,1024]{2,1,0:T(8,128)(2,1)}, bf16[2,96,1024]{2,1,0:T(8,128)(2,1)S(1)}, u32[]{:S(2)}) copy-start(bf16[2,96,1024]{2,1,0:T(8,128)(2,1)S(1)} %collective-permute-done.168.refs_2_) | copy-start | bytes 1179652
  44.3 15.7 %collective-permute-start.172 = (bf16[2,96,1024]{2,1,0:T(8,128)(2,1)S(1)}, bf16[2,96,1024]{2,1,0:T(8,128)(2,1)S(1)}, u32[]{:S(2)}, u32[]{:S(2)}) collective-permute-start(bf16[2,96,1024]{2,1,0:T(8,128)(2,1)S(1)} %collective-permute-done.168.refs_2_), channel_id=1, source_target_pairs={{0,1},{1,0},{2,3},{3,2},{4,5},{5,4},{6,7},{7,6},{8,9},{9,8},{10,11... | collective-permute-start | bytes 1179656 | tf_op jit(solution)/shard_map/ppermute | solution.py:459
  50.0 4.9 %collective-permute-start.174 = (bf16[32,4096]{1,0:T(8,128)(2,1)S(1)}, bf16[32,4096]{1,0:T(8,128)(2,1)S(1)}, u32[]{:S(2)}, u32[]{:S(2)}) collective-permute-start(bf16[32,4096]{1,0:T(8,128)(2,1)S(1)} %copy-done.12), channel_id=1, source_target_pairs={{0,1},{1,2},{2,6},{8,9},{9,10},{10,14},{16,17},{17,18},{18,22},{24... | collective-permute-start | bytes 786440 | tf_op jit(solution)/shard_map/ppermute | solution.py:448
  51.9 8.1 %copy-start.20 = (bf16[2,32,1024]{2,1,0:T(8,128)(2,1)}, bf16[2,32,1024]{2,1,0:T(8,128)(2,1)S(1)}, u32[]{:S(2)}) copy-start(bf16[2,32,1024]{2,1,0:T(8,128)(2,1)S(1)} %collective-permute-done.169.refs_3_) | copy-start | bytes 393220
  51.9 8.0 %collective-permute-start.175 = (bf16[32,4096]{1,0:T(8,128)(2,1)S(1)}, bf16[32,4096]{1,0:T(8,128)(2,1)S(1)}, u32[]{:S(2)}, u32[]{:S(2)}) collective-permute-start(bf16[32,4096]{1,0:T(8,128)(2,1)S(1)} %copy-done.11), channel_id=1, source_target_pairs={{0,2},{1,3},{2,7},{8,10},{9,11},{10,15},{16,18},{17,19},{18,23},{2... | collective-permute-start | bytes 786440 | tf_op jit(solution)/shard_map/ppermute | solution.py:448
  53.3 6.8 %copy-start.7 = (bf16[2,96,1024]{2,1,0:T(8,128)(2,1)}, bf16[2,96,1024]{2,1,0:T(8,128)(2,1)S(1)}, u32[]{:S(2)}) copy-start(bf16[2,96,1024]{2,1,0:T(8,128)(2,1)S(1)} %collective-permute-done.170.refs_4_) | copy-start | bytes 1179652
  53.3 6.7 %collective-permute-start.176 = (bf16[32,4096]{1,0:T(8,128)(2,1)S(1)}, bf16[32,4096]{1,0:T(8,128)(2,1)S(1)}, u32[]{:S(2)}, u32[]{:S(2)}) collective-permute-start(bf16[32,4096]{1,0:T(8,128)(2,1)S(1)} %copy-done.10), channel_id=1, source_target_pairs={{1,7},{9,15},{17,23},{25,31}} | collective-permute-start | bytes 786440 | tf_op jit(solution)/shard_map/ppermute | solution.py:448
  54.2 5.9 %copy-start.14 = (bf16[2,64,1024]{2,1,0:T(8,128)(2,1)}, bf16[2,64,1024]{2,1,0:T(8,128)(2,1)S(1)}, u32[]{:S(2)}) copy-start(bf16[2,64,1024]{2,1,0:T(8,128)(2,1)S(1)} %collective-permute-done.166.halo_ref) | copy-start | bytes 786436
  54.2 5.8 %collective-permute-start.173 = (bf16[2,32,1024]{2,1,0:T(8,128)(2,1)S(1)}, bf16[2,32,1024]{2,1,0:T(8,128)(2,1)S(1)}, u32[]{:S(2)}, u32[]{:S(2)}) collective-permute-start(bf16[2,32,1024]{2,1,0:T(8,128)(2,1)S(1)} %collective-permute-done.169.refs_3_), channel_id=1, source_target_pairs={{0,1},{1,0},{2,3},{3,2},{4,5},{5,4},{6,7},{7,6},{8,9},{9,8},{10,11... | collective-permute-start | bytes 393224 | tf_op jit(solution)/shard_map/ppermute | solution.py:459
  54.9 5.2 %copy-start.15 = (bf16[32,4096]{1,0:T(8,128)(2,1)}, bf16[32,4096]{1,0:T(8,128)(2,1)S(1)}, u32[]{:S(2)}) copy-start(bf16[32,4096]{1,0:T(8,128)(2,1)S(1)} %collective-permute-done.174.refs_9_) | copy-start | bytes 786436
  60.0 0.7 copy-start.16
  60.0 0.8 copy-start.17
  60.0 0.8 copy-start.21
  60.0 1.0 copy-start.8
  77.1 5.7 %collective-permute-start.177 = (bf16[2,192,1024]{2,1,0:T(8,128)(2,1)}, bf16[2,192,1024]{2,1,0:T(8,128)(2,1)S(1)}, u32[]{:S(2)}, u32[]{:S(2)}) collective-permute-start(bf16[2,192,1024]{2,1,0:T(8,128)(2,1)} %get-tuple-element.575.refs_1_), channel_id=1, source_target_pairs={{0,1},{1,0},{2,3},{3,2},{4,5},{5,4},{6,7},{7,6},{8,9},{9,8},{10,11... | collective-permute-start | bytes 2359304 | tf_op jit(solution)/shard_map/ppermute | solution.py:459
  82.8 0.9 copy-start
  83.7 2.5 %copy-start.13 = (bf16[2,64,1024]{2,1,0:T(8,128)(2,1)S(1)}, bf16[2,64,1024]{2,1,0:T(8,128)(2,1)}, u32[]{:S(2)}) copy-start(bf16[2,64,1024]{2,1,0:T(8,128)(2,1)} %get-tuple-element.586) | copy-start | bytes 786436
  86.1 15.0 %collective-permute-start.179 = (bf16[2,96,1024]{2,1,0:T(8,128)(2,1)}, bf16[2,96,1024]{2,1,0:T(8,128)(2,1)S(1)}, u32[]{:S(2)}, u32[]{:S(2)}) collective-permute-start(bf16[2,96,1024]{2,1,0:T(8,128)(2,1)} %get-tuple-element.579), channel_id=1, source_target_pairs={{0,4},{1,5},{2,6},{3,7},{4,0},{5,1},{6,2},{7,3},{8,12},{9,13},{10,... | collective-permute-start | bytes 1179656 | tf_op jit(solution)/shard_map/ppermute | solution.py:459
  86.1 34.9 %collective-permute-start.181 = (bf16[2,64,1024]{2,1,0:T(8,128)(2,1)S(1)}, bf16[2,64,1024]{2,1,0:T(8,128)(2,1)S(1)}, u32[]{:S(2)}, u32[]{:S(2)}) collective-permute-start(bf16[2,64,1024]{2,1,0:T(8,128)(2,1)S(1)} %copy-done.13), channel_id=1, source_target_pairs={{1,0},{2,1},{3,2},{4,3},{5,4},{6,5},{7,6},{9,8},{10,9},{11,10},{12... | collective-permute-start | bytes 786440 | tf_op jit(solution)/shard_map/ppermute | solution.py:692
  87.4 12.8 %collective-permute-start.178 = (bf16[2,32,1024]{2,1,0:T(8,128)(2,1)}, bf16[2,32,1024]{2,1,0:T(8,128)(2,1)S(1)}, u32[]{:S(2)}, u32[]{:S(2)}) collective-permute-start(bf16[2,32,1024]{2,1,0:T(8,128)(2,1)} %get-tuple-element.578), channel_id=1, source_target_pairs={{0,2},{1,3},{2,0},{3,1},{4,6},{5,7},{6,4},{7,5},{8,10},{9,11},{10,... | collective-permute-start | bytes 393224 | tf_op jit(solution)/shard_map/ppermute | solution.py:459
  91.8 9.4 %collective-permute-start.180 = (bf16[2,32,1024]{2,1,0:T(8,128)(2,1)}, bf16[2,32,1024]{2,1,0:T(8,128)(2,1)S(1)}, u32[]{:S(2)}, u32[]{:S(2)}) collective-permute-start(bf16[2,32,1024]{2,1,0:T(8,128)(2,1)} %get-tuple-element.580), channel_id=1, source_target_pairs={{0,6},{1,7},{2,4},{3,5},{4,2},{5,3},{6,0},{7,1},{8,14},{9,15},{10,... | collective-permute-start | bytes 393224 | tf_op jit(solution)/shard_map/ppermute | solution.py:459
  100.2 0.9 copy-start.3
  101.2 0.7 copy-start.4
  101.2 0.8 copy-start.1
  103.5 17.6 %collective-permute-start.163 = (bf16[2,64,1024]{2,1,0:T(8,128)(2,1)S(1)}, bf16[2,64,1024]{2,1,0:T(8,128)(2,1)}, u32[]{:S(2)}, u32[]{:S(2)}) collective-permute-start(bf16[2,64,1024]{2,1,0:T(8,128)(2,1)S(1)} %get-tuple-element.501), channel_id=1, source_target_pairs={{0,2},{1,3},{2,0},{3,1},{4,6},{5,7},{6,4},{7,5},{8,10},{9,11},{10,... | collective-permute-start | bytes 786440 | tf_op jit(solution)/shard_map/cond/branch_22_fun/ppermute | solution.py:406
  107.6 13.4 %collective-permute-start.162 = (bf16[2,32,1024]{2,1,0:T(8,128)(2,1)S(1)}, bf16[2,32,1024]{2,1,0:T(8,128)(2,1)S(1)}, u32[]{:S(2)}, u32[]{:S(2)}) collective-permute-start(bf16[2,32,1024]{2,1,0:T(8,128)(2,1)S(1)} %get-tuple-element.500), channel_id=1, source_target_pairs={{0,24},{8,16},{16,0},{24,8},{1,25},{9,17},{17,1},{25,9},{2,26},{10... | collective-permute-start | bytes 393224 | tf_op jit(solution)/shard_map/cond/branch_22_fun/ppermute | solution.py:417
  121.0 0.7 copy-start.2
Sparse Core Ops, SparseCore 0:
  10.1 36.8 all-gather.4
  77.2 39.5 all-gather.6

commit v3 on v2

--- a/solution.py
+++ b/solution.py
@@ -22,6 +22,7 @@
 KV_WIDTH = KV_HEADS * HEAD_DIM
 GROUP_WIDTH = RATIO * HEAD_DIM
 IMAGE_BLOCK = 32
+IMAGE_HALF = IMAGE_BLOCK // 2
 HIDDEN = -1e30
 SCORE_SCALE = 1.0 / math.sqrt(HEAD_DIM)
 
@@ -44,7 +45,7 @@
     )
 
 
-def first_kernel(halo, seq_ref, vis_ref, image_ref, kv_ref, number_ref, *out_refs):
+def send_first(halo, seq_ref, vis_ref, image_ref, kv_ref, number_ref, *out_refs):
     ikv_ref, iq_ref, text_ref, tail_ref = out_refs
     groups = seq_ref.shape[0]
     group = lax.axis_index("rollout")
@@ -78,25 +79,6 @@
         tail_ref[part] = kv_ref[0, part, tok_rows - halo :]
 
 
-def first_arrays(seq_image, vis_start, image_rows, keys_values, halo):
-    rows = image_rows.shape[1]
-    smem = pl.BlockSpec(memory_space=pltpu.SMEM)
-    vmem = pl.BlockSpec(memory_space=pltpu.VMEM)
-    tail = min(halo, keys_values.shape[2])
-    return pl.pallas_call(
-        functools.partial(first_kernel, tail),
-        in_specs=[smem, smem, vmem, vmem],
-        out_specs=[smem, vmem, vmem, vmem, vmem],
-        out_shape=[
-            jax.ShapeDtypeStruct((3,), jnp.int32),
-            jax.ShapeDtypeStruct((2, rows, KV_WIDTH), jnp.bfloat16),
-            jax.ShapeDtypeStruct((rows, Q_WIDTH), jnp.bfloat16),
-            jax.ShapeDtypeStruct((2, PROMPT, KV_WIDTH), jnp.bfloat16),
-            jax.ShapeDtypeStruct((2, tail, KV_WIDTH), jnp.bfloat16),
-        ],
-    )(seq_image, vis_start, image_rows, keys_values)
-
-
 def segments(positions, length_ref):
     end = jnp.int32(PREFIX)
     segment = jnp.where(positions < PREFIX, 0, 1)
@@ -110,28 +92,34 @@
     return jnp.where(visible, 0.0, HIDDEN)
 
 
-def second_kernel(
-    rounds, tok_rows, image_rows, halo, vis_ref, length_ref, d_ref, *out_refs
-):
-    *window_refs, near_ref, whole_ref, image_ref = out_refs
+def first_kernel(targets, halo, tail, seq_ref, vis_ref, length_ref, *refs):
+    image_in_ref, kv_ref, d_ref, *out_refs = refs
+    first_refs, window_refs, mask_refs = out_refs[:5], out_refs[5:-3], out_refs[-3:]
+    near_ref, whole_ref, image_ref = mask_refs
     here = lax.axis_index("ctx")
     ctx_size = lax.axis_size("ctx")
+    tok_rows = d_ref.shape[0]
+    image_rows = image_in_ref.shape[1]
     row = lax.broadcasted_iota(jnp.int32, (IMAGE_BLOCK, tok_rows), 0)
     column = lax.broadcasted_iota(jnp.int32, (IMAGE_BLOCK, tok_rows), 1)
     place = jnp.where(row < image_rows, row, 1 << 20)
     picks = []
-    for pairs in [[]] + rounds:
-        target = here
-        for source, other in pairs:
-            target = jnp.where(here == source, other, target)
-        begin = vis_ref[0] + image_rows * target - tok_rows * here
-        picks.append(jnp.where(column == place + begin, 1.0, 0.0).astype(jnp.bfloat16))
+    for blocks in targets:
+        for default, special in blocks:
+            target = here if default is None else default
+            for source, other in special:
+                target = jnp.where(here == source, other, target)
+            begin = vis_ref[0] + image_rows * target - tok_rows * here
+            picks.append(jnp.where(column == place + begin, 1.0, 0.0).astype(jnp.bfloat16))
     picked = dot_nn(jnp.concatenate(picks, axis=0), d_ref[...]).astype(jnp.bfloat16)
-    for at, window_ref in enumerate(window_refs):
-        window_ref[...] = picked[at * IMAGE_BLOCK : (at + 1) * IMAGE_BLOCK]
+    at = 0
+    for window_ref in window_refs:
+        window_ref[...] = picked[at : at + window_ref.shape[0]]
+        at += window_ref.shape[0]
 
     @pl.when(pl.program_id(0) == 0)
     def _():
+        send_first(tail, seq_ref, vis_ref, image_in_ref, kv_ref, *first_refs)
         vis = vis_ref[0]
         own_at = lax.broadcasted_iota(jnp.int32, (8, tok_rows), 1) + here * tok_rows
         own_segment = segments(own_at, length_ref)[:1]
@@ -160,35 +148,50 @@
         image_ref[VIS:] = hide(text_at <= image_row)
 
 
-def second_arrays(vis_start, lengths, cotangent, image_rows, halo):
+def first_arrays(seq_image, vis_start, lengths, image_rows, keys_values, cotangent, halo, targets):
+    rows = image_rows.shape[1]
     tok_rows, width = cotangent.shape
-    rounds = window_rounds(lax.axis_size("ctx"), tok_rows, image_rows)
-    count = len(rounds) + 1
+    tail = min(halo, tok_rows)
     block = 2048
     spec = pl.BlockSpec
     smem = spec(memory_space=pltpu.SMEM)
     lanes = RATIO * IMAGE_BLOCK
     near = PROMPT + halo + tok_rows
     whole = lambda *shape: spec(shape, lambda at: (0,) * len(shape))
-    out = pl.pallas_call(
-        functools.partial(second_kernel, rounds, tok_rows, image_rows, halo),
+    kept = [
+        ((2, rows, KV_WIDTH), jnp.bfloat16),
+        ((rows, Q_WIDTH), jnp.bfloat16),
+        ((2, PROMPT, KV_WIDTH), jnp.bfloat16),
+        ((2, tail, KV_WIDTH), jnp.bfloat16),
+    ]
+    masks = [
+        ((near, tok_rows), jnp.float32),
+        ((8, tok_rows), jnp.float32),
+        ((PREFIX, lanes), jnp.float32),
+    ]
+    counts = [len(blocks) * IMAGE_BLOCK for blocks in targets]
+    number, *out = pl.pallas_call(
+        functools.partial(first_kernel, targets, halo, tail),
         grid=(width // block,),
-        in_specs=[smem, smem, spec((tok_rows, block), lambda at: (0, at))],
-        out_specs=[spec((IMAGE_BLOCK, block), lambda at: (0, at)) for _ in range(count)]
-        + [whole(near, tok_rows), whole(8, tok_rows), whole(PREFIX, lanes)],
-        out_shape=[jax.ShapeDtypeStruct((IMAGE_BLOCK, width), jnp.bfloat16) for _ in range(count)]
-        + [
-            jax.ShapeDtypeStruct((near, tok_rows), jnp.float32),
-            jax.ShapeDtypeStruct((8, tok_rows), jnp.float32),
-            jax.ShapeDtypeStruct((PREFIX, lanes), jnp.float32),
+        in_specs=[
+            smem,
+            smem,
+            smem,
+            whole(*image_rows.shape),
+            whole(*keys_values.shape),
+            spec((tok_rows, block), lambda at: (0, at)),
         ],
-        cost_estimate=pl.CostEstimate(
-            flops=2 * count * IMAGE_BLOCK * tok_rows * width,
-            bytes_accessed=8 * 1024 * 1024,
-            transcendentals=0,
-        ),
-    )(vis_start, lengths, cotangent)
-    return out[:count], rounds, list(out[count:])
+        out_specs=[smem]
+        + [whole(*shape) for shape, _ in kept]
+        + [spec((count, block), lambda at: (0, at)) for count in counts]
+        + [whole(*shape) for shape, _ in masks],
+        out_shape=[jax.ShapeDtypeStruct((3,), jnp.int32)]
+        + [jax.ShapeDtypeStruct(*pair) for pair in kept]
+        + [jax.ShapeDtypeStruct((count, width), jnp.bfloat16) for count in counts]
+        + [jax.ShapeDtypeStruct(*pair) for pair in masks],
+        compiler_params=pltpu.CompilerParams(vmem_limit_bytes=40 * 1024 * 1024),
+    )(seq_image, vis_start, lengths, image_rows, keys_values, cotangent)
+    return number, out[:4], out[4 : 4 + len(targets)], out[4 + len(targets) :]
 
 
 def rows_backward(parts, q_rows, d_rows):
@@ -250,7 +253,7 @@
     block_refs, refs = refs[:block_count], refs[block_count:]
     text_refs, refs = refs[:text_count], refs[text_count:]
     window_refs, refs = refs[:window_count], refs[window_count:]
-    dq_ref, diq_ref, dmine_ref, dpair_ref, dhalo_ref, down_ref = refs
+    dq_ref, *diq_refs, dmine_ref, dpair_ref, dhalo_ref, down_ref = refs
     text_refs = text_refs or [ref for ref in block_refs if ref.shape[1] > block_rows]
     near_bias = jnp.concatenate([near_ref[...]] * 2, axis=1)
     whole_bias = jnp.concatenate([whole_ref[:1]] * 2, axis=1)
@@ -305,7 +308,9 @@
         d_scores = jnp.concatenate([part[1] for part in outcome], axis=0)
         dq = (dot_tn(keys[:PREFIX], d_scores) * SCORE_SCALE).T.astype(jnp.bfloat16)
         for at, span in enumerate(spans):
-            diq_ref[:, span] = dq[at * IMAGE_BLOCK : (at + 1) * IMAGE_BLOCK]
+            for half, diq_ref in enumerate(diq_refs):
+                begin = at * IMAGE_BLOCK + half * IMAGE_HALF
+                diq_ref[:, span] = dq[begin : begin + IMAGE_HALF]
         (visual_w, visual_d), (text_w, text_d) = outcome
         for part, sums, pieces, rows, scale in (
             (0, dk_sums, (visual_d, text_d), q_rows, SCORE_SCALE),
@@ -363,7 +368,8 @@
         + [q_spec(IMAGE_BLOCK) for _ in windows],
         out_specs=[
             q_spec(own),
-            q_spec(IMAGE_BLOCK),
+            q_spec(IMAGE_HALF),
+            q_spec(IMAGE_HALF),
             kv_spec(VIS // 2),
             kv_spec(VIS // 2 + PROMPT),
             kv_spec(halo),
@@ -371,7 +377,8 @@
         ],
         out_shape=[
             jax.ShapeDtypeStruct((own, Q_WIDTH), jnp.bfloat16),
-            jax.ShapeDtypeStruct((IMAGE_BLOCK, Q_WIDTH), jnp.bfloat16),
+            jax.ShapeDtypeStruct((IMAGE_HALF, Q_WIDTH), jnp.bfloat16),
+            jax.ShapeDtypeStruct((IMAGE_HALF, Q_WIDTH), jnp.bfloat16),
             jax.ShapeDtypeStruct((2, VIS // 2, KV_WIDTH), jnp.bfloat16),
             jax.ShapeDtypeStruct((2, VIS // 2 + PROMPT, KV_WIDTH), jnp.bfloat16),
             jax.ShapeDtypeStruct((2, halo, KV_WIDTH), jnp.bfloat16),
@@ -437,18 +444,26 @@
     return rounds
 
 
-def window_beside(ctx_size, rounds):
-    return [2, 3, 4] if ctx_size == 8 and len(rounds) == 6 else []
-
-
-def image_windows(windows, rounds, beside, moved):
-    moved = dict(zip(beside, moved))
-    parts = [windows[0]]
-    for at, (rows, pairs) in enumerate(zip(windows[1:], rounds)):
-        parts.append(moved[at] if at in moved else lax.ppermute(rows, "ctx", pairs))
-    if len(parts) > 8:
-        parts = [sum(part.astype(jnp.float32) for part in parts).astype(jnp.bfloat16)]
-    return parts
+def window_targets(ctx_size, tok_rows, image_rows):
+    rounds = window_rounds(ctx_size, tok_rows, image_rows)
+    if ctx_size != 8:
+        return [[(None, [])]] + [[(None, pairs)] for pairs in rounds], rounds
+    rounds = [[(0, 2), (1, 4), (2, 6)], [(0, 3), (1, 5), (2, 7)], [(1, 6)], [(1, 7)]]
+    swapped = [(2, [(0, 1)]), (3, [])]
+    return [[(None, [])]] + [[(None, pairs)] for pairs in rounds] + [swapped], rounds
+
+
+def join_first(image_kv, text, received, own, one, two, swapped):
+    here = lax.axis_index("ctx")
+    wide = lambda rows: rows.astype(jnp.float32)
+    near, far = swapped[:IMAGE_BLOCK], swapped[IMAGE_BLOCK:]
+    sums = [
+        jnp.where(here == 1, wide(own) + wide(near), wide(own)),
+        jnp.where(here == 0, wide(one) + wide(near), wide(one)),
+        jnp.where(here == 0, wide(two) + wide(far), wide(two)),
+    ]
+    kv = jnp.concatenate([image_kv, add_text(text, received)], axis=1)
+    return [kv] + [part.astype(jnp.bfloat16) for part in sums]
 
 
 def xor_pairs(step):
@@ -462,7 +477,6 @@
 def on_device(function, *arrays):
     if lax.axis_size("ctx") != 8:
         return function(*arrays)
-    block = KV_WIDTH // 2
     shapes = jax.eval_shape(function, *arrays)
 
     def kernel(*refs):
@@ -471,7 +485,10 @@
         ):
             out_ref[...] = value
 
-    spec = lambda array: pl.BlockSpec(array.shape[:2] + (block,), lambda at: (0, 0, at))
+    def spec(array):
+        *rows, width = array.shape
+        return pl.BlockSpec((*rows, width // 2), lambda at: (0,) * len(rows) + (at,))
+
     return pl.pallas_call(
         kernel,
         grid=(2,),
@@ -491,19 +508,14 @@
     return list(range(2, ctx_size, 2))
 
 
-def join_text(image_kv, text, received):
-    return [jnp.concatenate([image_kv, add_text(text, received)], axis=1)]
-
-
 def add_text(text, received):
     return (text.astype(jnp.float32) + received.astype(jnp.float32)).astype(jnp.bfloat16)
 
 
-def gather_prefix(image_kv, text, received, late_shard):
+def gather_prefix(image_kv, text):
     ctx_size = lax.axis_size("ctx")
     steps = chip_steps(ctx_size)
     if ctx_size == 8:
-        (text,) = on_device(join_text, image_kv, text, received)
         mine = [text, xor_permute(image_kv, 2), xor_permute(text, 4), xor_permute(image_kv, 6)]
         pair = [xor_permute(mine[0], 1)]
         for at, earlier in ((1, None), (3, 0), (2, 1)):
@@ -515,7 +527,7 @@
     mine = jnp.concatenate(
         [image_kv] + [xor_permute(image_kv, step) for step in steps], axis=1
     )
-    return [mine, xor_permute(mine, 1)], list(spread_text(add_text(text, received), late_shard))
+    return [mine, xor_permute(mine, 1)], None
 
 
 def split_sums(image_rows, steps, d_mine, d_pair, other):
@@ -584,13 +596,15 @@
     return parts
 
 
-def last_kernel(
-    number_ref, vis_ref, dq_ref, dkv_ref, down_ref, text_ref, other_ref, *refs
-):
-    *part_refs, image_ref, kv_ref = refs
+def last_kernel(part_count, vis_ref, dkv_ref, down_ref, text_ref, other_ref, *refs):
+    part_refs = refs[:part_count]
+    *dq_refs, image_ref, kv_ref = refs[part_count:]
     here = lax.axis_index("ctx")
     tok_rows = down_ref.shape[1]
-    image_ref[0, :, :Q_WIDTH] = dq_ref[0]
+    at = 0
+    for dq_ref in dq_refs:
+        image_ref[0, at : at + dq_ref.shape[0], :Q_WIDTH] = dq_ref[...]
+        at += dq_ref.shape[0]
     image_ref[0, :, Q_WIDTH : Q_WIDTH + KV_WIDTH] = dkv_ref[0]
     image_ref[0, :, Q_WIDTH + KV_WIDTH :] = dkv_ref[1]
     at = lax.broadcasted_iota(jnp.int32, (PROMPT, KV_WIDTH), 0)
@@ -612,28 +626,19 @@
         kv_ref[0, part] = sums.astype(jnp.bfloat16)
 
 
-def last_arrays(number, vis_start, every_dq, image_dkv, d_own_kv, text, other_text, parts):
+def last_arrays(vis_start, image_dq, image_dkv, d_own_kv, text, other_text, parts):
     rows = image_dkv.shape[1]
-    whole = lambda array: pl.BlockSpec(array.shape, lambda at, number: (0,) * len(array.shape))
-    kept = [image_dkv, d_own_kv, text, other_text, *parts]
-    shapes = [
-        jax.ShapeDtypeStruct((1, rows, Q_WIDTH + 2 * KV_WIDTH), jnp.bfloat16),
-        jax.ShapeDtypeStruct((1,) + d_own_kv.shape, jnp.bfloat16),
-    ]
+    smem = pl.BlockSpec(memory_space=pltpu.SMEM)
+    vmem = pl.BlockSpec(memory_space=pltpu.VMEM)
     return pl.pallas_call(
-        last_kernel,
-        grid_spec=pltpu.PrefetchScalarGridSpec(
-            num_scalar_prefetch=1,
-            grid=(1,),
-            in_specs=[
-                pl.BlockSpec(memory_space=pltpu.SMEM),
-                pl.BlockSpec((1, rows, Q_WIDTH), lambda at, number: (number[2], 0, 0)),
-            ]
-            + [whole(array) for array in kept],
-            out_specs=[whole(shape) for shape in shapes],
-        ),
-        out_shape=shapes,
-    )(number, vis_start, every_dq, *kept)
+        functools.partial(last_kernel, len(parts)),
+        in_specs=[smem] + [vmem] * (4 + len(parts) + len(image_dq)),
+        out_specs=[vmem, vmem],
+        out_shape=[
+            jax.ShapeDtypeStruct((1, rows, Q_WIDTH + 2 * KV_WIDTH), jnp.bfloat16),
+            jax.ShapeDtypeStruct((1,) + d_own_kv.shape, jnp.bfloat16),
+        ],
+    )(vis_start, image_dkv, d_own_kv, text, other_text, *parts, *image_dq)
 
 
 def gather_queries(image_q):
@@ -652,23 +657,35 @@
     halo = -(-(longest - 1) // 64) * 64
     q_own, d_own = queries[0], cotangent[0]
 
-    number, image_kv, image_q, text, tail = first_arrays(
-        seq_image, vis_start, image_rows, keys_values, halo
+    targets, rounds = window_targets(ctx_size, tok_rows, image_count)
+    number, (image_kv, image_q, text, tail), windows, masks = first_arrays(
+        seq_image, vis_start, comp_lengths, image_rows, keys_values, d_own, halo, targets
     )
     every_q = gather_queries(image_q)
-    windows, rounds, masks = second_arrays(vis_start, comp_lengths, d_own, image_count, halo)
-    beside = window_beside(ctx_size, rounds)
-    image_kv, received, *moved = route(
-        image_kv,
-        number,
-        False,
-        [(text, xor_pairs(late_shard))] + [(windows[at + 1], rounds[at]) for at in beside],
-    )
-    windows = image_windows(windows, rounds, beside, moved)
-    blocks, texts = gather_prefix(image_kv, text, received, late_shard)
+    beside = [(text, xor_pairs(late_shard))]
+    if ctx_size == 8:
+        own, one, two, three, four, swapped = windows
+        beside += [(swapped, xor_pairs(1)), (three, rounds[2]), (four, rounds[3])]
+    image_kv, received, *moved = route(image_kv, number, False, beside)
+    if ctx_size == 8:
+        text, own, one, two = on_device(
+            join_first, image_kv, text, received, own, one, two, moved[0]
+        )
+        windows = [own] + [
+            lax.ppermute(rows, "ctx", pairs) for rows, pairs in zip((one, two), rounds)
+        ]
+        windows += moved[1:]
+        blocks, texts = gather_prefix(image_kv, text)
+    else:
+        windows = [windows[0]] + [
+            lax.ppermute(rows, "ctx", pairs) for rows, pairs in zip(windows[1:], rounds)
+        ]
+        windows = [sum(part.astype(jnp.float32) for part in windows).astype(jnp.bfloat16)]
+        blocks, _ = gather_prefix(image_kv, text)
+        texts = list(spread_text(add_text(text, received), late_shard))
     halo_kv = halo_rows(tail, halo, tok_rows)
 
-    grad_q, d_image_q, d_mine, d_pair, d_halo, d_own_kv = attend(
+    grad_q, *d_image_q, d_mine, d_pair, d_halo, d_own_kv = attend(
         number,
         masks,
         q_own,
@@ -681,22 +698,31 @@
         windows,
     )
 
-    every_dq = lax.all_gather(d_image_q[:image_count], "rollout", axis=0)
+    d_image_q = [
+        half[: image_count - at * IMAGE_HALF]
+        for at, half in enumerate(d_image_q)
+        if at * IMAGE_HALF < image_count
+    ]
+    image_dq, other = route(d_image_q[0], number, True, [(d_pair, xor_pairs(1))])
+    image_dq = [image_dq]
     steps = chip_steps(ctx_size)
-    other = xor_permute(d_pair, 1)
     own, *sent, d_text = on_device(
         functools.partial(split_sums, image_count, steps), d_mine, d_pair, other
     )
-    moved = [xor_permute(rows, step) for rows, step in zip(sent, steps)]
-    halo_back = [
-        lax.ppermute(rows, "ctx", pairs) for rows, pairs in halo_parts(d_halo, tok_rows)
-    ]
+    beside = [(rows, xor_pairs(step)) for rows, step in zip(sent, steps)]
+    if len(d_image_q) > 1:
+        second, *moved = route(d_image_q[1], number, True, beside)
+        image_dq.append(second)
+    else:
+        moved = [lax.ppermute(rows, "ctx", pairs) for rows, pairs in beside]
     sums, d_text = on_device(functools.partial(add_sums, image_count), own, d_text, *moved)
     if ctx_size != 8:
         d_text = collect_text(d_text, late_shard)
-    image_dkv, other_text = route(sums, number, True, [(d_text, xor_pairs(late_shard))])
+    image_dkv, other_text, *halo_back = route(
+        sums, number, True, [(d_text, xor_pairs(late_shard))] + halo_parts(d_halo, tok_rows)
+    )
     grad_image, grad_kv = last_arrays(
-        number, vis_start, every_dq, image_dkv, d_own_kv, d_text, other_text, halo_back
+        vis_start, image_dq, image_dkv, d_own_kv, d_text, other_text, halo_back
     )
     return (grad_q[None], grad_kv, grad_image)
 

time: 129 us -> 125 us (0.969); the launches traced: 132 us -> 123 us
  starting transfers between devices: 50.9 us -> 39.8 us
  local copies, waits for them, and re-layouts: 4.58 us -> 9.43 us
  Pallas kernels: 29.8 us -> 26.8 us
    ppermute x11 -> x7, waiting for transfers between devices: 13.7 us -> 3.06 us  [xor_permute(): return lax.ppermute(rows, 'ctx', xor_pairs(step))]
    ppermute x2 -> x4, waiting for transfers between devices: 12.2 us -> 20.4 us  [branch(): lax.ppermute(rows, 'rollout', pairs)]
    ppermute x11 -> x7, starting transfers between devices: 20.6 us -> 13.4 us  [xor_permute(): return lax.ppermute(rows, 'ctx', xor_pairs(step))]
    ppermute x2 -> x4, starting transfers between devices: 11.4 us -> 4.47 us  [branch(): lax.ppermute(rows, 'rollout', pairs)]
    ppermute x5 -> x10, waiting for transfers between devices: 0.01 us -> 5.87 us  [move_beside(): lax.ppermute(array, 'ctx', pairs)]
    ppermute x3 -> x0, waiting for transfers between devices: 5.12 us -> none  [image_windows(): parts.append(moved[at] if at in moved else lax.ppermute(rows, 'ctx', pairs))]
    unnamed x44, local copies, waits for them, and re-layouts: 4.56 us -> 9.39 us
    ppermute x3 -> x0, starting transfers between devices: 4.07 us -> none  [image_windows(): parts.append(moved[at] if at in moved else lax.ppermute(rows, 'ctx', pairs))]
  transfers between devices with their start and end apart: 25 -> 25, of which waited for: 8 -> 10; matrix products, arithmetic and copies ran while one was open for 0% -> 0% of each run, Pallas kernels for 7% -> 2%
where the time goes in v3:
time: 125 us; the launch traced here: 123 us
  starting transfers between devices  39.8 us (32%)
  waiting for transfers between devices  31.9 us (26%)
  Pallas kernels  26.8 us (21%)
  between operations  14.9 us (12%)
  local copies, waits for them, and re-layouts  9.43 us (8%)
    ppermute x4, waiting for transfers between devices, branch(): lax.ppermute(rows, 'rollout', pairs)  20.4 us
    pallas_call x1, Pallas kernels, attend(): pl.pallas_call(functools.partial(attend_kernel, VIS // len(blocks), len(b...  16.1 us
    ppermute x10, starting transfers between devices, move_beside(): lax.ppermute(array, 'ctx', pairs)  14.6 us
    ppermute x7, starting transfers between devices, xor_permute(): return lax.ppermute(rows, 'ctx', xor_pairs(step))  13.4 us
    unnamed x44, local copies, waits for them, and re-layouts  9.39 us
    pallas_call x3, Pallas kernels, on_device(): pl.pallas_call(kernel, grid=(2,), in_specs=[spec(array) for array in arra...  5.95 us
    ppermute x10, waiting for transfers between devices, move_beside(): lax.ppermute(array, 'ctx', pairs)  5.87 us
    ppermute x4, starting transfers between devices, branch(): lax.ppermute(rows, 'rollout', pairs)  4.47 us
  transfers between devices with their start and end apart: 25, of which 10 were waited for; matrix products, arithmetic and copies ran while one was open for 0% of the time, Pallas kernels for 2%

profile of v3, /device:TPU:0, one launch (start us, length us, event | category | flops | bytes accessed | tf_op | source)
XLA Modules:
  0.0 123.3 jit_solution(10027587665320529716)
XLA Ops:
  8.5 1.2 copy-done
  9.8 1.0 copy-done.1
  10.8 1.0 copy-done.2
  11.8 2.5 %shard_map.94 = (s32[3]{0:T(128)S(1)}, bf16[2,32,1024]{2,1,0:T(8,128)(2,1)S(1)}, bf16[32,4096]{1,0:T(8,128)(2,1)}, bf16[2,64,1024]{2,1,0:T(8,128)(2,1)S(1)}, bf1...) custom-call(s32[4]{0:T(128)S(1)} %copy-done.7, ...), custom_call_target="tpu_custom_call" | custom-call | tf_op jit(solution)/shard_map/pallas_call | solution.py:173
  14.3 0.7 copy-done.3
  15.0 0.7 copy-done.4
  15.7 0.7 copy-done.5
  16.5 0.7 copy-done.9
  17.1 0.7 copy-done.10
  18.9 12.6 %conditional.4 = (bf16[2,32,1024]{2,1,0:T(8,128)(2,1)S(1)}, bf16[2,64,1024]{2,1,0:T(8,128)(2,1)}, bf16[64,4096]{1,0:T(8,128)(2,1)}, bf16[32,4096]{1,0:T(8,128)(2,1)}, bf16[32,4096]{1,0:T(8,128)(2,1)}) conditional(s32[]{:T(128)} %bitcast.3, (bf16[2,64,1024]{2,1,0:T(8,128)(2,1)S(1)}, bf16[64,4096]{1,0:T(8,128)(2,1)S(1)}, ...), branch_computations={%region_0.0_spmd, %region_1.0_spmd, %region_2.0_spmd, %region_3.0_... | conditional | bytes 6029552 | solution.py:427
  19.5 2.6 %collective-permute-start.50 = (bf16[2,64,1024]{2,1,0:T(8,128)(2,1)S(1)}, bf16[2,64,1024]{2,1,0:T(8,128)(2,1)}, u32[]{:S(2)}, u32[]{:S(2)}) collective-permute-start(bf16[2,64,1024]{2,1,0:T(8,128)(2,1)S(1)} %get-tuple-element.723), channel_id=1, source_target_pairs={{0,2},{1,3},{2,0},{3,1},{4,6},{5,7},{6,4},{7,5},{8,10},{9,11},{10,... | collective-permute-start | bytes 786440 | tf_op jit(solution)/shard_map/cond/branch_10_fun/ppermute | solution.py:413
  22.1 1.4 %collective-permute-start.52 = (bf16[32,4096]{1,0:T(8,128)(2,1)S(1)}, bf16[32,4096]{1,0:T(8,128)(2,1)}, u32[]{:S(2)}, u32[]{:S(2)}) collective-permute-start(bf16[32,4096]{1,0:T(8,128)(2,1)S(1)} %get-tuple-element.725), channel_id=1, source_target_pairs={{1,6},{9,14},{17,22},{25,30}} | collective-permute-start | bytes 786440 | tf_op jit(solution)/shard_map/cond/branch_10_fun/ppermute | solution.py:413
  23.5 1.4 %collective-permute-start.53 = (bf16[32,4096]{1,0:T(8,128)(2,1)S(1)}, bf16[32,4096]{1,0:T(8,128)(2,1)}, u32[]{:S(2)}, u32[]{:S(2)}) collective-permute-start(bf16[32,4096]{1,0:T(8,128)(2,1)S(1)} %get-tuple-element.726), channel_id=1, source_target_pairs={{1,7},{9,15},{17,23},{25,31}} | collective-permute-start | bytes 786440 | tf_op jit(solution)/shard_map/cond/branch_10_fun/ppermute | solution.py:413
  24.8 2.6 %collective-permute-start.49 = (bf16[2,32,1024]{2,1,0:T(8,128)(2,1)S(1)}, bf16[2,32,1024]{2,1,0:T(8,128)(2,1)S(1)}, u32[]{:S(2)}, u32[]{:S(2)}) collective-permute-start(bf16[2,32,1024]{2,1,0:T(8,128)(2,1)S(1)} %get-tuple-element.722), channel_id=1, source_target_pairs={{8,0},{24,8},{0,16},{16,24},{9,1},{25,9},{1,17},{17,25},{10,2},{26... | collective-permute-start | bytes 393224 | tf_op jit(solution)/shard_map/cond/branch_10_fun/ppermute | solution.py:424
  27.4 3.9 %collective-permute-done.49 = bf16[2,32,1024]{2,1,0:T(8,128)(2,1)S(1)} collective-permute-done((bf16[2,32,1024]{2,1,0:T(8,128)(2,1)S(1)}, bf16[2,32,1024]{2,1,0:T(8,128)(2,1)S(1)}, u32[]{:S(2)}, u32[]{:S(2)}) %collective-permute-start.49) | collective-permute-done | bytes 131104 | tf_op jit(solution)/shard_map/cond/branch_10_fun/ppermute | solution.py:424
  31.5 2.4 %shard_map.95 = (bf16[2,96,1024]{2,1,0:T(8,128)(2,1)}, bf16[32,4096]{1,0:T(8,128)(2,1)}, bf16[32,4096]{1,0:T(8,128)(2,1)}, bf16[32,4096]{1,0:T(8,128)(2,1)}) custom-call(bf16[2,32,1024]{2,1,0:T(8,128)(2,1)S(1)} %get-tuple-element.1074.refs_0_, bf16[2,64,1024]{2,1,0:T(8,128)(2,1)S(1)} %get-tuple-element.1069.refs_1_, ...), custom_call_target="tpu_custom_call" | custom-call | flops 1 | bytes 1 | tf_op jit(solution)/shard_map/pallas_call | solution.py:492
  33.9 2.5 %collective-permute-start.334 = (bf16[2,96,1024]{2,1,0:T(8,128)(2,1)}, bf16[2,96,1024]{2,1,0:T(8,128)(2,1)S(1)}, u32[]{:S(2)}, u32[]{:S(2)}) collective-permute-start(bf16[2,96,1024]{2,1,0:T(8,128)(2,1)} %get-tuple-element.1080.refs_0_), channel_id=1, source_target_pairs={{0,4},{1,5},{2,6},{3,7},{4,0},{5,1},{6,2},{7,3},{8,12},{9,13},{10,... | collective-permute-start | bytes 1179656 | tf_op jit(solution)/shard_map/ppermute | solution.py:474
  36.4 1.1 collective-permute-start.333
  37.5 2.4 %collective-permute-start.336 = (bf16[2,96,1024]{2,1,0:T(8,128)(2,1)}, bf16[2,96,1024]{2,1,0:T(8,128)(2,1)S(1)}, u32[]{:S(2)}, u32[]{:S(2)}) collective-permute-start(bf16[2,96,1024]{2,1,0:T(8,128)(2,1)} %get-tuple-element.1080.refs_0_), channel_id=1, source_target_pairs={{0,1},{1,0},{2,3},{3,2},{4,5},{5,4},{6,7},{7,6},{8,9},{9,8},{10,11... | collective-permute-start | bytes 1179656 | tf_op jit(solution)/shard_map/ppermute | solution.py:474
  39.9 1.9 %collective-permute-done.333.refs_1_ = bf16[2,32,1024]{2,1,0:T(8,128)(2,1)S(1)} collective-permute-done((bf16[2,32,1024]{2,1,0:T(8,128)(2,1)S(1)}, bf16[2,32,1024]{2,1,0:T(8,128)(2,1)S(1)}, u32[]{:S(2)}, u32[]{:S(2)}) %collective-permute-start.333) | collective-permute-done | bytes 131104 | tf_op jit(solution)/shard_map/ppermute | solution.py:474
  41.8 1.2 %collective-permute-start.337 = (bf16[2,32,1024]{2,1,0:T(8,128)(2,1)S(1)}, bf16[2,32,1024]{2,1,0:T(8,128)(2,1)S(1)}, u32[]{:S(2)}, u32[]{:S(2)}) collective-permute-start(bf16[2,32,1024]{2,1,0:T(8,128)(2,1)S(1)} %collective-permute-done.333.refs_1_), channel_id=1, source_target_pairs={{0,1},{1,0},{2,3},{3,2},{4,5},{5,4},{6,7},{7,6},{8,9},{9,8},{10,11... | collective-permute-start | bytes 393224 | tf_op jit(solution)/shard_map/ppermute | solution.py:474
  43.0 1.1 collective-permute-start.335
  44.2 1.1 collective-permute-done.334.refs_2_
  45.3 3.9 %collective-permute-start.338 = (bf16[2,96,1024]{2,1,0:T(8,128)(2,1)S(1)}, bf16[2,96,1024]{2,1,0:T(8,128)(2,1)S(1)}, u32[]{:S(2)}, u32[]{:S(2)}) collective-permute-start(bf16[2,96,1024]{2,1,0:T(8,128)(2,1)S(1)} %collective-permute-done.334.refs_2_), channel_id=1, source_target_pairs={{0,1},{1,0},{2,3},{3,2},{4,5},{5,4},{6,7},{7,6},{8,9},{9,8},{10,11... | collective-permute-start | bytes 1179656 | tf_op jit(solution)/shard_map/ppermute | solution.py:474
  49.2 3.0 %collective-permute-start.340 = (bf16[32,4096]{1,0:T(8,128)(2,1)}, bf16[32,4096]{1,0:T(8,128)(2,1)S(1)}, u32[]{:S(2)}, u32[]{:S(2)}) collective-permute-start(bf16[32,4096]{1,0:T(8,128)(2,1)} %get-tuple-element.1086), channel_id=1, source_target_pairs={{0,2},{1,4},{2,6},{8,10},{9,12},{10,14},{16,18},{17,20},{18,22},{2... | collective-permute-start | bytes 786440 | tf_op jit(solution)/shard_map/ppermute | solution.py:675
  52.2 1.3 %collective-permute-start.341 = (bf16[32,4096]{1,0:T(8,128)(2,1)}, bf16[32,4096]{1,0:T(8,128)(2,1)S(1)}, u32[]{:S(2)}, u32[]{:S(2)}) collective-permute-start(bf16[32,4096]{1,0:T(8,128)(2,1)} %get-tuple-element.1087), channel_id=1, source_target_pairs={{0,3},{1,5},{2,7},{8,11},{9,13},{10,15},{16,19},{17,21},{18,23},{2... | collective-permute-start | bytes 786440 | tf_op jit(solution)/shard_map/ppermute | solution.py:675
  53.5 3.0 %collective-permute-start.332 = (bf16[2,64,1024]{2,1,0:T(8,128)(2,1)S(1)}, bf16[2,64,1024]{2,1,0:T(8,128)(2,1)S(1)}, u32[]{:S(2)}, u32[]{:S(2)}) collective-permute-start(bf16[2,64,1024]{2,1,0:T(8,128)(2,1)S(1)} %get-tuple-element.1068), channel_id=1, source_target_pairs={{0,1},{1,2},{2,3},{3,4},{4,5},{5,6},{6,7},{8,9},{9,10},{10,11},{11... | collective-permute-start | bytes 786440 | tf_op jit(solution)/shard_map/ppermute | solution.py:583
  56.6 1.1 collective-permute-start.339
  57.7 2.5 %collective-permute-done.341.refs_10_ = bf16[32,4096]{1,0:T(8,128)(2,1)S(1)} collective-permute-done((bf16[32,4096]{1,0:T(8,128)(2,1)}, bf16[32,4096]{1,0:T(8,128)(2,1)S(1)}, u32[]{:S(2)}, u32[]{:S(2)}) %collective-permute-start.341) | collective-permute-done | bytes 262176 | tf_op jit(solution)/shard_map/ppermute | solution.py:675
  61.2 16.1 %shard_map.96 = (bf16[128,4096]{1,0:T(8,128)(2,1)}, bf16[16,4096]{1,0:T(8,128)(2,1)S(1)}, bf16[16,4096]{1,0:T(8,128)(2,1)S(1)}, bf16[2,128,1024]{2,1,0:T(8,128)(...) custom-call(s32[3]{0:T(128)} %copy-done.6, ...), custom_call_target="tpu_custom_call" | custom-call | flops 3103784960 | bytes 12582912 | tf_op jit(solution)/shard_map/pallas_call | solution.py:344
  77.3 9.6 %conditional.5 = (bf16[16,4096]{1,0:T(8,128)(2,1)S(1)}, bf16[2,192,1024]{2,1,0:T(8,128)(2,1)}) conditional(s32[]{:T(128)} %bitcast.3, (bf16[2,192,1024]{2,1,0:T(8,128)(2,1)S(1)}, bf16[16,4096]{1,0:T(8,128)(2,1)S(1)}) %tuple.398, (bf16[16,4096]{1,0:T(8,128)(2,1)S(1)}, bf16[2,192,1024]{2,1,0:T(8,128)(2,1)S(1)}) %tuple.399, ...), branch_computations={%region_24.0_spmd, %region_25.0_spmd, %region_26.0_spmd, %region_2... | conditional | bytes 3932256 | solution.py:427
  77.3 2.4 %collective-permute-start.139 = (bf16[2,192,1024]{2,1,0:T(8,128)(2,1)S(1)}, bf16[2,192,1024]{2,1,0:T(8,128)(2,1)}, u32[]{:S(2)}, u32[]{:S(2)}) collective-permute-start(bf16[2,192,1024]{2,1,0:T(8,128)(2,1)S(1)} %get-tuple-element.813), channel_id=1, source_target_pairs={{0,1},{1,0},{2,3},{3,2},{4,5},{5,4},{6,7},{7,6},{8,9},{9,8},{10,11... | collective-permute-start | bytes 2359304 | tf_op jit(solution)/shard_map/cond/branch_10_fun/ppermute | solution.py:413
  79.7 1.0 collective-permute-start.138
  80.7 6.1 %collective-permute-done.138 = bf16[16,4096]{1,0:T(8,128)(2,1)S(1)} collective-permute-done((bf16[16,4096]{1,0:T(8,128)(2,1)S(1)}, bf16[16,4096]{1,0:T(8,128)(2,1)S(1)}, u32[]{:S(2)}, u32[]{:S(2)}) %collective-permute-start.138) | collective-permute-done | bytes 131104 | tf_op jit(solution)/shard_map/cond/branch_10_fun/ppermute | solution.py:424
  86.9 2.1 %shard_map.97 = (f32[2,32,1024]{2,1,0:T(8,128)}, bf16[2,32,1024]{2,1,0:T(8,128)(2,1)S(1)}, bf16[2,96,1024]{2,1,0:T(8,128)(2,1)S(1)}, bf16[2,32,1024]{2,1,0:T(8,128)(2,1)S(1)}, f32[2,64,1024]{2,1,0:T(8,128)}) custom-call(bf16[2,128,1024]{2,1,0:T(8,128)(2,1)} %get-tuple-element.1091.refs_0_, bf16[2,192,1024]{2,1,0:T(8,128)(2,1)S(1)} %get-tuple-element.1092.refs_1_, ...), custom_call_target="tpu_custom_call" | custom-call | flops 1 | bytes 1 | tf_op jit(solution)/shard_map/pallas_call | solution.py:492
  89.0 13.8 %conditional.6 = (bf16[16,4096]{1,0:T(8,128)(2,1)S(1)}, bf16[2,32,1024]{2,1,0:T(8,128)(2,1)}, bf16[2,96,1024]{2,1,0:T(8,128)(2,1)}, bf16[2,32,1024]{2,1,0:T(8,128)(2,1)}) conditional(s32[]{:T(128)} %bitcast.3, (bf16[2,32,1024]{2,1,0:T(8,128)(2,1)S(1)}, bf16[2,96,1024]{2,1,0:T(8,128)(2,1)S(1)}, ...), branch_computations={%region_48.0_spmd, %region_49.0_spmd, %region_50.0_spmd, %region_5... | conditional | bytes 3408064 | solution.py:427
  89.0 2.1 %collective-permute-start.207 = (bf16[2,96,1024]{2,1,0:T(8,128)(2,1)S(1)}, bf16[2,96,1024]{2,1,0:T(8,128)(2,1)}, u32[]{:S(2)}, u32[]{:S(2)}) collective-permute-start(bf16[2,96,1024]{2,1,0:T(8,128)(2,1)S(1)} %get-tuple-element.882), channel_id=1, source_target_pairs={{0,4},{1,5},{2,6},{3,7},{4,0},{5,1},{6,2},{7,3},{8,12},{9,13},{10,... | collective-permute-start | bytes 1179656 | tf_op jit(solution)/shard_map/cond/branch_10_fun/ppermute | solution.py:413
  91.4 1.5 %collective-permute-start.208 = (bf16[2,32,1024]{2,1,0:T(8,128)(2,1)S(1)}, bf16[2,32,1024]{2,1,0:T(8,128)(2,1)}, u32[]{:S(2)}, u32[]{:S(2)}) collective-permute-start(bf16[2,32,1024]{2,1,0:T(8,128)(2,1)S(1)} %get-tuple-element.883), channel_id=1, source_target_pairs={{0,6},{1,7},{2,4},{3,5},{4,2},{5,3},{6,0},{7,1},{8,14},{9,15},{10,... | collective-permute-start | bytes 393224 | tf_op jit(solution)/shard_map/cond/branch_10_fun/ppermute | solution.py:413
  92.8 4.2 %collective-permute-done.205 = bf16[16,4096]{1,0:T(8,128)(2,1)S(1)} collective-permute-done((bf16[16,4096]{1,0:T(8,128)(2,1)S(1)}, bf16[16,4096]{1,0:T(8,128)(2,1)S(1)}, u32[]{:S(2)}, u32[]{:S(2)}) %collective-permute-start.205) | collective-permute-done | bytes 131104 | tf_op jit(solution)/shard_map/cond/branch_10_fun/ppermute | solution.py:424
  97.3 1.3 %collective-permute-done.208 = bf16[2,32,1024]{2,1,0:T(8,128)(2,1)} collective-permute-done((bf16[2,32,1024]{2,1,0:T(8,128)(2,1)S(1)}, bf16[2,32,1024]{2,1,0:T(8,128)(2,1)}, u32[]{:S(2)}, u32[]{:S(2)}) %collective-permute-start.208) | collective-permute-done | bytes 131104 | tf_op jit(solution)/shard_map/cond/branch_10_fun/ppermute | solution.py:413
  98.5 4.3 %collective-permute-done.207 = bf16[2,96,1024]{2,1,0:T(8,128)(2,1)} collective-permute-done((bf16[2,96,1024]{2,1,0:T(8,128)(2,1)S(1)}, bf16[2,96,1024]{2,1,0:T(8,128)(2,1)}, u32[]{:S(2)}, u32[]{:S(2)}) %collective-permute-start.207) | collective-permute-done | bytes 393248 | tf_op jit(solution)/shard_map/cond/branch_10_fun/ppermute | solution.py:413
  102.8 1.4 %shard_map.98 = (bf16[2,32,1024]{2,1,0:T(8,128)(2,1)S(1)}, bf16[2,64,1024]{2,1,0:T(8,128)(2,1)S(1)}) custom-call(f32[2,32,1024]{2,1,0:T(8,128)} %get-tuple-element.1095.refs_0_, f32[2,64,1024]{2,1,0:T(8,128)} %get-tuple-element.1096.refs_1_, bf16[2,32,1024]{2,1,0:T(8,128)(2,1)} %get-tuple-element.1101.refs_2_, ...), custom_call_target="tpu_custom_call" | custom-call | flops 1 | bytes 1 | tf_op jit(solution)/shard_map/pallas_call | solution.py:492
  104.3 9.9 %conditional.7 = (bf16[2,32,1024]{2,1,0:T(8,128)(2,1)S(1)}, bf16[2,64,1024]{2,1,0:T(8,128)(2,1)}, bf16[2,64,1024]{2,1,0:T(8,128)(2,1)}) conditional(s32[]{:T(128)} %bitcast.3, (bf16[2,64,1024]{2,1,0:T(8,128)(2,1)S(1)}, bf16[2,64,1024]{2,1,0:T(8,128)(2,1)S(1)}, bf16[2,32,1024]{2,1,0:T(8,128)(2,1)S(1)}) %tuple.402, ...), branch_computations={%region_72.0_spmd, %region_73.0_spmd, %region_74.0_spmd, %region_7... | conditional | bytes 2883728 | solution.py:427
  104.3 1.3 %collective-permute-start.291 = (bf16[2,64,1024]{2,1,0:T(8,128)(2,1)S(1)}, bf16[2,64,1024]{2,1,0:T(8,128)(2,1)}, u32[]{:S(2)}, u32[]{:S(2)}) collective-permute-start(bf16[2,64,1024]{2,1,0:T(8,128)(2,1)S(1)} %get-tuple-element.967), channel_id=1, source_target_pairs={{0,2},{1,3},{2,0},{3,1},{4,6},{5,7},{6,4},{7,5},{8,10},{9,11},{10,... | collective-permute-start | bytes 786440 | tf_op jit(solution)/shard_map/cond/branch_10_fun/ppermute | solution.py:413
  105.6 1.3 %collective-permute-start.292 = (bf16[2,64,1024]{2,1,0:T(8,128)(2,1)S(1)}, bf16[2,64,1024]{2,1,0:T(8,128)(2,1)}, u32[]{:S(2)}, u32[]{:S(2)}) collective-permute-start(bf16[2,64,1024]{2,1,0:T(8,128)(2,1)S(1)} %get-tuple-element.968), channel_id=1, source_target_pairs={{1,0},{2,1},{3,2},{4,3},{5,4},{6,5},{7,6},{9,8},{10,9},{11,10},{12... | collective-permute-start | bytes 786440 | tf_op jit(solution)/shard_map/cond/branch_10_fun/ppermute | solution.py:413
  106.9 0.9 collective-permute-start.290
  107.8 6.3 %collective-permute-done.290 = bf16[2,32,1024]{2,1,0:T(8,128)(2,1)S(1)} collective-permute-done((bf16[2,32,1024]{2,1,0:T(8,128)(2,1)S(1)}, bf16[2,32,1024]{2,1,0:T(8,128)(2,1)S(1)}, u32[]{:S(2)}, u32[]{:S(2)}) %collective-permute-start.290) | collective-permute-done | bytes 131104 | tf_op jit(solution)/shard_map/cond/branch_10_fun/ppermute | solution.py:424
  114.1 2.3 %shard_map.99 = (bf16[1,32,6144]{2,1,0:T(8,128)(2,1)}, bf16[1,2,128,1024]{3,2,1,0:T(8,128)(2,1)}) custom-call(s32[1]{0:T(128)S(6)} %copy.346.vis_ref, bf16[2,32,1024]{2,1,0:T(8,128)(2,1)S(1)} %get-tuple-element.1107.dkv_ref, f32[2,128,1024]{2,1,0:T(8,128)} %get-tuple-element.1108.down_ref, bf16[2,64,1024]{2,1,0:T(8,128)(2,1)S(1)} %get-tuple-element.1104.text_ref, ...), custom_call_target="tpu_custom_call" | custom-call | tf_op jit(solution)/shard_map/pallas_call | solution.py:633
  (61 shorter events, 3.9 us)
Async XLA Ops:
  7.2 53.1 %all-gather.3.cloned.1.call-start = ((), (), s32[]{:S(2)}) async-start(), calls=%async_computation | async-start | bytes 1310720 | tf_op jit(solution)/shard_map/all_gather | solution.py:645
  7.9 0.7 copy-start.7
  7.9 0.7 copy-start.8
  8.5 1.2 copy-start
  9.8 1.0 copy-start.1
  10.8 1.0 copy-start.2
  14.3 0.7 copy-start.3
  15.0 0.7 copy-start.4
  15.7 0.7 copy-start.5
  16.5 0.7 copy-start.9
  17.1 0.7 copy-start.10
  17.8 0.6 copy-start.11
  18.4 0.5 copy-start.6
  19.0 12.3 %collective-permute-start.51 = (bf16[64,4096]{1,0:T(8,128)(2,1)S(1)}, bf16[64,4096]{1,0:T(8,128)(2,1)}, u32[]{:S(2)}, u32[]{:S(2)}) collective-permute-start(bf16[64,4096]{1,0:T(8,128)(2,1)S(1)} %get-tuple-element.724), channel_id=1, source_target_pairs={{0,1},{1,0},{2,3},{3,2},{4,5},{5,4},{6,7},{7,6},{8,9},{9,8},{10,11... | collective-permute-start | bytes 1572872 | tf_op jit(solution)/shard_map/cond/branch_10_fun/ppermute | solution.py:413
  19.5 11.8 %collective-permute-start.50 = (bf16[2,64,1024]{2,1,0:T(8,128)(2,1)S(1)}, bf16[2,64,1024]{2,1,0:T(8,128)(2,1)}, u32[]{:S(2)}, u32[]{:S(2)}) collective-permute-start(bf16[2,64,1024]{2,1,0:T(8,128)(2,1)S(1)} %get-tuple-element.723), channel_id=1, source_target_pairs={{0,2},{1,3},{2,0},{3,1},{4,6},{5,7},{6,4},{7,5},{8,10},{9,11},{10,... | collective-permute-start | bytes 786440 | tf_op jit(solution)/shard_map/cond/branch_10_fun/ppermute | solution.py:413
  22.1 9.2 %collective-permute-start.52 = (bf16[32,4096]{1,0:T(8,128)(2,1)S(1)}, bf16[32,4096]{1,0:T(8,128)(2,1)}, u32[]{:S(2)}, u32[]{:S(2)}) collective-permute-start(bf16[32,4096]{1,0:T(8,128)(2,1)S(1)} %get-tuple-element.725), channel_id=1, source_target_pairs={{1,6},{9,14},{17,22},{25,30}} | collective-permute-start | bytes 786440 | tf_op jit(solution)/shard_map/cond/branch_10_fun/ppermute | solution.py:413
  23.5 7.8 %collective-permute-start.53 = (bf16[32,4096]{1,0:T(8,128)(2,1)S(1)}, bf16[32,4096]{1,0:T(8,128)(2,1)}, u32[]{:S(2)}, u32[]{:S(2)}) collective-permute-start(bf16[32,4096]{1,0:T(8,128)(2,1)S(1)} %get-tuple-element.726), channel_id=1, source_target_pairs={{1,7},{9,15},{17,23},{25,31}} | collective-permute-start | bytes 786440 | tf_op jit(solution)/shard_map/cond/branch_10_fun/ppermute | solution.py:413
  24.8 6.5 %collective-permute-start.49 = (bf16[2,32,1024]{2,1,0:T(8,128)(2,1)S(1)}, bf16[2,32,1024]{2,1,0:T(8,128)(2,1)S(1)}, u32[]{:S(2)}, u32[]{:S(2)}) collective-permute-start(bf16[2,32,1024]{2,1,0:T(8,128)(2,1)S(1)} %get-tuple-element.722), channel_id=1, source_target_pairs={{8,0},{24,8},{0,16},{16,24},{9,1},{25,9},{1,17},{17,25},{10,2},{26... | collective-permute-start | bytes 393224 | tf_op jit(solution)/shard_map/cond/branch_10_fun/ppermute | solution.py:424
  33.9 11.4 %collective-permute-start.334 = (bf16[2,96,1024]{2,1,0:T(8,128)(2,1)}, bf16[2,96,1024]{2,1,0:T(8,128)(2,1)S(1)}, u32[]{:S(2)}, u32[]{:S(2)}) collective-permute-start(bf16[2,96,1024]{2,1,0:T(8,128)(2,1)} %get-tuple-element.1080.refs_0_), channel_id=1, source_target_pairs={{0,4},{1,5},{2,6},{3,7},{4,0},{5,1},{6,2},{7,3},{8,12},{9,13},{10,... | collective-permute-start | bytes 1179656 | tf_op jit(solution)/shard_map/ppermute | solution.py:474
  36.4 5.4 %collective-permute-start.333 = (bf16[2,32,1024]{2,1,0:T(8,128)(2,1)S(1)}, bf16[2,32,1024]{2,1,0:T(8,128)(2,1)S(1)}, u32[]{:S(2)}, u32[]{:S(2)}) collective-permute-start(bf16[2,32,1024]{2,1,0:T(8,128)(2,1)S(1)} %get-tuple-element.1074.refs_0_), channel_id=1, source_target_pairs={{0,2},{1,3},{2,0},{3,1},{4,6},{5,7},{6,4},{7,5},{8,10},{9,11},{10,... | collective-permute-start | bytes 393224 | tf_op jit(solution)/shard_map/ppermute | solution.py:474
  37.5 19.0 %collective-permute-start.336 = (bf16[2,96,1024]{2,1,0:T(8,128)(2,1)}, bf16[2,96,1024]{2,1,0:T(8,128)(2,1)S(1)}, u32[]{:S(2)}, u32[]{:S(2)}) collective-permute-start(bf16[2,96,1024]{2,1,0:T(8,128)(2,1)} %get-tuple-element.1080.refs_0_), channel_id=1, source_target_pairs={{0,1},{1,0},{2,3},{3,2},{4,5},{5,4},{6,7},{7,6},{8,9},{9,8},{10,11... | collective-permute-start | bytes 1179656 | tf_op jit(solution)/shard_map/ppermute | solution.py:474
  41.8 19.1 %copy-start.18 = (bf16[2,32,1024]{2,1,0:T(8,128)(2,1)}, bf16[2,32,1024]{2,1,0:T(8,128)(2,1)S(1)}, u32[]{:S(2)}) copy-start(bf16[2,32,1024]{2,1,0:T(8,128)(2,1)S(1)} %collective-permute-done.333.refs_1_) | copy-start | bytes 393220
  41.8 2.4 %collective-permute-start.337 = (bf16[2,32,1024]{2,1,0:T(8,128)(2,1)S(1)}, bf16[2,32,1024]{2,1,0:T(8,128)(2,1)S(1)}, u32[]{:S(2)}, u32[]{:S(2)}) collective-permute-start(bf16[2,32,1024]{2,1,0:T(8,128)(2,1)S(1)} %collective-permute-done.333.refs_1_), channel_id=1, source_target_pairs={{0,1},{1,0},{2,3},{3,2},{4,5},{5,4},{6,7},{7,6},{8,9},{9,8},{10,11... | collective-permute-start | bytes 393224 | tf_op jit(solution)/shard_map/ppermute | solution.py:474
  43.0 10.5 %collective-permute-start.335 = (bf16[2,32,1024]{2,1,0:T(8,128)(2,1)S(1)}, bf16[2,32,1024]{2,1,0:T(8,128)(2,1)S(1)}, u32[]{:S(2)}, u32[]{:S(2)}) collective-permute-start(bf16[2,32,1024]{2,1,0:T(8,128)(2,1)S(1)} %get-tuple-element.1074.refs_0_), channel_id=1, source_target_pairs={{0,6},{1,7},{2,4},{3,5},{4,2},{5,3},{6,0},{7,1},{8,14},{9,15},{10,... | collective-permute-start | bytes 393224 | tf_op jit(solution)/shard_map/ppermute | solution.py:474
  44.2 16.7 %copy-start.19 = (bf16[2,32,1024]{2,1,0:T(8,128)(2,1)}, bf16[2,32,1024]{2,1,0:T(8,128)(2,1)S(1)}, u32[]{:S(2)}) copy-start(bf16[2,32,1024]{2,1,0:T(8,128)(2,1)S(1)} %collective-permute-done.337.refs_5_) | copy-start | bytes 393220
  45.3 15.6 %copy-start.12 = (bf16[2,96,1024]{2,1,0:T(8,128)(2,1)}, bf16[2,96,1024]{2,1,0:T(8,128)(2,1)S(1)}, u32[]{:S(2)}) copy-start(bf16[2,96,1024]{2,1,0:T(8,128)(2,1)S(1)} %collective-permute-done.334.refs_2_) | copy-start | bytes 1179652
  45.3 14.9 %collective-permute-start.338 = (bf16[2,96,1024]{2,1,0:T(8,128)(2,1)S(1)}, bf16[2,96,1024]{2,1,0:T(8,128)(2,1)S(1)}, u32[]{:S(2)}, u32[]{:S(2)}) collective-permute-start(bf16[2,96,1024]{2,1,0:T(8,128)(2,1)S(1)} %collective-permute-done.334.refs_2_), channel_id=1, source_target_pairs={{0,1},{1,0},{2,3},{3,2},{4,5},{5,4},{6,7},{7,6},{8,9},{9,8},{10,11... | collective-permute-start | bytes 1179656 | tf_op jit(solution)/shard_map/ppermute | solution.py:474
  49.2 8.5 %collective-permute-start.340 = (bf16[32,4096]{1,0:T(8,128)(2,1)}, bf16[32,4096]{1,0:T(8,128)(2,1)S(1)}, u32[]{:S(2)}, u32[]{:S(2)}) collective-permute-start(bf16[32,4096]{1,0:T(8,128)(2,1)} %get-tuple-element.1086), channel_id=1, source_target_pairs={{0,2},{1,4},{2,6},{8,10},{9,12},{10,14},{16,18},{17,20},{18,22},{2... | collective-permute-start | bytes 786440 | tf_op jit(solution)/shard_map/ppermute | solution.py:675
  52.2 8.0 %collective-permute-start.341 = (bf16[32,4096]{1,0:T(8,128)(2,1)}, bf16[32,4096]{1,0:T(8,128)(2,1)S(1)}, u32[]{:S(2)}, u32[]{:S(2)}) collective-permute-start(bf16[32,4096]{1,0:T(8,128)(2,1)} %get-tuple-element.1087), channel_id=1, source_target_pairs={{0,3},{1,5},{2,7},{8,11},{9,13},{10,15},{16,19},{17,21},{18,23},{2... | collective-permute-start | bytes 786440 | tf_op jit(solution)/shard_map/ppermute | solution.py:675
  53.5 6.7 %copy-start.20 = (bf16[2,32,1024]{2,1,0:T(8,128)(2,1)}, bf16[2,32,1024]{2,1,0:T(8,128)(2,1)S(1)}, u32[]{:S(2)}) copy-start(bf16[2,32,1024]{2,1,0:T(8,128)(2,1)S(1)} %collective-permute-done.335.refs_3_) | copy-start | bytes 393220
  53.5 6.7 %collective-permute-start.332 = (bf16[2,64,1024]{2,1,0:T(8,128)(2,1)S(1)}, bf16[2,64,1024]{2,1,0:T(8,128)(2,1)S(1)}, u32[]{:S(2)}, u32[]{:S(2)}) collective-permute-start(bf16[2,64,1024]{2,1,0:T(8,128)(2,1)S(1)} %get-tuple-element.1068), channel_id=1, source_target_pairs={{0,1},{1,2},{2,3},{3,4},{4,5},{5,6},{6,7},{8,9},{9,10},{10,11},{11... | collective-permute-start | bytes 786440 | tf_op jit(solution)/shard_map/ppermute | solution.py:583
  56.6 4.3 %copy-start.13 = (bf16[2,96,1024]{2,1,0:T(8,128)(2,1)}, bf16[2,96,1024]{2,1,0:T(8,128)(2,1)S(1)}, u32[]{:S(2)}) copy-start(bf16[2,96,1024]{2,1,0:T(8,128)(2,1)S(1)} %collective-permute-done.336.refs_4_) | copy-start | bytes 1179652
  56.6 3.6 %collective-permute-start.339 = (bf16[2,32,1024]{2,1,0:T(8,128)(2,1)S(1)}, bf16[2,32,1024]{2,1,0:T(8,128)(2,1)S(1)}, u32[]{:S(2)}, u32[]{:S(2)}) collective-permute-start(bf16[2,32,1024]{2,1,0:T(8,128)(2,1)S(1)} %collective-permute-done.335.refs_3_), channel_id=1, source_target_pairs={{0,1},{1,0},{2,3},{3,2},{4,5},{5,4},{6,7},{7,6},{8,9},{9,8},{10,11... | collective-permute-start | bytes 393224 | tf_op jit(solution)/shard_map/ppermute | solution.py:474
  57.7 3.2 %copy-start.15 = (bf16[32,4096]{1,0:T(8,128)(2,1)}, bf16[32,4096]{1,0:T(8,128)(2,1)S(1)}, u32[]{:S(2)}) copy-start(bf16[32,4096]{1,0:T(8,128)(2,1)S(1)} %collective-permute-done.340.refs_9_) | copy-start | bytes 786436
  60.2 0.8 copy-start.16
  60.2 0.8 copy-start.17
  60.2 0.7 copy-start.21
  60.2 1.0 copy-start.14
  77.3 9.5 %collective-permute-start.139 = (bf16[2,192,1024]{2,1,0:T(8,128)(2,1)S(1)}, bf16[2,192,1024]{2,1,0:T(8,128)(2,1)}, u32[]{:S(2)}, u32[]{:S(2)}) collective-permute-start(bf16[2,192,1024]{2,1,0:T(8,128)(2,1)S(1)} %get-tuple-element.813), channel_id=1, source_target_pairs={{0,1},{1,0},{2,3},{3,2},{4,5},{5,4},{6,7},{7,6},{8,9},{9,8},{10,11... | collective-permute-start | bytes 2359304 | tf_op jit(solution)/shard_map/cond/branch_10_fun/ppermute | solution.py:413
  79.7 7.1 %collective-permute-start.138 = (bf16[16,4096]{1,0:T(8,128)(2,1)S(1)}, bf16[16,4096]{1,0:T(8,128)(2,1)S(1)}, u32[]{:S(2)}, u32[]{:S(2)}) collective-permute-start(bf16[16,4096]{1,0:T(8,128)(2,1)S(1)} %get-tuple-element.812), channel_id=1, source_target_pairs={{0,8},{8,24},{16,0},{24,16},{1,9},{9,25},{17,1},{25,17},{2,10},{10... | collective-permute-start | bytes 393224 | tf_op jit(solution)/shard_map/cond/branch_10_fun/ppermute | solution.py:424
  89.0 13.8 %collective-permute-start.207 = (bf16[2,96,1024]{2,1,0:T(8,128)(2,1)S(1)}, bf16[2,96,1024]{2,1,0:T(8,128)(2,1)}, u32[]{:S(2)}, u32[]{:S(2)}) collective-permute-start(bf16[2,96,1024]{2,1,0:T(8,128)(2,1)S(1)} %get-tuple-element.882), channel_id=1, source_target_pairs={{0,4},{1,5},{2,6},{3,7},{4,0},{5,1},{6,2},{7,3},{8,12},{9,13},{10,... | collective-permute-start | bytes 1179656 | tf_op jit(solution)/shard_map/cond/branch_10_fun/ppermute | solution.py:413
  91.1 5.9 %collective-permute-start.205 = (bf16[16,4096]{1,0:T(8,128)(2,1)S(1)}, bf16[16,4096]{1,0:T(8,128)(2,1)S(1)}, u32[]{:S(2)}, u32[]{:S(2)}) collective-permute-start(bf16[16,4096]{1,0:T(8,128)(2,1)S(1)} %get-tuple-element.880), channel_id=1, source_target_pairs={{0,8},{8,24},{16,0},{24,16},{1,9},{9,25},{17,1},{25,17},{2,10},{10... | collective-permute-start | bytes 393224 | tf_op jit(solution)/shard_map/cond/branch_10_fun/ppermute | solution.py:424
  91.1 6.2 %collective-permute-start.206 = (bf16[2,32,1024]{2,1,0:T(8,128)(2,1)S(1)}, bf16[2,32,1024]{2,1,0:T(8,128)(2,1)}, u32[]{:S(2)}, u32[]{:S(2)}) collective-permute-start(bf16[2,32,1024]{2,1,0:T(8,128)(2,1)S(1)} %get-tuple-element.881), channel_id=1, source_target_pairs={{0,2},{1,3},{2,0},{3,1},{4,6},{5,7},{6,4},{7,5},{8,10},{9,11},{10,... | collective-permute-start | bytes 393224 | tf_op jit(solution)/shard_map/cond/branch_10_fun/ppermute | solution.py:413
  91.4 7.2 %collective-permute-start.208 = (bf16[2,32,1024]{2,1,0:T(8,128)(2,1)S(1)}, bf16[2,32,1024]{2,1,0:T(8,128)(2,1)}, u32[]{:S(2)}, u32[]{:S(2)}) collective-permute-start(bf16[2,32,1024]{2,1,0:T(8,128)(2,1)S(1)} %get-tuple-element.883), channel_id=1, source_target_pairs={{0,6},{1,7},{2,4},{3,5},{4,2},{5,3},{6,0},{7,1},{8,14},{9,15},{10,... | collective-permute-start | bytes 393224 | tf_op jit(solution)/shard_map/cond/branch_10_fun/ppermute | solution.py:413
  104.3 9.8 %collective-permute-start.291 = (bf16[2,64,1024]{2,1,0:T(8,128)(2,1)S(1)}, bf16[2,64,1024]{2,1,0:T(8,128)(2,1)}, u32[]{:S(2)}, u32[]{:S(2)}) collective-permute-start(bf16[2,64,1024]{2,1,0:T(8,128)(2,1)S(1)} %get-tuple-element.967), channel_id=1, source_target_pairs={{0,2},{1,3},{2,0},{3,1},{4,6},{5,7},{6,4},{7,5},{8,10},{9,11},{10,... | collective-permute-start | bytes 786440 | tf_op jit(solution)/shard_map/cond/branch_10_fun/ppermute | solution.py:413
  105.6 8.5 %collective-permute-start.292 = (bf16[2,64,1024]{2,1,0:T(8,128)(2,1)S(1)}, bf16[2,64,1024]{2,1,0:T(8,128)(2,1)}, u32[]{:S(2)}, u32[]{:S(2)}) collective-permute-start(bf16[2,64,1024]{2,1,0:T(8,128)(2,1)S(1)} %get-tuple-element.968), channel_id=1, source_target_pairs={{1,0},{2,1},{3,2},{4,3},{5,4},{6,5},{7,6},{9,8},{10,9},{11,10},{12... | collective-permute-start | bytes 786440 | tf_op jit(solution)/shard_map/cond/branch_10_fun/ppermute | solution.py:413
  106.9 7.2 %collective-permute-start.290 = (bf16[2,32,1024]{2,1,0:T(8,128)(2,1)S(1)}, bf16[2,32,1024]{2,1,0:T(8,128)(2,1)S(1)}, u32[]{:S(2)}, u32[]{:S(2)}) collective-permute-start(bf16[2,32,1024]{2,1,0:T(8,128)(2,1)S(1)} %get-tuple-element.966), channel_id=1, source_target_pairs={{0,8},{8,24},{16,0},{24,16},{1,9},{9,25},{17,1},{25,17},{2,10},{10... | collective-permute-start | bytes 393224 | tf_op jit(solution)/shard_map/cond/branch_10_fun/ppermute | solution.py:424
Sparse Core Ops, SparseCore 0:
  18.5 32.5 all-gather.2
